TPU v7x, 512 devices: a whole 4x4x16 slice. The times are simulated.
512 devices in a mesh: src: 64 (over z, x_lo, core), tgt: 8 (over x_hi, y).
Axes of the slice: x: 4 (x_hi: 2, x_lo: 2; x = x_hi * 2 + x_lo), y: 4, z: 16, core: 2. Of those that a mesh axis runs over, the one named last changes fastest.
Arguments:
- source_cells: bfloat16 [1048576, 64], P('src'), may hold values from -6 to 6
- target_cells: bfloat16 [65536, 64], P(('tgt', 'src')), may hold values from -6 to 6
- start_potential: float32 [65536], P('tgt'), may hold values from -30 to 30
- source_logmass: float32 [1048576], P('src'), may hold values from -1 to 1
- target_logmass: float32 [65536], P('tgt'), may hold values from -1 to 1
- pair_src: int32 [64, 8, 256], P('src', 'tgt'), may hold values from 0 to 127, as said below
- pair_tgt: int32 [64, 8, 256], P('src', 'tgt'), may hold values from 0 to 63, as said below
- pair_count: int32 [64, 8], P('src', 'tgt'), may hold values from 64 to 256, as said below
Outputs:
- source_potential: float32 [1048576], P('src')
- target_potential: float32 [65536], P(('tgt', 'src'))
Inputs may be any that keep to these rules, and one draw needn't show every extreme that they name: `pair_count`: on each device a whole number of slots is in use; in every draw some device uses all 256 slots. `pair_src`: no pair of blocks is listed twice on one device; every source block of a src index has a pair among the used slots of some device of that src index. `pair_tgt`: every target block of a tgt index has a pair among the used slots of some device of that tgt index.
All inputs are finite; a program needn't handle non-finite values.
Results may differ from a plain program's by a relative error of at most 0.0003.
Values may be sent and summed in bfloat16 or wider, within the bound.
No kernel may reach another device: no remote copies, remote signals or barrier semaphores. Data moves between devices by JAX's collectives and lax.ppermute only.
A program may use at most 64 MiB of HBM per device.

v0:
```python
import jax
import jax.numpy as jnp
from jax import lax
from jax.sharding import PartitionSpec as P

DIM = 64
BLK = 128
ITERS = 2


epsilon = 0.1
lowest = -1e30
tile_group = 16
highest = lax.Precision.HIGHEST


def combined_all(value, axis, combine):
    everything = jax.tree.map(lambda part: lax.all_gather(part, axis), value)
    first = jax.tree.map(lambda part: part[0], everything)

    def lap(k, so_far):
        return combine(so_far, jax.tree.map(lambda part: part[k], everything))

    return lax.fori_loop(1, lax.axis_size(axis), lap, first)


def merge_pair(former, latter):
    new_max = jnp.maximum(former[0], latter[0])
    return (
        new_max,
        former[1] * jnp.exp(former[0] - new_max) + latter[1] * jnp.exp(latter[0] - new_max),
    )


def sweep(tables, values, used_slots, by_source):
    source_blocks, source_norms, target_blocks, target_norms, src_rows, tgt_rows = tables
    owner_count = source_norms.shape[0] if by_source else target_norms.shape[0]

    def one_group(group_index, running):
        maxima, totals = running
        offset_row = group_index * tile_group
        src_pick = lax.dynamic_slice_in_dim(src_rows, offset_row, tile_group)
        tgt_pick = lax.dynamic_slice_in_dim(tgt_rows, offset_row, tile_group)
        in_use = offset_row + jnp.arange(tile_group, dtype=jnp.int32) < used_slots
        products = jnp.einsum(
            "gid,gjd->gij",
            source_blocks[src_pick],
            target_blocks[tgt_pick],
            preferred_element_type=jnp.float32,
        )
        pair_cost = (
            source_norms[src_pick][:, :, None] + target_norms[tgt_pick][:, None, :] - 2.0 * products
        ) / DIM
        if by_source:
            scores = (values[tgt_pick][:, None, :] - pair_cost) / epsilon
            tile_max = jnp.max(scores, axis=2)
            tile_sum = jnp.sum(jnp.exp(scores - tile_max[:, :, None]), axis=2)
            owner_ids = src_pick
        else:
            scores = (values[src_pick][:, :, None] - pair_cost) / epsilon
            tile_max = jnp.max(scores, axis=1)
            tile_sum = jnp.sum(jnp.exp(scores - tile_max[:, None, :]), axis=1)
            owner_ids = tgt_pick
        tile_max = jnp.where(in_use[:, None], tile_max, lowest)
        tile_sum = jnp.where(in_use[:, None], tile_sum, 0.0)
        member = (owner_ids[:, None] == jnp.arange(owner_count, dtype=jnp.int32)[None, :]) & in_use[
            :, None
        ]
        group_max = jnp.max(jnp.where(member[:, :, None], tile_max[:, None, :], lowest), axis=0)
        new_max = jnp.maximum(maxima, group_max)
        scaled = tile_sum * jnp.exp(tile_max - new_max[owner_ids])
        totals = totals * jnp.exp(maxima - new_max) + jnp.dot(
            member.astype(jnp.float32).T, scaled, precision=highest
        )
        return (new_max, totals)

    initial = (
        jnp.full((owner_count, BLK), lowest, jnp.float32),
        jnp.zeros((owner_count, BLK), jnp.float32),
    )
    rounds = (used_slots + tile_group - 1) // tile_group
    return lax.fori_loop(0, rounds, one_group, initial)


def on_device(
    source_cells,
    target_cells,
    start_potential,
    source_logmass,
    target_logmass,
    pair_src,
    pair_tgt,
    pair_count,
):
    source_blocks = source_cells.reshape(-1, BLK, DIM)
    source_norms = jnp.sum(jnp.square(source_blocks.astype(jnp.float32)), axis=2)
    target_all = lax.all_gather(target_cells, "src", axis=0, tiled=True)
    target_blocks = target_all.reshape(-1, BLK, DIM)
    target_norms = jnp.sum(jnp.square(target_blocks.astype(jnp.float32)), axis=2)
    src_rows = pair_src.reshape(-1)
    tgt_rows = pair_tgt.reshape(-1)
    used_slots = pair_count.reshape(-1)[0]
    tables = (source_blocks, source_norms, target_blocks, target_norms, src_rows, tgt_rows)
    source_mass = source_logmass.reshape(-1, BLK)
    own_cells = target_cells.shape[0]
    own_offset = lax.axis_index("src") * own_cells
    potential = start_potential
    source_potential = source_logmass
    target_potential = lax.dynamic_slice_in_dim(start_potential, own_offset, own_cells)
    for iteration in range(ITERS):
        maxima, totals = sweep(tables, potential.reshape(-1, BLK), used_slots, True)
        maxima, totals = combined_all((maxima, totals), "tgt", merge_pair)
        source_potential = (epsilon * (source_mass - (maxima + jnp.log(totals)))).reshape(-1)
        maxima, totals = sweep(tables, source_potential.reshape(-1, BLK), used_slots, False)
        maxima, totals = combined_all((maxima, totals), "src", merge_pair)
        potential = (
            epsilon * (target_logmass.reshape(-1, BLK) - (maxima + jnp.log(totals)))
        ).reshape(-1)
        target_potential = lax.dynamic_slice_in_dim(potential, own_offset, own_cells)
    return (source_potential, target_potential)


def solution(mesh):
    in_specs = (
        P("src", None),
        P(("tgt", "src"), None),
        P("tgt"),
        P("src"),
        P("tgt"),
        P("src", "tgt", None),
        P("src", "tgt", None),
        P("src", "tgt"),
    )
    out_specs = (P("src"), P(("tgt", "src")))
    return jax.shard_map(
        on_device, mesh=mesh, in_specs=in_specs, out_specs=out_specs, check_vma=False
    )
```

profile of v0, /device:TPU:1, one launch (start us, length us, event | category | flops | bytes accessed | tf_op | source)
XLA Modules:
  0.0 1416.7 jit_solution(8095214346875835429)
XLA Ops:
  8.6 4.9 copy.28
  14.1 119.5 %all-gather.14.cloned.1.call-done = bf16[8192,64]{0,1:T(8,128)(2,1)} async-done(((bf16[128,64]{0,1:T(8,128)(2,1)}), bf16[8192,64]{0,1:T(8,128)(2,1)}) %all-gather.14.cloned.1.call-update) | async-done | bytes 1048592 | tf_op jit(solution)/shard_map/all_gather | solution.py:97
  136.0 77.6 %while.116 = (s32[]{:T(128)}, f32[128,128]{1,0:T(8,128)S(1)}, f32[128,128]{1,0:T(8,128)S(1)}, s32[]{:T(128)}, s32[256]{0:T(256)S(1)}, /*index=5*/s32[]{:T(128)},...) while((s32[]{:T(128)}, f32[128,128]{1,0:T(8,128)S(1)}, ...), condition=%wide.region_6.7_spmd, body=%wide.region_2.6_spmd.sunk | while | flops 39649412 | bytes 4502735 | solution.py:82
  144.7 2.8 gather_fusion
  153.4 2.8 gather_fusion
  205.1 2.8 gather_fusion
  213.6 89.8 %all-gather = f32[1024,128]{1,0:T(8,128)S(1)} all-gather(f32[128,128]{1,0:T(8,128)S(1)} %get-tuple-element.790), channel_id=2, replica_groups=mesh['src'=64,'tgt'=8] {'tgt'}, dimensions={0}, use_global_device_ids=true | all-gather | bytes 589824 | tf_op jit(solution)/shard_map/all_gather | solution.py:18
  303.5 28.9 %all-gather.1 = f32[1024,128]{1,0:T(8,128)S(1)} all-gather(f32[128,128]{1,0:T(8,128)S(1)} %get-tuple-element.791), channel_id=3, replica_groups=mesh['src'=64,'tgt'=8] {'tgt'}, dimensions={0}, use_global_device_ids=true | all-gather | bytes 589824 | tf_op jit(solution)/shard_map/all_gather | solution.py:18
  333.0 76.0 %while.118 = (s32[]{:T(128)}, f32[64,128]{1,0:T(8,128)S(1)}, f32[64,128]{1,0:T(8,128)S(1)}, s32[]{:T(128)}, s32[256]{0:T(256)S(1)}, /*index=5*/s32[]{:T(128)}, s...) while((s32[]{:T(128)}, f32[64,128]{1,0:T(8,128)S(1)}, ...), condition=%wide.region_13.14_spmd, body=%wide.region_9.13_spmd.sunk | while | flops 37785732 | bytes 4173007 | solution.py:82
  367.0 2.8 gather_fusion.6
  375.4 2.8 gather_fusion.6
  383.8 2.8 gather_fusion.6
  392.3 2.8 gather_fusion.6
  400.7 2.8 gather_fusion.6
  410.5 188.2 %all-gather.16.cloned.1.call-done = f32[4096,128]{1,0:T(8,128)} async-done(((f32[64,128]{1,0:T(8,128)}), f32[4096,128]{1,0:T(8,128)}) %all-gather.16.cloned.1.call-update) | async-done | bytes 2097168 | tf_op jit(solution)/shard_map/all_gather | solution.py:18
  599.5 119.8 %all-gather.18.cloned.1.call-done = f32[4096,128]{1,0:T(8,128)} async-done(((f32[64,128]{1,0:T(8,128)}), f32[4096,128]{1,0:T(8,128)}) %all-gather.18.cloned.1.call-update) | async-done | bytes 2097168 | tf_op jit(solution)/shard_map/all_gather | solution.py:18
  720.1 52.7 %while.119 = (s32[]{:T(128)}, f32[64,128]{1,0:T(8,128)S(1)}, f32[64,128]{1,0:T(8,128)S(1)}, f32[64,64,128]{2,1,0:T(8,128)}, f32[64,64,128]{2,1,0:T(8,128)}, /*index=5*/s32[]{:T(128)}, s32[]{:T(128)}, s32[]{:T(128)}) while((s32[]{:T(128)}, f32[64,128]{1,0:T(8,128)S(1)}, f32[64,128]{1,0:T(8,128)S(1)}, f32[64,64,128]{2,1,0:T(8,128)}, ...), condition=%wide.region_15.16_spmd, body=%wide.region_14.15_spmd.sunk | while | flops 49157 | bytes 196739 | solution.py:24
  772.9 77.6 %while.120 = (s32[]{:T(128)}, f32[128,128]{1,0:T(8,128)S(1)}, f32[128,128]{1,0:T(8,128)S(1)}, s32[]{:T(128)}, s32[256]{0:T(256)S(1)}, /*index=5*/s32[]{:T(128)},...) while((s32[]{:T(128)}, f32[128,128]{1,0:T(8,128)S(1)}, ...), condition=%wide.region_20.21_spmd, body=%wide.region_16.20_spmd.sunk | while | flops 39649412 | bytes 4502735 | solution.py:82
  850.5 89.6 %all-gather.4 = f32[1024,128]{1,0:T(8,128)S(1)} all-gather(f32[128,128]{1,0:T(8,128)S(1)} %get-tuple-element.798), channel_id=6, replica_groups=mesh['src'=64,'tgt'=8] {'tgt'}, dimensions={0}, use_global_device_ids=true | all-gather | bytes 589824 | tf_op jit(solution)/shard_map/all_gather | solution.py:18
  940.1 29.0 %all-gather.5 = f32[1024,128]{1,0:T(8,128)S(1)} all-gather(f32[128,128]{1,0:T(8,128)S(1)} %get-tuple-element.799), channel_id=7, replica_groups=mesh['src'=64,'tgt'=8] {'tgt'}, dimensions={0}, use_global_device_ids=true | all-gather | bytes 589824 | tf_op jit(solution)/shard_map/all_gather | solution.py:18
  969.7 76.0 %while.122 = (s32[]{:T(128)}, f32[64,128]{1,0:T(8,128)S(1)}, f32[64,128]{1,0:T(8,128)S(1)}, s32[]{:T(128)}, s32[256]{0:T(256)S(1)}, /*index=5*/s32[]{:T(128)}, s...) while((s32[]{:T(128)}, f32[64,128]{1,0:T(8,128)S(1)}, ...), condition=%wide.region_27.28_spmd, body=%wide.region_23.27_spmd.sunk | while | flops 37785732 | bytes 4173007 | solution.py:82
  1047.0 188.6 %all-gather.20.cloned.1.call-done = f32[4096,128]{1,0:T(8,128)} async-done(((f32[64,128]{1,0:T(8,128)}), f32[4096,128]{1,0:T(8,128)}) %all-gather.20.cloned.1.call-update) | async-done | bytes 2097168 | tf_op jit(solution)/shard_map/all_gather | solution.py:18
  1236.4 119.7 %all-gather.22.cloned.1.call-done = f32[4096,128]{1,0:T(8,128)} async-done(((f32[64,128]{1,0:T(8,128)}), f32[4096,128]{1,0:T(8,128)}) %all-gather.22.cloned.1.call-update) | async-done | bytes 2097168 | tf_op jit(solution)/shard_map/all_gather | solution.py:18
  1356.8 52.7 %while.123 = (s32[]{:T(128)}, f32[64,128]{1,0:T(8,128)S(1)}, f32[64,128]{1,0:T(8,128)S(1)}, f32[64,64,128]{2,1,0:T(8,128)}, f32[64,64,128]{2,1,0:T(8,128)}, /*index=5*/s32[]{:T(128)}, s32[]{:T(128)}, s32[]{:T(128)}) while((s32[]{:T(128)}, f32[64,128]{1,0:T(8,128)S(1)}, f32[64,128]{1,0:T(8,128)S(1)}, f32[64,64,128]{2,1,0:T(8,128)}, ...), condition=%wide.region_29.30_spmd, body=%wide.region_28.29_spmd.sunk | while | flops 49157 | bytes 196739 | solution.py:24
  (840 shorter events, 395.9 us)
Async XLA Ops:
  7.2 126.4 %all-gather.14.cloned.1.call-start = ((), (), s32[]{:S(2)}) async-start(), calls=%async_computation | async-start | bytes 1064960 | tf_op jit(solution)/shard_map/all_gather | solution.py:97
  7.9 590.8 %all-gather.16.cloned.1.call-start = ((), (), s32[]{:S(2)}) async-start(), calls=%async_computation.1 | async-start | bytes 2129920 | tf_op jit(solution)/shard_map/all_gather | solution.py:18
  8.6 4.9 copy-start
  14.0 121.9 %copy-start.2 = (f32[8192]{0:T(1024)S(1)}, f32[8192]{0:T(1024)}, u32[]{:S(2)}) copy-start(f32[8192]{0:T(1024)} %param.26) | copy-start | bytes 98308
  14.1 121.9 %copy-start.10 = (s32[1,1,256]{2,1,0:T(1,128)S(1)}, s32[1,1,256]{2,1,0:T(1,128)}, u32[]{:S(2)}) copy-start(s32[1,1,256]{2,1,0:T(1,128)} %param.29) | copy-start | bytes 3076
  14.1 121.9 %copy-start.11 = (s32[1,1,256]{2,1,0:T(1,128)S(1)}, s32[1,1,256]{2,1,0:T(1,128)}, u32[]{:S(2)}) copy-start(s32[1,1,256]{2,1,0:T(1,128)} %param.30) | copy-start | bytes 3076
  133.5 2.1 copy-start.1
  213.6 119.4 %copy-start.6 = (f32[16384]{0:T(1024)S(1)}, f32[16384]{0:T(1024)}, u32[]{:S(2)}) copy-start(f32[16384]{0:T(1024)} %param.27) | copy-start | bytes 196612
  333.0 439.8 %copy-start.9 = (f32[8192]{0:T(1024)S(1)}, f32[8192]{0:T(1024)}, u32[]{:S(2)}) copy-start(f32[8192]{0:T(1024)} %param.28) | copy-start | bytes 98308
  409.1 0.6 copy-start.5
  409.1 0.7 copy-start.8
  409.7 309.6 %all-gather.18.cloned.1.call-start = ((), (), s32[]{:S(2)}) async-start(), calls=%async_computation.2 | async-start | bytes 2129920 | tf_op jit(solution)/shard_map/all_gather | solution.py:18
  410.5 825.2 %all-gather.20.cloned.1.call-start = ((), (), s32[]{:S(2)}) async-start(), calls=%async_computation.3 | async-start | bytes 2129920 | tf_op jit(solution)/shard_map/all_gather | solution.py:18
  1045.8 0.6 copy-start.4
  1045.8 0.7 copy-start.7
  1045.8 364.3 %copy-start.3 = (f32[128,128]{1,0:T(8,128)}, f32[128,128]{1,0:T(8,128)S(1)}, u32[]{:S(2)}) copy-start(f32[128,128]{1,0:T(8,128)S(1)} %get-tuple-element.1752) | copy-start | bytes 196612
  1046.4 309.7 %all-gather.22.cloned.1.call-start = ((), (), s32[]{:S(2)}) async-start(), calls=%async_computation.4 | async-start | bytes 2129920 | tf_op jit(solution)/shard_map/all_gather | solution.py:18
Sparse Core Ops, SparseCore 0:
  10.1 123.4 all-gather.13
  409.8 188.8 all-gather.15
  600.9 118.4 all-gather.17
  1046.5 189.0 all-gather.19
  1237.6 118.4 all-gather.21
where the time goes:
time: 1430 us; the launch traced here: 1420 us
  waiting for transfers between devices  738 us (52%)
  blocking collectives  237 us (17%)
  local copies, waits for them, and re-layouts  218 us (15%)
  other arithmetic  153 us (11%)
  matrix products  48.8 us (3%)
  between operations  14.8 us (1%)
    all_gather x4, waiting for transfers between devices, combined_all(): everything = jax.tree.map(lambda part: lax.all_gather(part, axis), value)  616 us
    all_gather x4, blocking collectives, combined_all(): everything = jax.tree.map(lambda part: lax.all_gather(part, axis), value)  237 us
    all_gather x1, waiting for transfers between devices, on_device(): target_all = lax.all_gather(target_cells, 'src', axis=0, tiled=True)  119 us
    add x140, other arithmetic, merge_pair(): former[1] * jnp.exp(former[0] - new_max)  104 us
    gather x36, local copies, waits for them, and re-layouts, one_group(): source_blocks[src_pick]  102 us
    dot_general x36, matrix products, one_group(): jnp.einsum('gid,gjd->gij', source_blocks[src_pick], target_blocks[tgt_pic...  37.4 us
  transfers between devices with their start and end apart: 5, of which 5 were waited for; matrix products, arithmetic and copies ran while one was open for 0% of the time, Pallas kernels for 0%

commit v1 on v0

v1 whole, which is shorter than its diff:
```python
import functools

import jax
import jax.numpy as jnp
from jax import lax
from jax.experimental import pallas as pl
from jax.experimental.pallas import tpu as pltpu
from jax.sharding import PartitionSpec as P

DIM = 64
BLK = 128
SLOTS = 256
EPS = 0.1
SCALE = 2.0 / (DIM * EPS)
LOG2E = 1.4426950408889634
KAPPA = SCALE * LOG2E
LOWEST = -1e30
UNROLL = 8
WAYS = 4
VMEM = pltpu.VMEM
SMEM = pltpu.SMEM
bf16 = jnp.bfloat16
f32 = jnp.float32


def nt_dot(a, b):
    return lax.dot_general(a, b, (((1,), (1,)), ((), ())), preferred_element_type=f32)


def split3(x):
    hi = x.astype(bf16).astype(f32)
    rest = x - hi
    mid = rest.astype(bf16).astype(f32)
    return hi, mid, rest - mid


def spread(potential, e1_ref, e2_ref):
    beta = potential * (1.0 / SCALE)
    for g in range(potential.shape[0] // 64):
        hi, mid, lo = split3(beta[g * 64 : g * 64 + 64])
        first = jnp.concatenate([jnp.zeros_like(hi), hi], axis=0)
        second = jnp.concatenate([mid, lo], axis=0)
        e1_ref[g] = first.T.astype(bf16)
        e2_ref[g] = second.T.astype(bf16)


def norm_row(block):
    x = block.astype(f32)
    square = x * x
    hi = square.astype(bf16)
    lo = (square - hi.astype(f32)).astype(bf16)
    ones = jnp.ones((16, BLK), bf16)
    return (nt_dot(ones, hi) + nt_dot(ones, lo))[:1]


def tall(row16):
    return jnp.concatenate([row16] * (BLK // 16), axis=0)


def pair_tile(x_ref, x_place, x_id, o_ref, o_place, e1_ref, e2_ref, hot_ref):
    g, r = x_id // 64, lax.rem(x_id, 64)
    left = jnp.concatenate([x_ref[x_place] + e1_ref[g], e2_ref[g]], axis=1)
    right = jnp.concatenate([o_ref[o_place] + tall(hot_ref[0, r]), tall(hot_ref[1, r])], axis=1)
    return nt_dot(left, right)


def over_pairs(count, pick, work):
    def group(n, carry):
        work([pick(n * UNROLL + q, n * UNROLL + q < count) for q in range(UNROLL)])
        return carry

    lax.fori_loop(0, (count + UNROLL - 1) // UNROLL, group, 0)


def fold_rows(accs, owners, combine):
    parts = []
    for g in range(owners // 8):
        total = None
        for acc in accs:
            for s in range(8):
                rows = acc[pl.ds(g * 64 + s, 8, stride=8), :]
                total = rows if total is None else combine(total, rows)
        parts.append(total)
    return jnp.concatenate(parts, axis=0)


def max_pass(count, pick, tile, accs, owners):
    for acc in accs:
        acc[...] = jnp.full(acc.shape, LOWEST, f32)

    def work(slots):
        tops = [jnp.max(tile(s).reshape(16, 8, BLK), axis=0) for s in slots]
        for q, (s, top) in enumerate(zip(slots, tops)):
            rows = pl.ds(pl.multiple_of(s["owner"] * 8, 8), 8)
            accs[q % WAYS][rows, :] = jnp.maximum(accs[q % WAYS][rows, :], top)

    over_pairs(count, pick, work)
    return fold_rows(accs, owners, jnp.maximum)


def sum_pass(count, pick, tile, accs, owners, offset_ref):
    for acc in accs:
        acc[...] = jnp.zeros(acc.shape, f32)

    def work(slots):
        sums = []
        for s in slots:
            offset = offset_ref[pl.ds(s["owner"], 1), :]
            sums.append(jnp.sum(jnp.exp2(tile(s) * KAPPA + offset).reshape(16, 8, BLK), axis=0))
        for q, (s, total) in enumerate(zip(slots, sums)):
            rows = pl.ds(pl.multiple_of(s["owner"] * 8, 8), 8)
            accs[q % WAYS][rows, :] = accs[q % WAYS][rows, :] + total

    over_pairs(count, pick, work)
    return fold_rows(accs, owners, jnp.add)


def picker(src_ref, tgt_ref, mine, by_source):
    def pick(k, used):
        s, t = src_ref[k], tgt_ref[k]
        s, t = jnp.where(used, s, 0), jnp.where(used, t, 0)
        place = lax.rem(t ^ mine, 4) * 16 + t // 4
        if by_source:
            return dict(x=t, x_place=place, o_place=s, owner=jnp.where(used, s, 128))
        return dict(x=s, x_place=s, o_place=place, owner=jnp.where(used, t, 64))

    return pick


def tiler(x_ref, o_ref, e1_ref, e2_ref, hot_ref):
    return lambda s: pair_tile(x_ref, s["x_place"], s["x"], o_ref, s["o_place"], e1_ref, e2_ref, hot_ref)


def stable_lse(count, pick, tile, accs, owners, offset_ref):
    top = max_pass(count, pick, tile, accs, owners)
    offset_ref[pl.ds(0, owners), :] = top * (-KAPPA)
    offset_ref[pl.ds(owners, 8), :] = jnp.zeros((8, BLK), f32)
    total = sum_pass(count, pick, tile, accs, owners, offset_ref)
    return jnp.where(total > 0.0, top * SCALE + jnp.log(jnp.maximum(total, 1e-37)), LOWEST)


def merge_lse(parts_ref):
    top = jnp.max(parts_ref[...], axis=0)
    total = jnp.sum(jnp.exp(parts_ref[...] - top[None]), axis=0)
    return top + jnp.log(total)


def first_kernel(info, src, tgt, cells, own, core, other, both, start, hot, out, packed, norms, e1, e2, offset, *accs):
    count, mine = info[0], info[1]
    lane = lax.broadcasted_iota(jnp.int32, (BLK // 2, BLK), 1)
    for d, part in enumerate((own, core, other, both)):

        def unpack(z, carry, d=d, part=part):
            half = part[z].astype(f32)
            low = jnp.where(lane < DIM, half, 0.0).astype(bf16)
            high = jnp.where(lane < DIM, pltpu.roll(half, DIM, 1), 0.0).astype(bf16)
            block = jnp.concatenate([low, high], axis=0)
            packed[d * 16 + z] = block
            norms[pl.ds(z * 4 + (d ^ mine), 1), :] = norm_row(block)
            return carry

        lax.fori_loop(0, 16, unpack, 0)
    spread(start[...] * (1.0 / EPS) - norms[...] * (SCALE / 2), e1, e2)
    tile = tiler(packed, cells, e1, e2, hot)
    lse = stable_lse(count, picker(src, tgt, mine, True), tile, accs, 128, offset)
    for k in range(8):
        out[k] = lse


def second_kernel(info, src, tgt, cells, packed, parts, mass, hot, out, potential, e1, e2, offset, *accs):
    count, mine = info[0], info[1]
    new = mass[...] - merge_lse(parts)
    potential[...] = new
    spread(new, e1, e2)
    tile = tiler(cells, packed, e1, e2, hot)
    lse = stable_lse(count, picker(src, tgt, mine, False), tile, accs, 64, offset)
    for k in range(4):
        out[k] = lse


def group_kernel(info, parts, out):
    lse = merge_lse(parts)
    half = jnp.where(info[2] == 0, lse[:32], lse[32:])
    for k in range(16):
        out[k] = half


def ring_kernel(parts, out):
    out[...] = merge_lse(parts)


def third_kernel(info, src, tgt, cells, packed, lse, mass, reference, hot, out, potential, e1, e2, offset, *accs):
    count, mine = info[0], info[1]
    new = mass[...] - lse[...]
    potential[...] = new
    spread(new, e1, e2)
    offset[pl.ds(0, 128), :] = reference[...] * LOG2E
    offset[pl.ds(128, 8), :] = jnp.zeros((8, BLK), f32)
    tile = tiler(packed, cells, e1, e2, hot)
    total = sum_pass(count, picker(src, tgt, mine, True), tile, accs, 128, offset)
    for k in range(8):
        out[k] = total


def fourth_kernel(info, src, tgt, cells, packed, parts, mass, former, reference, hot, out, final, e1, e2, offset, total, *accs):
    count, mine = info[0], info[1]
    new = former[...] + mass[...] - jnp.log(jnp.sum(parts[...], axis=0))
    spread(new, e1, e2)

    def finish(b, carry):
        final[pl.ds(b, 1), :] = norm_row(cells[b])
        return carry

    lax.fori_loop(0, 128, finish, 0)
    final[...] = EPS * (new + final[...] * (SCALE / 2))
    offset[pl.ds(0, 64), :] = reference[...] * LOG2E
    offset[pl.ds(64, 8), :] = jnp.zeros((8, BLK), f32)
    tile = tiler(cells, packed, e1, e2, hot)
    total[...] = sum_pass(count, picker(src, tgt, mine, False), tile, accs, 64, offset)
    for k in range(4):
        out[k] = total[pl.ds(k, 16, stride=4), :]


def total_kernel(parts, out):
    out[...] = jnp.sum(parts[...], axis=0)[:, None, :]


def last_kernel(info, parts, mass, potential, cells, out):
    me = info[3]
    total = jnp.sum(parts[...], axis=0)
    x = cells[...].astype(f32)
    square = x * x
    hi = square.astype(bf16)
    lo = (square - hi.astype(f32)).astype(bf16)
    ones = jnp.ones((16, DIM), bf16)
    norm = (nt_dot(ones, hi) + nt_dot(ones, lo))[:1]
    new = potential[pl.ds(me, 1), :] + mass[pl.ds(me, 1), :] - jnp.log(total)
    out[...] = EPS * (new + norm * (SCALE / 2))


def call(kernel, kinds, outs, scratch=()):
    specs = [pl.BlockSpec(memory_space=SMEM if kind == "s" else VMEM) for kind in kinds]
    out_specs = [pl.BlockSpec(memory_space=VMEM) for _ in outs]
    shapes = [jax.ShapeDtypeStruct(shape, dtype) for shape, dtype in outs]
    single = len(outs) == 1
    return pl.pallas_call(
        kernel,
        in_specs=specs,
        out_specs=out_specs[0] if single else out_specs,
        out_shape=shapes[0] if single else shapes,
        scratch_shapes=list(scratch),
        compiler_params=pltpu.CompilerParams(vmem_limit_bytes=40 * 1024 * 1024),
    )


def sweep_scratch(groups, owners):
    return [
        VMEM((groups, BLK, BLK), bf16),
        VMEM((groups, BLK, BLK), bf16),
        VMEM((owners + 8, BLK), f32),
    ]


def accumulators(owners):
    return [VMEM(((owners + 1) * 8, BLK), f32) for _ in range(WAYS)]


def on_device(source_cells, target_cells, start, source_logmass, target_logmass, pair_src, pair_tgt, pair_count):
    ring = [[z * 4 + r for z in range(16)] for r in range(4)]
    chips = [[z * 4 + r for r in range(4)] for z in range(16)]
    cores = [[i, i + 1] for i in range(0, 64, 2)]
    to_core = [(i, i ^ 1) for i in range(64)]
    to_chip = [(i, i ^ 2) for i in range(64)]

    me = lax.axis_index("src")
    mine = lax.rem(me, 4)
    info = jnp.stack([pair_count.reshape(()), mine, lax.rem(me, 2), me]).astype(jnp.int32)
    src, tgt = pair_src.reshape(-1), pair_tgt.reshape(-1)

    small = jnp.concatenate([target_cells[:64], target_cells[64:]], axis=1)
    own = lax.all_to_all(jnp.broadcast_to(small[None], (16, 64, BLK)), "src", 0, 0, axis_index_groups=ring)
    other = lax.ppermute(own, "src", to_chip)
    core = lax.ppermute(own, "src", to_core)
    both = lax.ppermute(other, "src", to_core)

    cells = jnp.pad(source_cells, ((0, 0), (0, BLK - DIM))).reshape(-1, BLK, BLK)
    source_mass = source_logmass.reshape(-1, BLK)
    target_mass = target_logmass.reshape(-1, BLK)
    first = jnp.arange(64)[:, None] + 64 == jnp.arange(BLK)[None, :]
    second = jnp.arange(64)[:, None] == jnp.arange(BLK)[None, :] % 64
    hot = jnp.broadcast_to(jnp.stack([first, second])[:, :, None, :], (2, 64, 16, BLK)).astype(bf16)

    parts, packed = call(
        first_kernel,
        "sssvvvvvvv",
        [((8, 128, BLK), f32), ((64, BLK, BLK), bf16)],
        [VMEM((64, BLK), f32)] + sweep_scratch(1, 128) + accumulators(128),
    )(info, src, tgt, cells, own, core, other, both, start.reshape(-1, BLK), hot)
    parts = lax.all_to_all(parts, "tgt", 0, 0)
    lse, first_u = call(
        second_kernel,
        "sssvvvvv",
        [((4, 64, BLK), f32), ((128, BLK), f32)],
        sweep_scratch(2, 64) + accumulators(64),
    )(info, src, tgt, cells, packed, parts, source_mass, hot)
    lse = lax.all_to_all(lse, "src", 0, 0, axis_index_groups=chips)
    lse = call(group_kernel, "sv", [((16, 32, BLK), f32)])(info, lse)
    lse = lax.all_to_all(lse, "src", 0, 0, axis_index_groups=ring)
    lse = call(ring_kernel, "v", [((32, BLK), f32)])(lse)
    lse = lax.all_gather(lse, "src", axis=0, axis_index_groups=cores, tiled=True)
    parts, first_v = call(
        third_kernel,
        "sssvvvvvv",
        [((8, 128, BLK), f32), ((64, BLK), f32)],
        sweep_scratch(1, 128) + accumulators(128),
    )(info, src, tgt, cells, packed, lse, target_mass, first_u, hot)
    parts = lax.all_to_all(parts, "tgt", 0, 0)
    sums, last_u = call(
        fourth_kernel,
        "sssvvvvvvv",
        [((4, 16, BLK), f32), ((128, BLK), f32)],
        sweep_scratch(2, 64) + [VMEM((64, BLK), f32)] + accumulators(64),
    )(info, src, tgt, cells, packed, parts, source_mass, first_u, first_v, hot)
    sums = lax.all_to_all(sums, "src", 0, 0, axis_index_groups=chips)
    sums = call(total_kernel, "v", [((16, 1, BLK), f32)])(sums)
    sums = lax.all_to_all(sums, "src", 0, 0, axis_index_groups=ring)
    last_v = call(last_kernel, "svvvv", [((1, BLK), f32)])(info, sums, target_mass, first_v, target_cells)
    return last_u.reshape(-1), last_v.reshape(-1)


def solution(mesh):
    in_specs = (
        P("src", None),
        P(("tgt", "src"), None),
        P("tgt"),
        P("src"),
        P("tgt"),
        P("src", "tgt", None),
        P("src", "tgt", None),
        P("src", "tgt"),
    )
    out_specs = (P("src"), P(("tgt", "src")))
    return jax.shard_map(
        on_device, mesh=mesh, in_specs=in_specs, out_specs=out_specs, check_vma=False
    )
```

time: 1430 us -> 248 us (0.17)
  waiting for transfers between devices: 738 us -> 11.1 us
  local copies, waits for them, and re-layouts: 218 us -> 8.71 us
  other arithmetic: 153 us -> 0.19 us
  blocking collectives: 237 us -> 133 us
  Pallas kernels: 0 us -> 67.3 us
  matrix products: 48.8 us -> 0 us
  starting transfers between devices: 0.2 us -> 25.2 us
    all_gather x5 -> x0, waiting for transfers between devices: 736 us -> none  [the longest x4 616 us: combined_all(): everything = jax.tree.map(lambda part: lax.all_gather(part, axis), value)]
    all_gather x4 -> x1, blocking collectives: 237 us -> 7.98 us  [on_device(): lax.all_gather(lse, 'src', axis=0, axis_index_groups=cores, tiled=True)]
    gather x216 -> x0, local copies, waits for them, and re-layouts: 206 us -> none  [the longest x36 102 us: one_group(): source_blocks[src_pick]]
    all_to_all x0 -> x6, blocking collectives: none -> 125 us  [the longest x2 41.6 us: on_device(): parts = lax.all_to_all(parts, 'tgt', 0, 0)]
    add x140 -> x1, other arithmetic: 104 us -> 0.01 us  [on_device(): first = jnp.arange(64)[:, None] + 64 == jnp.arange(BLK)[None, :]]
    pallas_call x0 -> x8, Pallas kernels: none -> 67.3 us  [the longest x1 25.9 us: on_device(): call(fourth_kernel, 'sssvvvvvvv', [((4, 16, BLK), f32), ((128, BLK), f32)...]
    dot_general x72 -> x0, matrix products: 48.8 us -> none  [the longest x36 37.4 us: one_group(): jnp.einsum('gid,gjd->gij', source_blocks[src_pick], target_blocks[tgt_pic...]
    lt x36 -> x0, other arithmetic: 23.5 us -> none  [one_group(): in_use = offset_row + jnp.arange(tile_group, dtype=jnp.int32) < used_slots]
  transfers between devices with their start and end apart: 5 -> 4, of which waited for: 5 -> 1; matrix products, arithmetic and copies ran while one was open for 0% -> 3% of each run, Pallas kernels for 0% -> 0%
where the time goes in v1:
time: 248 us; the launch traced here: 247 us
  blocking collectives  133 us (54%)
  Pallas kernels  67.3 us (27%)
  starting transfers between devices  25.2 us (10%)
  waiting for transfers between devices  11.1 us (4%)
  local copies, waits for them, and re-layouts  8.71 us (4%)
    all_to_all x2, blocking collectives, on_device(): parts = lax.all_to_all(parts, 'tgt', 0, 0)  41.6 us
    all_to_all x1, blocking collectives, on_device(): lax.all_to_all(jnp.broadcast_to(small[None], (16, 64, BLK)), 'src', 0, 0,...  28.7 us
    pallas_call x1, Pallas kernels, on_device(): call(fourth_kernel, 'sssvvvvvvv', [((4, 16, BLK), f32), ((128, BLK), f32)...  25.9 us
    pallas_call x1, Pallas kernels, on_device(): call(first_kernel, 'sssvvvvvvv', [((8, 128, BLK), f32), ((64, BLK, BLK),...  23.6 us
    all_to_all x1, blocking collectives, on_device(): lse = lax.all_to_all(lse, 'src', 0, 0, axis_index_groups=ring)  23.5 us
    all_to_all x1, blocking collectives, on_device(): lse = lax.all_to_all(lse, 'src', 0, 0, axis_index_groups=chips)  18.8 us
    all_to_all x1, blocking collectives, on_device(): sums = lax.all_to_all(sums, 'src', 0, 0, axis_index_groups=chips)  12.3 us
    all_to_all x1, waiting for transfers between devices, on_device(): sums = lax.all_to_all(sums, 'src', 0, 0, axis_index_groups=ring)  11.1 us
  transfers between devices with their start and end apart: 4, of which 1 were waited for; matrix products, arithmetic and copies ran while one was open for 3% of the time, Pallas kernels for 0%

profile of v1, /device:TPU:1, one launch (start us, length us, event | category | flops | bytes accessed | tf_op | source)
XLA Modules:
  0.0 246.8 jit_solution(6486459422477120520)
XLA Ops:
  0.6 0.9 fusion
  1.5 0.1 copy.11
  1.7 28.7 %all_to_all.35.own = bf16[16,64,128]{2,1,0:T(8,128)(2,1)S(1)} all-to-all(bf16[16,64,128]{2,1,0:T(8,128)(2,1)S(1)} %broadcast_in_dim.4), channel_id=1, replica_groups={{0,32,64,96,128,160,192,224,256,288,320,352,384,416,448,480},{8,40,72,1..., dimensions={0} | all-to-all | bytes 524288 | tf_op jit(solution)/shard_map/all_to_all | solution.py:281
  30.4 3.1 %collective-permute-start.1 = (bf16[16,64,128]{2,1,0:T(8,128)(2,1)S(1)}, bf16[16,64,128]{2,1,0:T(8,128)(2,1)S(1)}, u32[]{:S(2)}, u32[]{:S(2)}) collective-permute-start(bf16[16,64,128]{2,1,0:T(8,128)(2,1)S(1)} %all_to_all.35.own), channel_id=1, source_target_pairs={{0,16},{8,24},{16,0},{24,8},{32,48},{40,56},{48,32},{56,40},{64,80... | collective-permute-start | bytes 786440 | tf_op jit(solution)/shard_map/ppermute | solution.py:282
  33.5 8.4 %collective-permute-start = (bf16[16,64,128]{2,1,0:T(8,128)(2,1)S(1)}, bf16[16,64,128]{2,1,0:T(8,128)(2,1)S(1)}, u32[]{:S(2)}, u32[]{:S(2)}) collective-permute-start(bf16[16,64,128]{2,1,0:T(8,128)(2,1)S(1)} %all_to_all.35.own), channel_id=1, source_target_pairs={{0,8},{8,0},{16,24},{24,16},{32,40},{40,32},{48,56},{56,48},{64,72... | collective-permute-start | bytes 786440 | tf_op jit(solution)/shard_map/ppermute | solution.py:283
  41.9 4.8 %collective-permute-start.2 = (bf16[16,64,128]{2,1,0:T(8,128)(2,1)S(1)}, bf16[16,64,128]{2,1,0:T(8,128)(2,1)S(1)}, u32[]{:S(2)}, u32[]{:S(2)}) collective-permute-start(bf16[16,64,128]{2,1,0:T(8,128)(2,1)S(1)} %collective-permute-done.1.other), channel_id=1, source_target_pairs={{0,8},{8,0},{16,24},{24,16},{32,40},{40,32},{48,56},{56,48},{64,72... | collective-permute-start | bytes 786440 | tf_op jit(solution)/shard_map/ppermute | solution.py:284
  47.4 4.8 %copy.13 = bf16[16384,64]{1,0:T(8,128)(2,1)} copy(bf16[16384,64]{0,1:T(8,128)(2,1)} %param.8) | data formatting | bytes 4194304
  52.2 2.7 %pad.4.clone = bf16[16384,128]{1,0:T(8,128)(2,1)S(1)} pad(bf16[16384,64]{1,0:T(8,128)(2,1)} %copy.13, bf16[]{:T(256)} %constant.31.clone.1), padding=0_0x0_64 | pad | bytes 6291458 | tf_op jit(solution)/shard_map/jit(_pad)/pad | solution.py:286
  55.2 23.6 %shard_map.95 = (f32[8,128,128]{2,1,0:T(8,128)S(1)}, bf16[64,128,128]{2,1,0:T(8,128)(2,1)S(1)}) custom-call(s32[4]{0:T(128)S(1)} %pad_add_fusion.info, s32[256]{0:T(256)S(1)} %bitcast.22, s32[256]{0:T(256)S(1)} %bitcast.26, bf16[128,128,128]{2,1,0:T(8,128)(2,1)S(1)} %bitcast.13, bf16[16,64,128]{2,1,0:T(8,128)(2,1)S(1)} %all_to_all.35.own, ...), custom_call_target="tpu_custom_call" | custom-call | tf_op jit(solution)/shard_map/pallas_call | solution.py:293
  78.8 25.3 %all_to_all.36.parts = f32[8,128,128]{2,1,0:T(8,128)S(1)} all-to-all(f32[8,128,128]{2,1,0:T(8,128)S(1)} %get-tuple-element.11), channel_id=1, replica_groups=mesh['src'=64,'tgt'=8] {'tgt'}, dimensions={0} | all-to-all | bytes 1048576 | tf_op jit(solution)/shard_map/all_to_all | solution.py:299
  104.1 9.9 %shard_map.96 = (f32[4,64,128]{2,1,0:T(8,128)S(1)}, f32[128,128]{1,0:T(8,128)S(1)}) custom-call(s32[4]{0:T(128)S(1)} %pad_add_fusion.info, s32[256]{0:T(256)S(1)} %bitcast.23, s32[256]{0:T(256)S(1)} %bitcast.27, bf16[128,128,128]{2,1,0:T(8,128)(2,1)S(1)} %bitcast.14, bf16[64,128,128]{2,1,0:T(8,128)(2,1)S(1)} %get-tuple-element.10.packed, ...), custom_call_target="tpu_custom_call" | custom-call | tf_op jit(solution)/shard_map/pallas_call | solution.py:300
  114.0 18.8 %all_to_all.37.parts = f32[4,64,128]{2,1,0:T(8,128)S(1)} all-to-all(f32[4,64,128]{2,1,0:T(8,128)S(1)} %get-tuple-element.12), channel_id=1, replica_groups={{0,8,16,24},{32,40,48,56},{64,72,80,88},{96,104,112,120},{128,136,144,1..., dimensions={0} | all-to-all | bytes 262144 | tf_op jit(solution)/shard_map/all_to_all | solution.py:306
  132.9 0.6 shard_map.97
  133.5 23.5 %all_to_all.38.parts = f32[16,32,128]{2,1,0:T(8,128)S(1)} all-to-all(f32[16,32,128]{2,1,0:T(8,128)S(1)} %shard_map.97), channel_id=1, replica_groups={{0,32,64,96,128,160,192,224,256,288,320,352,384,416,448,480},{8,40,72,1..., dimensions={0} | all-to-all | bytes 524288 | tf_op jit(solution)/shard_map/all_to_all | solution.py:308
  157.0 8.0 %all_gather.3.lse = f32[64,128]{1,0:T(8,128)S(1)} all-gather(f32[32,128]{1,0:T(8,128)S(1)} %shard_map.98), channel_id=1, replica_groups={{0,8},{16,24},{32,40},{48,56},{64,72},{80,88},{96,104},{112,120},{128,1..., dimensions={0}, use_global_device_ids=true | all-gather | bytes 49152 | tf_op jit(solution)/shard_map/all_gather | solution.py:310
  165.0 5.4 %shard_map.99 = (f32[8,128,128]{2,1,0:T(8,128)S(1)}, f32[64,128]{1,0:T(8,128)S(1)}) custom-call(s32[4]{0:T(128)S(1)} %pad_add_fusion.info, s32[256]{0:T(256)S(1)} %bitcast.24, s32[256]{0:T(256)S(1)} %bitcast.28, bf16[128,128,128]{2,1,0:T(8,128)(2,1)S(1)} %bitcast.15, bf16[64,128,128]{2,1,0:T(8,128)(2,1)S(1)} %get-tuple-element.10.packed, ...), custom_call_target="tpu_custom_call" | custom-call | tf_op jit(solution)/shard_map/pallas_call | solution.py:311
  170.4 16.3 %all_to_all.39.parts = f32[8,128,128]{2,1,0:T(8,128)S(1)} all-to-all(f32[8,128,128]{2,1,0:T(8,128)S(1)} %get-tuple-element.14), channel_id=1, replica_groups=mesh['src'=64,'tgt'=8] {'tgt'}, dimensions={0} | all-to-all | bytes 1048576 | tf_op jit(solution)/shard_map/all_to_all | solution.py:317
  186.7 25.9 %shard_map.100 = (f32[4,16,128]{2,1,0:T(8,128)S(1)}, f32[128,128]{1,0:T(8,128)}) custom-call(s32[4]{0:T(128)S(1)} %pad_add_fusion.info, s32[256]{0:T(256)S(1)} %bitcast.25, s32[256]{0:T(256)S(1)} %bitcast.29, bf16[128,128,128]{2,1,0:T(8,128)(2,1)S(1)} %bitcast.16, bf16[64,128,128]{2,1,0:T(8,128)(2,1)S(1)} %get-tuple-element.10.packed, ...), custom_call_target="tpu_custom_call" | custom-call | tf_op jit(solution)/shard_map/pallas_call | solution.py:318
  212.6 12.3 %all_to_all.40.parts = f32[4,16,128]{2,1,0:T(8,128)S(1)} all-to-all(f32[4,16,128]{2,1,0:T(8,128)S(1)} %get-tuple-element.17), channel_id=1, replica_groups={{0,8,16,24},{32,40,48,56},{64,72,80,88},{96,104,112,120},{128,136,144,1..., dimensions={0} | all-to-all | bytes 65536 | tf_op jit(solution)/shard_map/all_to_all | solution.py:324
  224.9 0.6 shard_map.101
  225.5 8.9 %all-to-all-start.6 = ((f32[16,1,128]{2,1,0:T(1,128)}), f32[16,1,128]{2,1,0:T(1,128)S(1)}, u32[]{:S(2)}, u32[]{:S(2)}) async-start(f32[16,1,128]{2,1,0:T(1,128)} %shard_map.101), calls=%async_computation.6 | async-start | bytes 16384 | tf_op jit(solution)/shard_map/all_to_all | solution.py:326
  234.4 0.1 copy.12.cells
  234.5 11.1 %all-to-all-done.6.parts = f32[16,1,128]{2,1,0:T(1,128)S(1)} async-done(((f32[16,1,128]{2,1,0:T(1,128)}), f32[16,1,128]{2,1,0:T(1,128)S(1)}, u32[]{:S(2)}, u32[]{:S(2)}) %all-to-all-start.6) | async-done | bytes 8224 | tf_op jit(solution)/shard_map/all_to_all | solution.py:326
  245.6 1.2 shard_map.102
  (24 shorter events, 0.4 us)
Async XLA Ops:
  30.4 11.5 %collective-permute-start.1 = (bf16[16,64,128]{2,1,0:T(8,128)(2,1)S(1)}, bf16[16,64,128]{2,1,0:T(8,128)(2,1)S(1)}, u32[]{:S(2)}, u32[]{:S(2)}) collective-permute-start(bf16[16,64,128]{2,1,0:T(8,128)(2,1)S(1)} %all_to_all.35.own), channel_id=1, source_target_pairs={{0,16},{8,24},{16,0},{24,8},{32,48},{40,56},{48,32},{56,40},{64,80... | collective-permute-start | bytes 786440 | tf_op jit(solution)/shard_map/ppermute | solution.py:282
  33.5 21.5 %collective-permute-start = (bf16[16,64,128]{2,1,0:T(8,128)(2,1)S(1)}, bf16[16,64,128]{2,1,0:T(8,128)(2,1)S(1)}, u32[]{:S(2)}, u32[]{:S(2)}) collective-permute-start(bf16[16,64,128]{2,1,0:T(8,128)(2,1)S(1)} %all_to_all.35.own), channel_id=1, source_target_pairs={{0,8},{8,0},{16,24},{24,16},{32,40},{40,32},{48,56},{56,48},{64,72... | collective-permute-start | bytes 786440 | tf_op jit(solution)/shard_map/ppermute | solution.py:283
  41.9 13.2 %collective-permute-start.2 = (bf16[16,64,128]{2,1,0:T(8,128)(2,1)S(1)}, bf16[16,64,128]{2,1,0:T(8,128)(2,1)S(1)}, u32[]{:S(2)}, u32[]{:S(2)}) collective-permute-start(bf16[16,64,128]{2,1,0:T(8,128)(2,1)S(1)} %collective-permute-done.1.other), channel_id=1, source_target_pairs={{0,8},{8,0},{16,24},{24,16},{32,40},{40,32},{48,56},{56,48},{64,72... | collective-permute-start | bytes 786440 | tf_op jit(solution)/shard_map/ppermute | solution.py:284
  52.2 2.9 %copy-start.2 = (f32[8192]{0:T(1024)S(1)}, f32[8192]{0:T(1024)}, u32[]{:S(2)}) copy-start(f32[8192]{0:T(1024)} %param.10) | copy-start | bytes 98308
  52.2 2.9 %copy-start.3 = (s32[1,1,256]{2,1,0:T(1,128)S(1)}, s32[1,1,256]{2,1,0:T(1,128)}, u32[]{:S(2)}) copy-start(s32[1,1,256]{2,1,0:T(1,128)} %param.13) | copy-start | bytes 3076
  52.2 2.9 %copy-start.4 = (s32[1,1,256]{2,1,0:T(1,128)S(1)}, s32[1,1,256]{2,1,0:T(1,128)}, u32[]{:S(2)}) copy-start(s32[1,1,256]{2,1,0:T(1,128)} %param.14) | copy-start | bytes 3076
  54.9 49.2 %copy-start = (f32[16384]{0:T(1024)S(1)}, f32[16384]{0:T(1024)}, u32[]{:S(2)}) copy-start(f32[16384]{0:T(1024)} %param.11) | copy-start | bytes 196612
  104.1 60.9 %copy-start.1 = (f32[8192]{0:T(1024)S(1)}, f32[8192]{0:T(1024)}, u32[]{:S(2)}) copy-start(f32[8192]{0:T(1024)} %param.12) | copy-start | bytes 98308
  170.4 64.0 %copy-start.5 = (bf16[128,64]{0,1:T(8,128)(2,1)S(1)}, bf16[128,64]{0,1:T(8,128)(2,1)}, u32[]{:S(2)}) copy-start(bf16[128,64]{0,1:T(8,128)(2,1)} %param.9) | copy-start | bytes 49156
  225.5 20.1 %all-to-all-start.6 = ((f32[16,1,128]{2,1,0:T(1,128)}), f32[16,1,128]{2,1,0:T(1,128)S(1)}, u32[]{:S(2)}, u32[]{:S(2)}) async-start(f32[16,1,128]{2,1,0:T(1,128)} %shard_map.101), calls=%async_computation.6 | async-start | bytes 16384 | tf_op jit(solution)/shard_map/all_to_all | solution.py:326

commit v2 on v1

v2 whole, which is shorter than its diff:
```python
import functools

import jax
import jax.numpy as jnp
from jax import lax
from jax.experimental import pallas as pl
from jax.experimental.pallas import tpu as pltpu
from jax.sharding import PartitionSpec as P

DIM = 64
BLK = 128
EPS = 0.1
SCALE = 2.0 / (DIM * EPS)
LOG2E = 1.4426950408889634
KAPPA = SCALE * LOG2E
LOWEST = -1e30
UNROLL = 32
WAYS = 4
VMEM = pltpu.VMEM
SMEM = pltpu.SMEM
bf16 = jnp.bfloat16
f32 = jnp.float32


def block_of(n):
    return pl.ds(pl.multiple_of(n * BLK, BLK), BLK)


def as_rows(block):
    return jnp.concatenate([block, jnp.zeros((BLK - DIM, BLK), bf16)], axis=0).T


def norm_row(block):
    x = block.astype(f32)
    return jnp.sum(x * x, axis=0, keepdims=True)


def spread(potential, columns_ref, extra_ref):
    blocks = potential.shape[0]
    beta = potential * (1.0 / SCALE)
    hi = beta.astype(bf16).astype(f32)
    rest = beta - hi
    mid = rest.astype(bf16).astype(f32)
    for s, part in enumerate((hi, mid, rest - mid, jnp.zeros_like(hi))):
        columns_ref[pl.ds(s, blocks, stride=4), :] = part
    for g in range(blocks // 16):
        half = columns_ref[g * 64 : g * 64 + 64, :]
        extra_ref[g] = jnp.concatenate([jnp.zeros_like(half), half], axis=0).T.astype(bf16)


def pair_tile(x_ref, extra_ref, hot_ref, x_place, x_id, other_block):
    left = x_ref[x_place] + extra_ref[x_id // 16]
    right = jnp.concatenate([other_block, hot_ref[lax.rem(x_id, 16)]], axis=0)
    return jnp.dot(left, right, preferred_element_type=f32).reshape(16, 8, BLK)


def over_pairs(count, pick, work):
    def group(n, carry):
        work([pick(n * UNROLL + q, n * UNROLL + q < count) for q in range(UNROLL)])
        return carry

    lax.fori_loop(0, (count + UNROLL - 1) // UNROLL, group, 0)


def owner_rows(slot):
    return pl.ds(pl.multiple_of(slot["owner"] * 8, 8), 8)


def strided(accs, g):
    return [acc[pl.ds(g * 64 + s, 8, stride=8), :] for acc in accs for s in range(8)]


def stable_lse(count, pick, tile, tops, sums, owners):
    for top, total in zip(tops, sums):
        top[...] = jnp.full(top.shape, LOWEST, f32)
        total[...] = jnp.zeros(total.shape, f32)

    def work(slots):
        stats = []
        for s in slots:
            z = tile(s)
            most = jnp.max(z, axis=0)
            stats.append((most, jnp.sum(jnp.exp2((z - most[None]) * KAPPA), axis=0)))
        for q, (s, (most, part)) in enumerate(zip(slots, stats)):
            rows, top, total = owner_rows(s), tops[q % WAYS], sums[q % WAYS]
            old = top[rows, :]
            new = jnp.maximum(old, most)
            total[rows, :] = total[rows, :] * jnp.exp2((old - new) * KAPPA) + part * jnp.exp2((most - new) * KAPPA)
            top[rows, :] = new

    over_pairs(count, pick, work)
    out = []
    for g in range(owners // 8):
        rows = strided(tops, g)
        most = functools.reduce(jnp.maximum, rows)
        parts = [p * jnp.exp2((r - most) * KAPPA) for r, p in zip(rows, strided(sums, g))]
        total = functools.reduce(jnp.add, parts)
        out.append(jnp.where(total > 0.0, most * SCALE + jnp.log(jnp.maximum(total, 1e-30)), LOWEST))
    return jnp.concatenate(out, axis=0)


def plain_sum(count, pick, tile, sums, owners, offset_ref):
    for total in sums:
        total[...] = jnp.zeros(total.shape, f32)

    def work(slots):
        parts = []
        for s in slots:
            offset = offset_ref[pl.ds(s["owner"], 1), :]
            parts.append(jnp.sum(jnp.exp2(tile(s) * KAPPA + offset[None]), axis=0))
        for q, (s, part) in enumerate(zip(slots, parts)):
            rows, total = owner_rows(s), sums[q % WAYS]
            total[rows, :] = total[rows, :] + part

    over_pairs(count, pick, work)
    return jnp.concatenate([functools.reduce(jnp.add, strided(sums, g)) for g in range(owners // 8)], axis=0)


def place_of(t, mine):
    return lax.rem(t ^ mine, 4) * 16 + t // 4


def picker(src_ref, tgt_ref, by_source):
    def pick(k, used):
        s, t = jnp.where(used, src_ref[k], 0), jnp.where(used, tgt_ref[k], 0)
        return dict(s=s, t=t, owner=jnp.where(used, s, 128) if by_source else jnp.where(used, t, 64))

    return pick


def by_source(targets, sources, extra, hot, mine):
    return lambda p: pair_tile(targets, extra, hot, place_of(p["t"], mine), p["t"], sources[:, block_of(p["s"])])


def by_target(sources, targets, extra, hot, mine):
    return lambda p: pair_tile(sources, extra, hot, p["s"], p["s"], targets[place_of(p["t"], mine)])


def prepare_kernel(cells, rows, norms, hot):
    def some(n, carry):
        for q in range(16):
            block = cells[:, block_of(n * 16 + q)]
            rows[n * 16 + q] = as_rows(block)
            norms[pl.ds(n * 16 + q, 1), :] = norm_row(block)
        return carry

    lax.fori_loop(0, 8, some, 0)
    line = lax.broadcasted_iota(jnp.int32, (DIM, BLK), 0)
    for r in range(16):
        hot[r] = jnp.where((line >= 4 * r) & (line < 4 * r + 3), 1.0, 0.0).astype(bf16)


def merge_lse(parts_ref):
    top = jnp.max(parts_ref[...], axis=0)
    total = jnp.sum(jnp.exp(parts_ref[...] - top[None]), axis=0)
    return top + jnp.log(total)


def first_kernel(
    info, src, tgt, sources, own, core, other, both, start, hot, out, rows, targets, norms, columns, extra, *accs
):
    count, mine = info[0], info[1]
    for d, part in enumerate((own, core, other, both)):
        for z in range(16):
            block = part[z]
            targets[d * 16 + z] = block
            rows[d * 16 + z] = as_rows(block)
            norms[pl.ds(z * 4 + (d ^ mine), 1), :] = norm_row(block)
    spread(start[...] * (1.0 / EPS) - norms[...] * (SCALE / 2), columns, extra)
    tile = by_source(rows, sources, extra, hot, mine)
    lse = stable_lse(count, picker(src, tgt, True), tile, accs[:WAYS], accs[WAYS:], 128)
    for k in range(8):
        out[k] = lse


def second_kernel(info, src, tgt, rows, targets, parts, mass, hot, out, potential, columns, extra, *accs):
    count, mine = info[0], info[1]
    new = mass[...] - merge_lse(parts)
    potential[...] = new
    spread(new, columns, extra)
    tile = by_target(rows, targets, extra, hot, mine)
    lse = stable_lse(count, picker(src, tgt, False), tile, accs[:WAYS], accs[WAYS:], 64)
    for k in range(4):
        out[k] = lse


def group_kernel(info, parts, out):
    lse = merge_lse(parts)
    half = jnp.where(info[2] == 0, lse[:32], lse[32:])
    for k in range(16):
        out[k] = half


def ring_kernel(parts, out):
    out[...] = merge_lse(parts)


def third_kernel(
    info, src, tgt, sources, rows, lse, mass, reference, hot, out, potential, columns, extra, offset, *accs
):
    count, mine = info[0], info[1]
    new = mass[...] - lse[...]
    potential[...] = new
    spread(new, columns, extra)
    offset[pl.ds(0, 128), :] = reference[...] * LOG2E
    offset[pl.ds(128, 8), :] = jnp.zeros((8, BLK), f32)
    tile = by_source(rows, sources, extra, hot, mine)
    total = plain_sum(count, picker(src, tgt, True), tile, accs, 128, offset)
    for k in range(8):
        out[k] = total


def fourth_kernel(
    info, src, tgt, rows, targets, parts, mass, former, reference, norms, hot,
    out, final, columns, extra, offset, total, *accs,
):
    count, mine = info[0], info[1]
    new = former[...] + mass[...] - jnp.log(jnp.sum(parts[...], axis=0))
    spread(new, columns, extra)
    final[...] = EPS * (new + norms[...] * (SCALE / 2))
    offset[pl.ds(0, 64), :] = reference[...] * LOG2E
    offset[pl.ds(64, 8), :] = jnp.zeros((8, BLK), f32)
    tile = by_target(rows, targets, extra, hot, mine)
    total[...] = plain_sum(count, picker(src, tgt, False), tile, accs, 64, offset)
    for k in range(4):
        out[k] = total[pl.ds(k, 16, stride=4), :]


def total_kernel(parts, out):
    out[...] = jnp.sum(parts[...], axis=0)[:, None, :]


def last_kernel(info, parts, mass, potential, cells, out):
    me = info[3]
    total = jnp.sum(parts[...], axis=0)
    new = potential[pl.ds(me, 1), :] + mass[pl.ds(me, 1), :] - jnp.log(total)
    out[...] = EPS * (new + norm_row(cells[...]) * (SCALE / 2))


def call(kernel, kinds, outs, scratch=()):
    specs = [pl.BlockSpec(memory_space=SMEM if kind == "s" else VMEM) for kind in kinds]
    out_specs = [pl.BlockSpec(memory_space=VMEM) for _ in outs]
    shapes = [jax.ShapeDtypeStruct(shape, dtype) for shape, dtype in outs]
    single = len(outs) == 1
    return pl.pallas_call(
        kernel,
        in_specs=specs,
        out_specs=out_specs[0] if single else out_specs,
        out_shape=shapes[0] if single else shapes,
        scratch_shapes=list(scratch),
        compiler_params=pltpu.CompilerParams(vmem_limit_bytes=32 * 1024 * 1024),
        name=kernel.__name__,
    )


def columns_of(blocks):
    return [VMEM((blocks * 4, BLK), f32), VMEM((blocks // 16, BLK, BLK), bf16)]


def accumulators(owners, kinds):
    return [VMEM(((owners + 1) * 8, BLK), f32) for _ in range(WAYS * kinds)]


def on_device(source_cells, target_cells, start, source_logmass, target_logmass, pair_src, pair_tgt, pair_count):
    ring = [[z * 4 + r for z in range(16)] for r in range(4)]
    chips = [[z * 4 + r for r in range(4)] for z in range(16)]
    cores = [[i, i + 1] for i in range(0, 64, 2)]
    to_core = [(i, i ^ 1) for i in range(64)]
    to_chip = [(i, i ^ 2) for i in range(64)]

    me = lax.axis_index("src")
    info = jnp.stack([pair_count.reshape(()), lax.rem(me, 4), lax.rem(me, 2), me]).astype(jnp.int32)
    src, tgt = pair_src.reshape(-1), pair_tgt.reshape(-1)

    mine = target_cells.T
    own = lax.all_to_all(jnp.broadcast_to(mine[None], (16, DIM, BLK)), "src", 0, 0, axis_index_groups=ring)
    other = lax.ppermute(own, "src", to_chip)
    core = lax.ppermute(own, "src", to_core)
    both = lax.ppermute(other, "src", to_core)

    sources = source_cells.T
    source_mass = source_logmass.reshape(-1, BLK)
    target_mass = target_logmass.reshape(-1, BLK)
    rows, norms, hot = call(
        prepare_kernel, "v", [((128, BLK, BLK), bf16), ((128, BLK), f32), ((16, DIM, BLK), bf16)]
    )(sources)

    parts, target_rows, targets = call(
        first_kernel,
        "sssvvvvvvv",
        [((8, 128, BLK), f32), ((64, BLK, BLK), bf16), ((64, DIM, BLK), bf16)],
        [VMEM((64, BLK), f32)] + columns_of(64) + accumulators(128, 2),
    )(info, src, tgt, sources, own, core, other, both, start.reshape(-1, BLK), hot)
    parts = lax.all_to_all(parts, "tgt", 0, 0)
    lse, first_u = call(
        second_kernel,
        "sssvvvvv",
        [((4, 64, BLK), f32), ((128, BLK), f32)],
        columns_of(128) + accumulators(64, 2),
    )(info, src, tgt, rows, targets, parts, source_mass, hot)
    lse = lax.all_to_all(lse, "src", 0, 0, axis_index_groups=chips)
    lse = call(group_kernel, "sv", [((16, 32, BLK), f32)])(info, lse)
    lse = lax.all_to_all(lse, "src", 0, 0, axis_index_groups=ring)
    lse = call(ring_kernel, "v", [((32, BLK), f32)])(lse)
    lse = lax.all_gather(lse, "src", axis=0, axis_index_groups=cores, tiled=True)
    parts, first_v = call(
        third_kernel,
        "sssvvvvvv",
        [((8, 128, BLK), f32), ((64, BLK), f32)],
        columns_of(64) + [VMEM((136, BLK), f32)] + accumulators(128, 1),
    )(info, src, tgt, sources, target_rows, lse, target_mass, first_u, hot)
    parts = lax.all_to_all(parts, "tgt", 0, 0)
    sums, last_u = call(
        fourth_kernel,
        "sssvvvvvvvv",
        [((4, 16, BLK), f32), ((128, BLK), f32)],
        columns_of(128) + [VMEM((72, BLK), f32), VMEM((64, BLK), f32)] + accumulators(64, 1),
    )(info, src, tgt, rows, targets, parts, source_mass, first_u, first_v, norms, hot)
    sums = lax.all_to_all(sums, "src", 0, 0, axis_index_groups=chips)
    sums = call(total_kernel, "v", [((16, 1, BLK), f32)])(sums)
    sums = lax.all_to_all(sums, "src", 0, 0, axis_index_groups=ring)
    last_v = call(last_kernel, "svvvv", [((1, BLK), f32)])(info, sums, target_mass, first_v, mine)
    return last_u.reshape(-1), last_v.reshape(-1)


def solution(mesh):
    in_specs = (
        P("src", None),
        P(("tgt", "src"), None),
        P("tgt"),
        P("src"),
        P("tgt"),
        P("src", "tgt", None),
        P("src", "tgt", None),
        P("src", "tgt"),
    )
    out_specs = (P("src"), P(("tgt", "src")))
    return jax.shard_map(
        on_device, mesh=mesh, in_specs=in_specs, out_specs=out_specs, check_vma=False
    )
```

time: 248 us -> 172 us (0.69)
  Pallas kernels: 67.3 us -> 19.1 us
  waiting for transfers between devices: 11.1 us -> 0.01 us
  starting transfers between devices: 25.2 us -> 16.3 us
  local copies, waits for them, and re-layouts: 8.71 us -> 2.39 us
    all_to_all x1 -> x2, blocking collectives: 28.7 us -> 49 us  [the longest x1 28.7 us: on_device(): lax.all_to_all(jnp.broadcast_to(mine[None], (16, DIM, BLK)), 'src', 0, 0,...]
    pallas_call x1 -> x2, Pallas kernels: 25.9 us -> 5.65 us  [the longest x1 4.01 us: on_device(): call(fourth_kernel, 'sssvvvvvvvv', [((4, 16, BLK), f32), ((128, BLK), f32...]
    pallas_call x1, Pallas kernels: 23.6 us -> 4.6 us  [on_device(): call(first_kernel, 'sssvvvvvvv', [((8, 128, BLK), f32), ((64, BLK, BLK),...]
    all_to_all x1, blocking collectives: 18.8 us -> 7.29 us  [on_device(): lse = lax.all_to_all(lse, 'src', 0, 0, axis_index_groups=chips)]
    all_to_all x1 -> x0, waiting for transfers between devices: 11.1 us -> none  [on_device(): sums = lax.all_to_all(sums, 'src', 0, 0, axis_index_groups=ring)]
    all_to_all x1 -> x0, starting transfers between devices: 8.91 us -> none  [on_device(): sums = lax.all_to_all(sums, 'src', 0, 0, axis_index_groups=ring)]
    pallas_call x1, Pallas kernels: 9.93 us -> 3.95 us  [on_device(): call(second_kernel, 'sssvvvvv', [((4, 64, BLK), f32), ((128, BLK), f32)],...]
    all_to_all x2, blocking collectives: 41.6 us -> 36.8 us  [on_device(): parts = lax.all_to_all(parts, 'tgt', 0, 0)]
  transfers between devices with their start and end apart: 4 -> 3, of which waited for: 1 -> 0; matrix products, arithmetic and copies ran while one was open for 3% -> 0% of each run, Pallas kernels for 0% -> 1%
where the time goes in v2:
time: 172 us
  blocking collectives  132 us (77%)
  Pallas kernels  19.1 us (11%)
  starting transfers between devices  16.3 us (9%)
  local copies, waits for them, and re-layouts  2.39 us (1%)
    all_to_all x2, blocking collectives, on_device(): parts = lax.all_to_all(parts, 'tgt', 0, 0)  36.8 us
    all_to_all x1, blocking collectives, on_device(): lax.all_to_all(jnp.broadcast_to(mine[None], (16, DIM, BLK)), 'src', 0, 0,...  28.7 us
    all_to_all x1, blocking collectives, on_device(): lse = lax.all_to_all(lse, 'src', 0, 0, axis_index_groups=ring)  23.6 us
    all_to_all x1, blocking collectives, on_device(): sums = lax.all_to_all(sums, 'src', 0, 0, axis_index_groups=ring)  20.3 us
    ppermute x1, starting transfers between devices, on_device(): core = lax.ppermute(own, 'src', to_core)  8.37 us
    all_gather x1, blocking collectives, on_device(): lax.all_gather(lse, 'src', axis=0, axis_index_groups=cores, tiled=True)  7.98 us
    all_to_all x1, blocking collectives, on_device(): sums = lax.all_to_all(sums, 'src', 0, 0, axis_index_groups=chips)  7.57 us
    all_to_all x1, blocking collectives, on_device(): lse = lax.all_to_all(lse, 'src', 0, 0, axis_index_groups=chips)  7.29 us
  transfers between devices with their start and end apart: 3, of which 0 were waited for; matrix products, arithmetic and copies ran while one was open for 0% of the time, Pallas kernels for 1%

profile of v2, /device:TPU:1, one launch (start us, length us, event | category | flops | bytes accessed | tf_op | source)
XLA Modules:
  0.0 171.6 jit_solution(2700981156110399271)
XLA Ops:
  0.7 0.8 broadcast_in_dim.2
  1.4 28.7 %all_to_all.35.own = bf16[16,64,128]{2,1,0:T(8,128)(2,1)S(1)} all-to-all(bf16[16,64,128]{2,1,0:T(8,128)(2,1)S(1)} %broadcast_in_dim.2), channel_id=1, replica_groups={{0,32,64,96,128,160,192,224,256,288,320,352,384,416,448,480},{8,40,72,1..., dimensions={0} | all-to-all | bytes 524288 | tf_op jit(solution)/shard_map/all_to_all | solution.py:276
  30.1 3.1 %collective-permute-start.1 = (bf16[16,64,128]{2,1,0:T(8,128)(2,1)S(1)}, bf16[16,64,128]{2,1,0:T(8,128)(2,1)S(1)}, u32[]{:S(2)}, u32[]{:S(2)}) collective-permute-start(bf16[16,64,128]{2,1,0:T(8,128)(2,1)S(1)} %all_to_all.35.own), channel_id=1, source_target_pairs={{0,16},{8,24},{16,0},{24,8},{32,48},{40,56},{48,32},{56,40},{64,80... | collective-permute-start | bytes 786440 | tf_op jit(solution)/shard_map/ppermute | solution.py:277
  33.2 8.4 %collective-permute-start = (bf16[16,64,128]{2,1,0:T(8,128)(2,1)S(1)}, bf16[16,64,128]{2,1,0:T(8,128)(2,1)S(1)}, u32[]{:S(2)}, u32[]{:S(2)}) collective-permute-start(bf16[16,64,128]{2,1,0:T(8,128)(2,1)S(1)} %all_to_all.35.own), channel_id=1, source_target_pairs={{0,8},{8,0},{16,24},{24,16},{32,40},{40,32},{48,56},{56,48},{64,72... | collective-permute-start | bytes 786440 | tf_op jit(solution)/shard_map/ppermute | solution.py:278
  41.6 4.8 %collective-permute-start.2 = (bf16[16,64,128]{2,1,0:T(8,128)(2,1)S(1)}, bf16[16,64,128]{2,1,0:T(8,128)(2,1)S(1)}, u32[]{:S(2)}, u32[]{:S(2)}) collective-permute-start(bf16[16,64,128]{2,1,0:T(8,128)(2,1)S(1)} %collective-permute-done.1.other), channel_id=1, source_target_pairs={{0,8},{8,0},{16,24},{24,16},{32,40},{40,32},{48,56},{56,48},{64,72... | collective-permute-start | bytes 786440 | tf_op jit(solution)/shard_map/ppermute | solution.py:279
  47.1 0.0 copy-start
  47.1 1.6 copy-done
  48.7 1.6 prepare_kernel.1
  50.4 0.1 pad_add_fusion.info
  50.5 0.0 copy-start.2
  50.5 4.6 %first_kernel.1 = (f32[8,128,128]{2,1,0:T(8,128)S(1)}, bf16[64,128,128]{2,1,0:T(8,128)(2,1)S(1)}, bf16[64,64,128]{2,1,0:T(8,128)(2,1)S(1)}) custom-call(s32[4]{0:T(128)S(1)} %pad_add_fusion.info, s32[256]{0:T(256)S(1)} %bitcast.24, s32[256]{0:T(256)S(1)} %bitcast.28, bf16[64,16384]{1,0:T(8,128)(2,1)S(1)} %bitcast.15, ...), custom_call_target="tpu_custom_call" | custom-call | tf_op jit(solution)/shard_map/first_kernel/pallas_call | solution.py:288
  55.1 20.4 %all_to_all.36.parts = f32[8,128,128]{2,1,0:T(8,128)S(1)} all-to-all(f32[8,128,128]{2,1,0:T(8,128)S(1)} %get-tuple-element.18), channel_id=1, replica_groups=mesh['src'=64,'tgt'=8] {'tgt'}, dimensions={0} | all-to-all | bytes 1048576 | tf_op jit(solution)/shard_map/all_to_all | solution.py:294
  75.5 3.9 %second_kernel.1 = (f32[4,64,128]{2,1,0:T(8,128)S(1)}, f32[128,128]{1,0:T(8,128)S(1)}) custom-call(s32[4]{0:T(128)S(1)} %pad_add_fusion.info, s32[256]{0:T(256)S(1)} %bitcast.25, s32[256]{0:T(256)S(1)} %bitcast.29, bf16[128,128,128]{2,1,0:T(8,128)(2,1)S(1)} %get-tuple-element.14.rows, bf16[64,64,128]{2,1,0:T(8,128)(2,1)S(1)} %get-tuple-element.16.targets, ...), custom_call_target="tpu_custom_call" | custom-call | tf_op jit(solution)/shard_map/second_kernel/pallas_call | solution.py:295
  79.5 7.3 %all_to_all.37.parts = f32[4,64,128]{2,1,0:T(8,128)S(1)} all-to-all(f32[4,64,128]{2,1,0:T(8,128)S(1)} %get-tuple-element.19), channel_id=1, replica_groups={{0,8,16,24},{32,40,48,56},{64,72,80,88},{96,104,112,120},{128,136,144,1..., dimensions={0} | all-to-all | bytes 262144 | tf_op jit(solution)/shard_map/all_to_all | solution.py:301
  86.8 0.6 group_kernel.1
  87.3 23.6 %all_to_all.38.parts = f32[16,32,128]{2,1,0:T(8,128)S(1)} all-to-all(f32[16,32,128]{2,1,0:T(8,128)S(1)} %group_kernel.1), channel_id=1, replica_groups={{0,32,64,96,128,160,192,224,256,288,320,352,384,416,448,480},{8,40,72,1..., dimensions={0} | all-to-all | bytes 524288 | tf_op jit(solution)/shard_map/all_to_all | solution.py:303
  111.0 0.1 ring_kernel.1
  111.0 8.0 %all_gather.3.lse = f32[64,128]{1,0:T(8,128)S(1)} all-gather(f32[32,128]{1,0:T(8,128)S(1)} %ring_kernel.1), channel_id=1, replica_groups={{0,8},{16,24},{32,40},{48,56},{64,72},{80,88},{96,104},{112,120},{128,1..., dimensions={0}, use_global_device_ids=true | all-gather | bytes 49152 | tf_op jit(solution)/shard_map/all_gather | solution.py:305
  119.0 3.2 %third_kernel.1 = (f32[8,128,128]{2,1,0:T(8,128)S(1)}, f32[64,128]{1,0:T(8,128)S(1)}) custom-call(s32[4]{0:T(128)S(1)} %pad_add_fusion.info, s32[256]{0:T(256)S(1)} %bitcast.26, s32[256]{0:T(256)S(1)} %bitcast.30, bf16[64,16384]{1,0:T(8,128)(2,1)S(1)} %bitcast.16, bf16[64,128,128]{2,1,0:T(8,128)(2,1)S(1)} %get-tuple-element.17.rows, ...), custom_call_target="tpu_custom_call" | custom-call | tf_op jit(solution)/shard_map/third_kernel/pallas_call | solution.py:306
  122.2 16.4 %all_to_all.39.parts = f32[8,128,128]{2,1,0:T(8,128)S(1)} all-to-all(f32[8,128,128]{2,1,0:T(8,128)S(1)} %get-tuple-element.21), channel_id=1, replica_groups=mesh['src'=64,'tgt'=8] {'tgt'}, dimensions={0} | all-to-all | bytes 1048576 | tf_op jit(solution)/shard_map/all_to_all | solution.py:312
  138.6 4.0 %fourth_kernel.1 = (f32[4,16,128]{2,1,0:T(8,128)S(1)}, f32[128,128]{1,0:T(8,128)}) custom-call(s32[4]{0:T(128)S(1)} %pad_add_fusion.info, s32[256]{0:T(256)S(1)} %bitcast.27, s32[256]{0:T(256)S(1)} %bitcast.31, bf16[128,128,128]{2,1,0:T(8,128)(2,1)S(1)} %get-tuple-element.14.rows, bf16[64,64,128]{2,1,0:T(8,128)(2,1)S(1)} %get-tuple-element.16.targets, ...), custom_call_target="tpu_custom_call" | custom-call | tf_op jit(solution)/shard_map/fourth_kernel/pallas_call | solution.py:313
  142.6 7.6 %all_to_all.40.parts = f32[4,16,128]{2,1,0:T(8,128)S(1)} all-to-all(f32[4,16,128]{2,1,0:T(8,128)S(1)} %get-tuple-element.25), channel_id=1, replica_groups={{0,8,16,24},{32,40,48,56},{64,72,80,88},{96,104,112,120},{128,136,144,1..., dimensions={0} | all-to-all | bytes 65536 | tf_op jit(solution)/shard_map/all_to_all | solution.py:319
  150.2 20.3 %all_to_all.41.parts = f32[16,1,128]{2,1,0:T(1,128)S(1)} all-to-all(f32[16,1,128]{2,1,0:T(1,128)S(1)} %total_kernel.1), channel_id=1, replica_groups={{0,32,64,96,128,160,192,224,256,288,320,352,384,416,448,480},{8,40,72,1..., dimensions={0} | all-to-all | bytes 16384 | tf_op jit(solution)/shard_map/all_to_all | solution.py:321
  170.5 1.1 last_kernel.1
  (17 shorter events, 0.0 us)
Async XLA Ops:
  0.6 49.8 %copy-start.7 = (s32[1,1,256]{2,1,0:T(1,128)S(1)}, s32[1,1,256]{2,1,0:T(1,128)}, u32[]{:S(2)}) copy-start(s32[1,1,256]{2,1,0:T(1,128)} %param.14) | copy-start | bytes 3076
  0.6 49.8 %copy-start.6 = (s32[1,1,256]{2,1,0:T(1,128)S(1)}, s32[1,1,256]{2,1,0:T(1,128)}, u32[]{:S(2)}) copy-start(s32[1,1,256]{2,1,0:T(1,128)} %param.13) | copy-start | bytes 3076
  0.7 49.8 %copy-start.5 = (f32[8192]{0:T(1024)S(1)}, f32[8192]{0:T(1024)}, u32[]{:S(2)}) copy-start(f32[8192]{0:T(1024)} %param.10) | copy-start | bytes 98308
  30.1 11.5 %collective-permute-start.1 = (bf16[16,64,128]{2,1,0:T(8,128)(2,1)S(1)}, bf16[16,64,128]{2,1,0:T(8,128)(2,1)S(1)}, u32[]{:S(2)}, u32[]{:S(2)}) collective-permute-start(bf16[16,64,128]{2,1,0:T(8,128)(2,1)S(1)} %all_to_all.35.own), channel_id=1, source_target_pairs={{0,16},{8,24},{16,0},{24,8},{32,48},{40,56},{48,32},{56,40},{64,80... | collective-permute-start | bytes 786440 | tf_op jit(solution)/shard_map/ppermute | solution.py:277
  33.2 17.2 %collective-permute-start = (bf16[16,64,128]{2,1,0:T(8,128)(2,1)S(1)}, bf16[16,64,128]{2,1,0:T(8,128)(2,1)S(1)}, u32[]{:S(2)}, u32[]{:S(2)}) collective-permute-start(bf16[16,64,128]{2,1,0:T(8,128)(2,1)S(1)} %all_to_all.35.own), channel_id=1, source_target_pairs={{0,8},{8,0},{16,24},{24,16},{32,40},{40,32},{48,56},{56,48},{64,72... | collective-permute-start | bytes 786440 | tf_op jit(solution)/shard_map/ppermute | solution.py:278
  41.6 8.8 %collective-permute-start.2 = (bf16[16,64,128]{2,1,0:T(8,128)(2,1)S(1)}, bf16[16,64,128]{2,1,0:T(8,128)(2,1)S(1)}, u32[]{:S(2)}, u32[]{:S(2)}) collective-permute-start(bf16[16,64,128]{2,1,0:T(8,128)(2,1)S(1)} %collective-permute-done.1.other), channel_id=1, source_target_pairs={{0,8},{8,0},{16,24},{24,16},{32,40},{40,32},{48,56},{56,48},{64,72... | collective-permute-start | bytes 786440 | tf_op jit(solution)/shard_map/ppermute | solution.py:279
  47.1 1.6 copy-start
  50.5 25.0 %copy-start.2 = (f32[16384]{0:T(1024)S(1)}, f32[16384]{0:T(1024)}, u32[]{:S(2)}) copy-start(f32[16384]{0:T(1024)} %param.11) | copy-start | bytes 196612
  75.5 43.5 %copy-start.1 = (bf16[16384,64]{0,1:T(8,128)(2,1)S(1)}, bf16[16384,64]{0,1:T(8,128)(2,1)}, u32[]{:S(2)}) copy-start(bf16[16384,64]{0,1:T(8,128)(2,1)} %param.8) | copy-start | bytes 6291460
  75.5 43.5 %copy-start.3 = (f32[8192]{0:T(1024)S(1)}, f32[8192]{0:T(1024)}, u32[]{:S(2)}) copy-start(f32[8192]{0:T(1024)} %param.12) | copy-start | bytes 98308
  138.6 31.9 %copy-start.4 = (bf16[128,64]{0,1:T(8,128)(2,1)S(1)}, bf16[128,64]{0,1:T(8,128)(2,1)}, u32[]{:S(2)}) copy-start(bf16[128,64]{0,1:T(8,128)(2,1)} %param.9) | copy-start | bytes 49156

commit v3 on v2

--- a/solution.py
+++ b/solution.py
@@ -14,7 +14,8 @@
 LOG2E = 1.4426950408889634
 KAPPA = SCALE * LOG2E
 LOWEST = -1e30
-UNROLL = 32
+CHUNKS = 8
+UNROLL = 64
 WAYS = 4
 VMEM = pltpu.VMEM
 SMEM = pltpu.SMEM
@@ -99,21 +100,20 @@
     return jnp.concatenate(out, axis=0)
 
 
-def plain_sum(count, pick, tile, sums, owners, offset_ref):
-    for total in sums:
-        total[...] = jnp.zeros(total.shape, f32)
+def plain_sum(count, pick, tile, total, owners, offset_ref):
+    total[...] = jnp.zeros(total.shape, f32)
 
     def work(slots):
         parts = []
         for s in slots:
             offset = offset_ref[pl.ds(s["owner"], 1), :]
             parts.append(jnp.sum(jnp.exp2(tile(s) * KAPPA + offset[None]), axis=0))
-        for q, (s, part) in enumerate(zip(slots, parts)):
-            rows, total = owner_rows(s), sums[q % WAYS]
+        for s, part in zip(slots, parts):
+            rows = owner_rows(s)
             total[rows, :] = total[rows, :] + part
 
     over_pairs(count, pick, work)
-    return jnp.concatenate([functools.reduce(jnp.add, strided(sums, g)) for g in range(owners // 8)], axis=0)
+    return jnp.concatenate([functools.reduce(jnp.add, strided([total], g)) for g in range(owners // 8)], axis=0)
 
 
 def place_of(t, mine):
@@ -136,18 +136,25 @@
     return lambda p: pair_tile(sources, extra, hot, p["s"], p["s"], targets[place_of(p["t"], mine)])
 
 
-def prepare_kernel(cells, rows, norms, hot):
-    def some(n, carry):
-        for q in range(16):
-            block = cells[:, block_of(n * 16 + q)]
-            rows[n * 16 + q] = as_rows(block)
-            norms[pl.ds(n * 16 + q, 1), :] = norm_row(block)
-        return carry
-
-    lax.fori_loop(0, 8, some, 0)
+def prepare_kernel(cells, sources, rows, norms, hot, sems):
+    width = sources.shape[1] // CHUNKS
+
+    def chunk(n):
+        part = pl.ds(n * width, width)
+        return pltpu.make_async_copy(cells.at[:, part], sources.at[:, part], sems.at[n])
+
+    for n in range(CHUNKS):
+        chunk(n).start()
     line = lax.broadcasted_iota(jnp.int32, (DIM, BLK), 0)
     for r in range(16):
         hot[r] = jnp.where((line >= 4 * r) & (line < 4 * r + 3), 1.0, 0.0).astype(bf16)
+    for n in range(CHUNKS):
+        chunk(n).wait()
+        for q in range(128 // CHUNKS):
+            b = n * (128 // CHUNKS) + q
+            block = sources[:, b * BLK : b * BLK + BLK]
+            rows[b] = as_rows(block)
+            norms[b : b + 1, :] = norm_row(block)
 
 
 def merge_lse(parts_ref):
@@ -181,14 +188,13 @@
     tile = by_target(rows, targets, extra, hot, mine)
     lse = stable_lse(count, picker(src, tgt, False), tile, accs[:WAYS], accs[WAYS:], 64)
     for k in range(4):
+        out[k] = lse[16 * k : 16 * k + 16]
+
+
+def group_kernel(parts, out):
+    lse = merge_lse(parts)
+    for k in range(16):
         out[k] = lse
-
-
-def group_kernel(info, parts, out):
-    lse = merge_lse(parts)
-    half = jnp.where(info[2] == 0, lse[:32], lse[32:])
-    for k in range(16):
-        out[k] = half
 
 
 def ring_kernel(parts, out):
@@ -196,7 +202,7 @@
 
 
 def third_kernel(
-    info, src, tgt, sources, rows, lse, mass, reference, hot, out, potential, columns, extra, offset, *accs
+    info, src, tgt, sources, rows, lse, mass, reference, hot, out, potential, columns, extra, offset, acc
 ):
     count, mine = info[0], info[1]
     new = mass[...] - lse[...]
@@ -205,14 +211,14 @@
     offset[pl.ds(0, 128), :] = reference[...] * LOG2E
     offset[pl.ds(128, 8), :] = jnp.zeros((8, BLK), f32)
     tile = by_source(rows, sources, extra, hot, mine)
-    total = plain_sum(count, picker(src, tgt, True), tile, accs, 128, offset)
+    total = plain_sum(count, picker(src, tgt, True), tile, acc, 128, offset)
     for k in range(8):
         out[k] = total
 
 
 def fourth_kernel(
     info, src, tgt, rows, targets, parts, mass, former, reference, norms, hot,
-    out, final, columns, extra, offset, total, *accs,
+    out, final, columns, extra, offset, acc,
 ):
     count, mine = info[0], info[1]
     new = former[...] + mass[...] - jnp.log(jnp.sum(parts[...], axis=0))
@@ -221,13 +227,12 @@
     offset[pl.ds(0, 64), :] = reference[...] * LOG2E
     offset[pl.ds(64, 8), :] = jnp.zeros((8, BLK), f32)
     tile = by_target(rows, targets, extra, hot, mine)
-    total[...] = plain_sum(count, picker(src, tgt, False), tile, accs, 64, offset)
-    for k in range(4):
-        out[k] = total[pl.ds(k, 16, stride=4), :]
-
-
-def total_kernel(parts, out):
-    out[...] = jnp.sum(parts[...], axis=0)[:, None, :]
+    out[...] = plain_sum(count, picker(src, tgt, False), tile, acc, 64, offset)
+
+
+def total_kernel(info, parts, out):
+    even, odd = [parts[0, pl.ds(k, 32, stride=2), :] + parts[1, pl.ds(k, 32, stride=2), :] for k in range(2)]
+    out[...] = jnp.where(info[2] == 0, even, odd)[:, None, :]
 
 
 def last_kernel(info, parts, mass, potential, cells, out):
@@ -238,7 +243,8 @@
 
 
 def call(kernel, kinds, outs, scratch=()):
-    specs = [pl.BlockSpec(memory_space=SMEM if kind == "s" else VMEM) for kind in kinds]
+    spaces = {"s": SMEM, "v": VMEM, "a": pl.ANY}
+    specs = [pl.BlockSpec(memory_space=spaces[kind]) for kind in kinds]
     out_specs = [pl.BlockSpec(memory_space=VMEM) for _ in outs]
     shapes = [jax.ShapeDtypeStruct(shape, dtype) for shape, dtype in outs]
     single = len(outs) == 1
@@ -257,52 +263,55 @@
     return [VMEM((blocks * 4, BLK), f32), VMEM((blocks // 16, BLK, BLK), bf16)]
 
 
-def accumulators(owners, kinds):
-    return [VMEM(((owners + 1) * 8, BLK), f32) for _ in range(WAYS * kinds)]
+def accumulators(owners, number):
+    return [VMEM(((owners + 1) * 8, BLK), f32) for _ in range(number)]
 
 
 def on_device(source_cells, target_cells, start, source_logmass, target_logmass, pair_src, pair_tgt, pair_count):
     ring = [[z * 4 + r for z in range(16)] for r in range(4)]
     chips = [[z * 4 + r for r in range(4)] for z in range(16)]
     cores = [[i, i + 1] for i in range(0, 64, 2)]
+    halves = [[2 * i + c for i in range(32)] for c in range(2)]
     to_core = [(i, i ^ 1) for i in range(64)]
     to_chip = [(i, i ^ 2) for i in range(64)]
 
     me = lax.axis_index("src")
     info = jnp.stack([pair_count.reshape(()), lax.rem(me, 4), lax.rem(me, 2), me]).astype(jnp.int32)
     src, tgt = pair_src.reshape(-1), pair_tgt.reshape(-1)
+    source_mass = source_logmass.reshape(-1, BLK)
+    target_mass = target_logmass.reshape(-1, BLK)
 
     mine = target_cells.T
     own = lax.all_to_all(jnp.broadcast_to(mine[None], (16, DIM, BLK)), "src", 0, 0, axis_index_groups=ring)
     other = lax.ppermute(own, "src", to_chip)
     core = lax.ppermute(own, "src", to_core)
+    sources, rows, norms, hot = call(
+        prepare_kernel,
+        "a",
+        [((DIM, 128 * BLK), bf16), ((128, BLK, BLK), bf16), ((128, BLK), f32), ((16, DIM, BLK), bf16)],
+        [pltpu.SemaphoreType.DMA((CHUNKS,))],
+    )(source_cells.T)
+    other, hot = lax.optimization_barrier((other, hot))
     both = lax.ppermute(other, "src", to_core)
-
-    sources = source_cells.T
-    source_mass = source_logmass.reshape(-1, BLK)
-    target_mass = target_logmass.reshape(-1, BLK)
-    rows, norms, hot = call(
-        prepare_kernel, "v", [((128, BLK, BLK), bf16), ((128, BLK), f32), ((16, DIM, BLK), bf16)]
-    )(sources)
 
     parts, target_rows, targets = call(
         first_kernel,
         "sssvvvvvvv",
         [((8, 128, BLK), f32), ((64, BLK, BLK), bf16), ((64, DIM, BLK), bf16)],
-        [VMEM((64, BLK), f32)] + columns_of(64) + accumulators(128, 2),
+        [VMEM((64, BLK), f32)] + columns_of(64) + accumulators(128, 2 * WAYS),
     )(info, src, tgt, sources, own, core, other, both, start.reshape(-1, BLK), hot)
     parts = lax.all_to_all(parts, "tgt", 0, 0)
     lse, first_u = call(
         second_kernel,
         "sssvvvvv",
-        [((4, 64, BLK), f32), ((128, BLK), f32)],
-        columns_of(128) + accumulators(64, 2),
+        [((4, 16, BLK), f32), ((128, BLK), f32)],
+        columns_of(128) + accumulators(64, 2 * WAYS),
     )(info, src, tgt, rows, targets, parts, source_mass, hot)
     lse = lax.all_to_all(lse, "src", 0, 0, axis_index_groups=chips)
-    lse = call(group_kernel, "sv", [((16, 32, BLK), f32)])(info, lse)
+    lse = call(group_kernel, "v", [((16, 16, BLK), f32)])(lse)
     lse = lax.all_to_all(lse, "src", 0, 0, axis_index_groups=ring)
-    lse = call(ring_kernel, "v", [((32, BLK), f32)])(lse)
-    lse = lax.all_gather(lse, "src", axis=0, axis_index_groups=cores, tiled=True)
+    lse = call(ring_kernel, "v", [((16, BLK), f32)])(lse)
+    lse = lax.all_gather(lse, "src", axis=0, axis_index_groups=chips, tiled=True)
     parts, first_v = call(
         third_kernel,
         "sssvvvvvv",
@@ -313,12 +322,12 @@
     sums, last_u = call(
         fourth_kernel,
         "sssvvvvvvvv",
-        [((4, 16, BLK), f32), ((128, BLK), f32)],
-        columns_of(128) + [VMEM((72, BLK), f32), VMEM((64, BLK), f32)] + accumulators(64, 1),
+        [((64, BLK), f32), ((128, BLK), f32)],
+        columns_of(128) + [VMEM((72, BLK), f32)] + accumulators(64, 1),
     )(info, src, tgt, rows, targets, parts, source_mass, first_u, first_v, norms, hot)
-    sums = lax.all_to_all(sums, "src", 0, 0, axis_index_groups=chips)
-    sums = call(total_kernel, "v", [((16, 1, BLK), f32)])(sums)
-    sums = lax.all_to_all(sums, "src", 0, 0, axis_index_groups=ring)
+    sums = lax.all_gather(sums, "src", axis=0, axis_index_groups=cores)
+    sums = call(total_kernel, "sv", [((32, 1, BLK), f32)])(info, sums)
+    sums = lax.all_to_all(sums, "src", 0, 0, axis_index_groups=halves)
     last_v = call(last_kernel, "svvvv", [((1, BLK), f32)])(info, sums, target_mass, first_v, mine)
     return last_u.reshape(-1), last_v.reshape(-1)
 

time: 172 us -> 164 us (0.953)
  blocking collectives: 132 us -> 122 us
  starting transfers between devices: 16.3 us -> 13.4 us
  Pallas kernels: 19.1 us -> 21.3 us
  local copies, waits for them, and re-layouts: 2.39 us -> 4.35 us
    all_to_all x2 -> x1, blocking collectives: 27.9 us -> 18.7 us  [on_device(): sums = lax.all_to_all(sums, 'src', 0, 0, axis_index_groups=halves)]
    all_to_all x1, blocking collectives: 23.6 us -> 18.4 us  [on_device(): lse = lax.all_to_all(lse, 'src', 0, 0, axis_index_groups=ring)]
    all_gather x1 -> x2, blocking collectives: 7.98 us -> 12.8 us  [the longest x1 8.76 us: on_device(): lax.all_gather(lse, 'src', axis=0, axis_index_groups=chips, tiled=True)]
    ppermute x1, starting transfers between devices: 4.83 us -> 1.92 us  [on_device(): both = lax.ppermute(other, 'src', to_core)]
    unnamed x16 -> x18, local copies, waits for them, and re-layouts: 1.62 us -> 3.58 us
  transfers between devices with their start and end apart: 3 -> 3, of which waited for: 0 -> 1; matrix products, arithmetic and copies ran while one was open for 0% -> 0% of each run, Pallas kernels for 1% -> 1%
where the time goes in v3:
time: 164 us
  blocking collectives  122 us (74%)
  Pallas kernels  21.3 us (13%)
  starting transfers between devices  13.4 us (8%)
  local copies, waits for them, and re-layouts  4.35 us (3%)
    all_to_all x2, blocking collectives, on_device(): parts = lax.all_to_all(parts, 'tgt', 0, 0)  35.2 us
    all_to_all x1, blocking collectives, on_device(): lax.all_to_all(jnp.broadcast_to(mine[None], (16, DIM, BLK)), 'src', 0, 0,...  28.7 us
    all_to_all x1, blocking collectives, on_device(): sums = lax.all_to_all(sums, 'src', 0, 0, axis_index_groups=halves)  18.7 us
    all_to_all x1, blocking collectives, on_device(): lse = lax.all_to_all(lse, 'src', 0, 0, axis_index_groups=ring)  18.4 us
    all_gather x1, blocking collectives, on_device(): lax.all_gather(lse, 'src', axis=0, axis_index_groups=chips, tiled=True)  8.76 us
    all_to_all x1, blocking collectives, on_device(): lse = lax.all_to_all(lse, 'src', 0, 0, axis_index_groups=chips)  8.39 us
    ppermute x1, starting transfers between devices, on_device(): core = lax.ppermute(own, 'src', to_core)  8.36 us
    pallas_call x1, Pallas kernels, on_device(): call(first_kernel, 'sssvvvvvvv', [((8, 128, BLK), f32), ((64, BLK, BLK),...  5.23 us
  transfers between devices with their start and end apart: 3, of which 1 were waited for; matrix products, arithmetic and copies ran while one was open for 0% of the time, Pallas kernels for 1%

profile of v3, /device:TPU:1, one launch (start us, length us, event | category | flops | bytes accessed | tf_op | source)
XLA Modules:
  0.0 163.5 jit_solution(16263365290834731932)
XLA Ops:
  0.7 0.8 broadcast_in_dim.2
  1.4 28.7 %all_to_all.30.own = bf16[16,64,128]{2,1,0:T(8,128)(2,1)S(1)} all-to-all(bf16[16,64,128]{2,1,0:T(8,128)(2,1)S(1)} %broadcast_in_dim.2), channel_id=1, replica_groups={{0,32,64,96,128,160,192,224,256,288,320,352,384,416,448,480},{8,40,72,1..., dimensions={0} | all-to-all | bytes 524288 | tf_op jit(solution)/shard_map/all_to_all | solution.py:285
  30.1 3.1 %collective-permute-start.1 = (bf16[16,64,128]{2,1,0:T(8,128)(2,1)S(1)}, bf16[16,64,128]{2,1,0:T(8,128)(2,1)S(1)}, u32[]{:S(2)}, u32[]{:S(2)}) collective-permute-start(bf16[16,64,128]{2,1,0:T(8,128)(2,1)S(1)} %all_to_all.30.own), channel_id=1, source_target_pairs={{0,16},{8,24},{16,0},{24,8},{32,48},{40,56},{48,32},{56,40},{64,80... | collective-permute-start | bytes 786440 | tf_op jit(solution)/shard_map/ppermute | solution.py:286
  33.3 1.6 copy-done.2
  34.8 1.9 %prepare_kernel.1 = (bf16[64,16384]{1,0:T(8,128)(2,1)S(1)}, bf16[128,128,128]{2,1,0:T(8,128)(2,1)S(1)}, f32[128,128]{1,0:T(8,128)S(1)}, bf16[16,64,128]{2,1,0:T(8,128)(2,1)S(1)}) custom-call(bf16[64,16384]{1,0:T(8,128)(2,1)S(1)} %bitcast.15), custom_call_target="tpu_custom_call" | custom-call | tf_op jit(solution)/shard_map/prepare_kernel/pallas_call | solution.py:288
  36.7 2.0 %copy-done = bf16[128,128,128]{2,1,0:T(8,128)(2,1)} copy-done((bf16[128,128,128]{2,1,0:T(8,128)(2,1)}, bf16[128,128,128]{2,1,0:T(8,128)(2,1)S(1)}, u32[]{:S(2)}) %copy-start) | copy-done | bytes 4194328
  38.7 8.4 %collective-permute-start = (bf16[16,64,128]{2,1,0:T(8,128)(2,1)S(1)}, bf16[16,64,128]{2,1,0:T(8,128)(2,1)S(1)}, u32[]{:S(2)}, u32[]{:S(2)}) collective-permute-start(bf16[16,64,128]{2,1,0:T(8,128)(2,1)S(1)} %all_to_all.30.own), channel_id=1, source_target_pairs={{0,8},{8,0},{16,24},{24,16},{32,40},{40,32},{48,56},{56,48},{64,72... | collective-permute-start | bytes 786440 | tf_op jit(solution)/shard_map/ppermute | solution.py:287
  47.1 1.9 %collective-permute-start.2 = (bf16[16,64,128]{2,1,0:T(8,128)(2,1)S(1)}, bf16[16,64,128]{2,1,0:T(8,128)(2,1)S(1)}, u32[]{:S(2)}, u32[]{:S(2)}) collective-permute-start(bf16[16,64,128]{2,1,0:T(8,128)(2,1)S(1)} %collective-permute-done.1.other), channel_id=1, source_target_pairs={{0,8},{8,0},{16,24},{24,16},{32,40},{40,32},{48,56},{56,48},{64,72... | collective-permute-start | bytes 786440 | tf_op jit(solution)/shard_map/ppermute | solution.py:295
  49.6 0.1 pad_add_fusion.info
  49.7 0.8 collective-permute-done.2.both
  50.5 0.0 copy-start.3
  50.5 5.2 %first_kernel.1 = (f32[8,128,128]{2,1,0:T(8,128)S(1)}, bf16[64,128,128]{2,1,0:T(8,128)(2,1)S(1)}, bf16[64,64,128]{2,1,0:T(8,128)(2,1)S(1)}) custom-call(s32[4]{0:T(128)S(1)} %pad_add_fusion.info, s32[256]{0:T(256)S(1)} %bitcast.24, s32[256]{0:T(256)S(1)} %bitcast.28, bf16[64,16384]{1,0:T(8,128)(2,1)S(1)} %get-tuple-element.18.sources, ...), custom_call_target="tpu_custom_call" | custom-call | tf_op jit(solution)/shard_map/first_kernel/pallas_call | solution.py:297
  55.8 19.4 %all_to_all.31.parts = f32[8,128,128]{2,1,0:T(8,128)S(1)} all-to-all(f32[8,128,128]{2,1,0:T(8,128)S(1)} %get-tuple-element.24), channel_id=1, replica_groups=mesh['src'=64,'tgt'=8] {'tgt'}, dimensions={0} | all-to-all | bytes 1048576 | tf_op jit(solution)/shard_map/all_to_all | solution.py:303
  75.2 4.5 %second_kernel.1 = (f32[4,16,128]{2,1,0:T(8,128)S(1)}, f32[128,128]{1,0:T(8,128)S(1)}) custom-call(s32[4]{0:T(128)S(1)} %pad_add_fusion.info, s32[256]{0:T(256)S(1)} %bitcast.25, s32[256]{0:T(256)S(1)} %bitcast.29, bf16[128,128,128]{2,1,0:T(8,128)(2,1)S(1)} %copy-done.1, bf16[64,64,128]{2,1,0:T(8,128)(2,1)S(1)} %get-tuple-element.22.targets, ...), custom_call_target="tpu_custom_call" | custom-call | tf_op jit(solution)/shard_map/second_kernel/pallas_call | solution.py:304
  79.7 8.4 %all_to_all.32.parts = f32[4,16,128]{2,1,0:T(8,128)S(1)} all-to-all(f32[4,16,128]{2,1,0:T(8,128)S(1)} %get-tuple-element.25), channel_id=1, replica_groups={{0,8,16,24},{32,40,48,56},{64,72,80,88},{96,104,112,120},{128,136,144,1..., dimensions={0} | all-to-all | bytes 65536 | tf_op jit(solution)/shard_map/all_to_all | solution.py:310
  88.1 18.4 %all_to_all.33.parts = f32[16,16,128]{2,1,0:T(8,128)S(1)} all-to-all(f32[16,16,128]{2,1,0:T(8,128)S(1)} %group_kernel.1), channel_id=1, replica_groups={{0,32,64,96,128,160,192,224,256,288,320,352,384,416,448,480},{8,40,72,1..., dimensions={0} | all-to-all | bytes 262144 | tf_op jit(solution)/shard_map/all_to_all | solution.py:312
  106.6 8.8 %all_gather.9.lse = f32[64,128]{1,0:T(8,128)S(1)} all-gather(f32[16,128]{1,0:T(8,128)S(1)} %ring_kernel.1), channel_id=1, replica_groups={{0,8,16,24},{32,40,48,56},{64,72,80,88},{96,104,112,120},{128,136,144,1..., dimensions={0}, use_global_device_ids=true | all-gather | bytes 40960 | tf_op jit(solution)/shard_map/all_gather | solution.py:314
  115.4 3.4 %third_kernel.1 = (f32[8,128,128]{2,1,0:T(8,128)S(1)}, f32[64,128]{1,0:T(8,128)S(1)}) custom-call(s32[4]{0:T(128)S(1)} %pad_add_fusion.info, s32[256]{0:T(256)S(1)} %bitcast.26, s32[256]{0:T(256)S(1)} %bitcast.30, bf16[64,16384]{1,0:T(8,128)(2,1)S(1)} %get-tuple-element.18.sources, bf16[64,128,128]{2,1,0:T(8,128)(2,1)S(1)} %get-tuple-element.23.rows, ...), custom_call_target="tpu_custom_call" | custom-call | tf_op jit(solution)/shard_map/third_kernel/pallas_call | solution.py:315
  118.7 15.8 %all_to_all.34.parts = f32[8,128,128]{2,1,0:T(8,128)S(1)} all-to-all(f32[8,128,128]{2,1,0:T(8,128)S(1)} %get-tuple-element.27), channel_id=1, replica_groups=mesh['src'=64,'tgt'=8] {'tgt'}, dimensions={0} | all-to-all | bytes 1048576 | tf_op jit(solution)/shard_map/all_to_all | solution.py:321
  134.5 4.6 %fourth_kernel.1 = (f32[64,128]{1,0:T(8,128)S(1)}, f32[128,128]{1,0:T(8,128)}) custom-call(s32[4]{0:T(128)S(1)} %pad_add_fusion.info, s32[256]{0:T(256)S(1)} %bitcast.27, s32[256]{0:T(256)S(1)} %bitcast.31, bf16[128,128,128]{2,1,0:T(8,128)(2,1)S(1)} %copy-done.1, bf16[64,64,128]{2,1,0:T(8,128)(2,1)S(1)} %get-tuple-element.22.targets, ...), custom_call_target="tpu_custom_call" | custom-call | tf_op jit(solution)/shard_map/fourth_kernel/pallas_call | solution.py:322
  139.1 4.0 %all-gather = f32[128,128]{1,0:T(8,128)S(1)} all-gather(f32[64,128]{1,0:T(8,128)S(1)} %get-tuple-element.31), channel_id=2, replica_groups={{0,8},{16,24},{32,40},{48,56},{64,72},{80,88},{96,104},{112,120},{128,1..., dimensions={0}, use_global_device_ids=true | all-gather | bytes 98304 | tf_op jit(solution)/shard_map/all_gather | solution.py:328
  143.2 0.6 total_kernel.1
  143.7 18.7 %all_to_all.35.parts = f32[32,1,128]{2,1,0:T(1,128)S(1)} all-to-all(f32[32,1,128]{2,1,0:T(1,128)S(1)} %total_kernel.1), channel_id=1, replica_groups={{0,16,32,48,64,80,96,112,128,144,160,176,192,208,224,240,256,272,288,30..., dimensions={0} | all-to-all | bytes 32768 | tf_op jit(solution)/shard_map/all_to_all | solution.py:330
  162.4 1.1 last_kernel.1
  (19 shorter events, 0.1 us)
Async XLA Ops:
  0.6 49.9 %copy-start.8 = (s32[1,1,256]{2,1,0:T(1,128)S(1)}, s32[1,1,256]{2,1,0:T(1,128)}, u32[]{:S(2)}) copy-start(s32[1,1,256]{2,1,0:T(1,128)} %param.14) | copy-start | bytes 3076
  0.6 49.9 %copy-start.7 = (s32[1,1,256]{2,1,0:T(1,128)S(1)}, s32[1,1,256]{2,1,0:T(1,128)}, u32[]{:S(2)}) copy-start(s32[1,1,256]{2,1,0:T(1,128)} %param.13) | copy-start | bytes 3076
  0.7 49.9 %copy-start.6 = (f32[8192]{0:T(1024)S(1)}, f32[8192]{0:T(1024)}, u32[]{:S(2)}) copy-start(f32[8192]{0:T(1024)} %param.10) | copy-start | bytes 98308
  30.1 16.9 %collective-permute-start.1 = (bf16[16,64,128]{2,1,0:T(8,128)(2,1)S(1)}, bf16[16,64,128]{2,1,0:T(8,128)(2,1)S(1)}, u32[]{:S(2)}, u32[]{:S(2)}) collective-permute-start(bf16[16,64,128]{2,1,0:T(8,128)(2,1)S(1)} %all_to_all.30.own), channel_id=1, source_target_pairs={{0,16},{8,24},{16,0},{24,8},{32,48},{40,56},{48,32},{56,40},{64,80... | collective-permute-start | bytes 786440 | tf_op jit(solution)/shard_map/ppermute | solution.py:286
  33.2 1.6 copy-start.2
  36.7 2.0 %copy-start = (bf16[128,128,128]{2,1,0:T(8,128)(2,1)}, bf16[128,128,128]{2,1,0:T(8,128)(2,1)S(1)}, u32[]{:S(2)}) copy-start(bf16[128,128,128]{2,1,0:T(8,128)(2,1)S(1)} %get-tuple-element.17.rows) | copy-start | bytes 12582916
  38.7 11.0 %collective-permute-start = (bf16[16,64,128]{2,1,0:T(8,128)(2,1)S(1)}, bf16[16,64,128]{2,1,0:T(8,128)(2,1)S(1)}, u32[]{:S(2)}, u32[]{:S(2)}) collective-permute-start(bf16[16,64,128]{2,1,0:T(8,128)(2,1)S(1)} %all_to_all.30.own), channel_id=1, source_target_pairs={{0,8},{8,0},{16,24},{24,16},{32,40},{40,32},{48,56},{56,48},{64,72... | collective-permute-start | bytes 786440 | tf_op jit(solution)/shard_map/ppermute | solution.py:287
  47.1 3.4 %collective-permute-start.2 = (bf16[16,64,128]{2,1,0:T(8,128)(2,1)S(1)}, bf16[16,64,128]{2,1,0:T(8,128)(2,1)S(1)}, u32[]{:S(2)}, u32[]{:S(2)}) collective-permute-start(bf16[16,64,128]{2,1,0:T(8,128)(2,1)S(1)} %collective-permute-done.1.other), channel_id=1, source_target_pairs={{0,8},{8,0},{16,24},{24,16},{32,40},{40,32},{48,56},{56,48},{64,72... | collective-permute-start | bytes 786440 | tf_op jit(solution)/shard_map/ppermute | solution.py:295
  50.5 24.7 %copy-start.1 = (bf16[128,128,128]{2,1,0:T(8,128)(2,1)S(1)}, bf16[128,128,128]{2,1,0:T(8,128)(2,1)}, u32[]{:S(2)}) copy-start(bf16[128,128,128]{2,1,0:T(8,128)(2,1)} %copy-done) | copy-start | bytes 12582916
  50.5 24.7 %copy-start.3 = (f32[16384]{0:T(1024)S(1)}, f32[16384]{0:T(1024)}, u32[]{:S(2)}) copy-start(f32[16384]{0:T(1024)} %param.11) | copy-start | bytes 196612
  75.2 40.2 %copy-start.4 = (f32[8192]{0:T(1024)S(1)}, f32[8192]{0:T(1024)}, u32[]{:S(2)}) copy-start(f32[8192]{0:T(1024)} %param.12) | copy-start | bytes 98308
  134.5 27.9 %copy-start.5 = (bf16[128,64]{0,1:T(8,128)(2,1)S(1)}, bf16[128,64]{0,1:T(8,128)(2,1)}, u32[]{:S(2)}) copy-start(bf16[128,64]{0,1:T(8,128)(2,1)} %param.9) | copy-start | bytes 49156

commit v4 on v3

v4 whole, which is shorter than its diff:
```python
import functools

import jax
import jax.numpy as jnp
from jax import lax
from jax.experimental import pallas as pl
from jax.experimental.pallas import tpu as pltpu
from jax.sharding import PartitionSpec as P

DIM = 64
BLK = 128
EPS = 0.1
SCALE = 2.0 / (DIM * EPS)
LOG2E = 1.4426950408889634
KAPPA = SCALE * LOG2E
LOWEST = -1e30
OWNER = 20
VMEM_LIMIT = 16 * 1024 * 1024
STEP_BITS = 6
UNROLL = 1 << STEP_BITS
WAYS = 4
VMEM = pltpu.VMEM
SMEM = pltpu.SMEM
bf16 = jnp.bfloat16
f32 = jnp.float32


def block_of(n):
    return pl.ds(pl.multiple_of(n * BLK, BLK), BLK)


def as_rows(block):
    return jnp.concatenate([block, jnp.zeros((BLK - DIM, BLK), bf16)], axis=0).T


def norm_row(block):
    x = block.astype(f32)
    return jnp.sum(x * x, axis=0, keepdims=True)


def spread(potential, columns_ref, extra_ref):
    blocks = potential.shape[0]
    beta = potential * (1.0 / SCALE)
    hi = beta.astype(bf16).astype(f32)
    rest = beta - hi
    mid = rest.astype(bf16).astype(f32)
    for s, part in enumerate((hi, mid, rest - mid, jnp.zeros_like(hi))):
        columns_ref[pl.ds(s, blocks, stride=4), :] = part
    for g in range(blocks // 16):
        half = columns_ref[g * 64 : g * 64 + 64, :]
        extra_ref[g] = jnp.concatenate([jnp.zeros_like(half), half], axis=0).T.astype(bf16)


def pair_tile(x_ref, extra_ref, hot_ref, x_place, x_id, other_block):
    left = x_ref[x_place] + extra_ref[x_id >> 4]
    right = jnp.concatenate([other_block, hot_ref[x_id & 15]], axis=0)
    return jnp.dot(left, right, preferred_element_type=f32).reshape(16, 8, BLK)


def over_pairs(info, work):
    def group(n, carry):
        row, first = 1 + (n >> (7 - STEP_BITS)), (n << STEP_BITS) & 127
        work([info[row, first + q] for q in range(UNROLL)])
        return carry

    lax.fori_loop(0, info[0, 1], group, 0)


def owner_rows(code):
    return pl.ds(pl.multiple_of(code >> OWNER, 8), 8)


def strided(accs, g):
    return [acc[pl.ds(g * 64 + s, 8, stride=8), :] for acc in accs for s in range(8)]


def stable_lse(info, tile, tops, sums, owners):
    for top, total in zip(tops, sums):
        top[...] = jnp.full(top.shape, LOWEST, f32)
        total[...] = jnp.zeros(total.shape, f32)

    def work(slots):
        stats = []
        for s in slots:
            z = tile(s)
            most = jnp.max(z, axis=0)
            stats.append((most, jnp.sum(jnp.exp2((z - most[None]) * KAPPA), axis=0)))
        for q, (s, (most, part)) in enumerate(zip(slots, stats)):
            rows, top, total = owner_rows(s), tops[q % WAYS], sums[q % WAYS]
            old = top[rows, :]
            new = jnp.maximum(old, most)
            total[rows, :] = total[rows, :] * jnp.exp2((old - new) * KAPPA) + part * jnp.exp2((most - new) * KAPPA)
            top[rows, :] = new

    over_pairs(info, work)
    out = []
    for g in range(owners // 8):
        rows = strided(tops, g)
        most = functools.reduce(jnp.maximum, rows)
        parts = [p * jnp.exp2((r - most) * KAPPA) for r, p in zip(rows, strided(sums, g))]
        total = functools.reduce(jnp.add, parts)
        out.append(jnp.where(total > 0.0, most * SCALE + jnp.log(jnp.maximum(total, 1e-30)), LOWEST))
    return jnp.concatenate(out, axis=0)


def plain_sum(info, tile, total, owners, offset):
    total[...] = jnp.zeros(total.shape, f32)

    def work(slots):
        parts = []
        for s in slots:
            parts.append(jnp.sum(jnp.exp2(tile(s) * KAPPA + offset[owner_rows(s), :][None]), axis=0))
        for s, part in zip(slots, parts):
            rows = owner_rows(s)
            total[rows, :] = total[rows, :] + part

    over_pairs(info, work)
    return jnp.concatenate([functools.reduce(jnp.add, strided([total], g)) for g in range(owners // 8)], axis=0)


def repeat_rows(values, offset):
    owners = values.shape[0]
    for k in range(8):
        offset[pl.ds(k, owners, stride=8), :] = values
    offset[pl.ds(owners * 8, 8), :] = jnp.zeros((8, BLK), f32)


def by_source(targets, sources, extra, hot):
    def tile(code):
        at = pl.multiple_of(code & 0x3F80, BLK)
        return pair_tile(targets, extra, hot, (code >> 14) & 63, code & 63, sources[:, pl.ds(at, BLK)])

    return tile


def by_target(sources, targets, extra, hot):
    def tile(code):
        s = code & 127
        return pair_tile(sources, extra, hot, s, s, targets[(code >> 14) & 63])

    return tile


def prepare_kernel(sources, pair_src, pair_tgt, pair_count, rows, norms, hot, by_src, by_tgt):
    me = lax.axis_index("src")
    lane = lax.broadcasted_iota(jnp.int32, (1, BLK), 1)
    count = jnp.broadcast_to(pair_count[...], (1, BLK))
    steps = (count + (UNROLL - 1)) >> STEP_BITS
    for k, value in enumerate((me, me & 1, me & 3, steps, count)):
        head = value if k == 0 else jnp.where(lane == 4 - k, value, head)
    by_src[0:1, :] = jnp.broadcast_to(head, (1, BLK))
    by_tgt[0:1, :] = jnp.broadcast_to(head, (1, BLK))
    for half in range(2):
        used = lane + half * BLK < count
        part = slice(half * BLK, (half + 1) * BLK)
        s, t = jnp.where(used, pair_src[:, part], 0), jnp.where(used, pair_tgt[:, part], 0)
        place = (((t ^ me) & 3) << 4) + (t >> 2)
        by_src[half + 1 : half + 2, :] = t + (s << 7) + (place << 14) + (jnp.where(used, s, 128) << (OWNER + 3))
        by_tgt[half + 1 : half + 2, :] = s + (place << 14) + (jnp.where(used, t, 64) << (OWNER + 3))
    line = lax.broadcasted_iota(jnp.int32, (DIM, BLK), 0)
    for r in range(16):
        hot[r] = jnp.where((line >= 4 * r) & (line < 4 * r + 3), 1.0, 0.0).astype(bf16)
    for b in range(128):
        block = sources[:, b * BLK : b * BLK + BLK]
        rows[b] = as_rows(block)
        norms[b : b + 1, :] = norm_row(block)


def merge_lse(parts_ref):
    top = jnp.max(parts_ref[...], axis=0)
    total = jnp.sum(jnp.exp(parts_ref[...] - top[None]), axis=0)
    return top + jnp.log(total)


def first_kernel(
    info, sources, own, core, other, both, start, hot, out, rows, targets, norms, columns, extra, *accs
):
    mine = info[0, 2]
    for d, part in enumerate((own, core, other, both)):
        for z in range(16):
            block = part[z]
            targets[d * 16 + z] = block
            rows[d * 16 + z] = as_rows(block)
            norms[pl.ds(z * 4 + (d ^ mine), 1), :] = norm_row(block)
    spread(start[...] * (1.0 / EPS) - norms[...] * (SCALE / 2), columns, extra)
    tile = by_source(rows, sources, extra, hot)
    lse = stable_lse(info, tile, accs[:WAYS], accs[WAYS:], 128)
    for k in range(8):
        out[k] = lse


def second_kernel(info, rows, targets, parts, mass, hot, out, potential, columns, extra, *accs):
    new = mass[...] - merge_lse(parts)
    potential[...] = new
    spread(new, columns, extra)
    tile = by_target(rows, targets, extra, hot)
    lse = stable_lse(info, tile, accs[:WAYS], accs[WAYS:], 64)
    for k in range(4):
        out[k] = lse[16 * k : 16 * k + 16]


def group_kernel(parts, out):
    lse = merge_lse(parts)
    for k in range(16):
        out[k] = lse


def ring_kernel(parts, out):
    out[...] = merge_lse(parts)


def third_kernel(
    info, sources, rows, lse, mass, reference, hot, mine, out, potential, base, columns, extra, offset, acc
):
    me = info[0, 4]
    new = mass[...] - lse[...]
    potential[...] = new
    base[...] = potential[pl.ds(me, 1), :] + mass[pl.ds(me, 1), :] + norm_row(mine[...]) * (SCALE / 2)
    spread(new, columns, extra)
    repeat_rows(reference[...] * LOG2E, offset)
    tile = by_source(rows, sources, extra, hot)
    total = plain_sum(info, tile, acc, 128, offset)
    for k in range(8):
        out[k] = total


def fourth_kernel(
    info, rows, targets, parts, mass, former, reference, norms, hot,
    out, final, odd, columns, extra, offset, acc,
):
    new = former[...] + mass[...] - jnp.log(jnp.sum(parts[...], axis=0))
    spread(new, columns, extra)
    final[...] = EPS * (new + norms[...] * (SCALE / 2))
    odd[...] = jnp.full(odd.shape, info[0, 3], jnp.int32)
    repeat_rows(reference[...] * LOG2E, offset)
    tile = by_target(rows, targets, extra, hot)
    out[...] = plain_sum(info, tile, acc, 64, offset)


def total_kernel(parts, odd, out):
    first, second = [parts[0, pl.ds(k, 32, stride=2), :] + parts[1, pl.ds(k, 32, stride=2), :] for k in range(2)]
    out[...] = jnp.where(odd[...] == 0, first, second)[:, None, :]


def last_kernel(parts, base, out):
    out[...] = EPS * (base[...] - jnp.log(jnp.sum(parts[...], axis=0)))


def call(kernel, kinds, outs, scratch=()):
    specs = [pl.BlockSpec(memory_space=SMEM if kind == "s" else VMEM) for kind in kinds]
    out_specs = [pl.BlockSpec(memory_space=VMEM) for _ in outs]
    shapes = [jax.ShapeDtypeStruct(shape, dtype) for shape, dtype in outs]
    single = len(outs) == 1
    return pl.pallas_call(
        kernel,
        in_specs=specs,
        out_specs=out_specs[0] if single else out_specs,
        out_shape=shapes[0] if single else shapes,
        scratch_shapes=list(scratch),
        compiler_params=pltpu.CompilerParams(vmem_limit_bytes=VMEM_LIMIT),
        name=kernel.__name__,
    )


def columns_of(blocks):
    return [VMEM((blocks * 4, BLK), f32), VMEM((blocks // 16, BLK, BLK), bf16)]


def accumulators(owners, number):
    return [VMEM(((owners + 1) * 8, BLK), f32) for _ in range(number)]


def on_device(source_cells, target_cells, start, source_logmass, target_logmass, pair_src, pair_tgt, pair_count):
    ring = [[z * 4 + r for z in range(16)] for r in range(4)]
    chips = [[z * 4 + r for r in range(4)] for z in range(16)]
    cores = [[i, i + 1] for i in range(0, 64, 2)]
    halves = [[2 * i + c for i in range(32)] for c in range(2)]
    to_core = [(i, i ^ 1) for i in range(64)]
    to_chip = [(i, i ^ 2) for i in range(64)]

    source_mass = source_logmass.reshape(-1, BLK)
    target_mass = target_logmass.reshape(-1, BLK)

    mine = target_cells.T
    own = lax.all_to_all(jnp.broadcast_to(mine[None], (16, DIM, BLK)), "src", 0, 0, axis_index_groups=ring)
    other = lax.ppermute(own, "src", to_chip)
    core = lax.ppermute(own, "src", to_core)
    sources = source_cells.T
    table = ((8, BLK), jnp.int32)
    rows, norms, hot, info_s, info_t = call(
        prepare_kernel,
        "vvvv",
        [((128, BLK, BLK), bf16), ((128, BLK), f32), ((16, DIM, BLK), bf16), table, table],
    )(sources, pair_src.reshape(1, -1), pair_tgt.reshape(1, -1), pair_count)
    other, hot = lax.optimization_barrier((other, hot))
    both = lax.ppermute(other, "src", to_core)

    parts, target_rows, targets = call(
        first_kernel,
        "svvvvvvv",
        [((8, 128, BLK), f32), ((64, BLK, BLK), bf16), ((64, DIM, BLK), bf16)],
        [VMEM((64, BLK), f32)] + columns_of(64) + accumulators(128, 2 * WAYS),
    )(info_s, sources, own, core, other, both, start.reshape(-1, BLK), hot)
    parts = lax.all_to_all(parts, "tgt", 0, 0)
    lse, first_u = call(
        second_kernel,
        "svvvvv",
        [((4, 16, BLK), f32), ((128, BLK), f32)],
        columns_of(128) + accumulators(64, 2 * WAYS),
    )(info_t, rows, targets, parts, source_mass, hot)
    lse = lax.all_to_all(lse, "src", 0, 0, axis_index_groups=chips)
    lse = call(group_kernel, "v", [((16, 16, BLK), f32)])(lse)
    lse = lax.all_to_all(lse, "src", 0, 0, axis_index_groups=ring)
    lse = call(ring_kernel, "v", [((16, BLK), f32)])(lse)
    lse = lax.all_gather(lse, "src", axis=0, axis_index_groups=chips, tiled=True)
    parts, first_v, base = call(
        third_kernel,
        "svvvvvvv",
        [((8, 128, BLK), f32), ((64, BLK), f32), ((1, BLK), f32)],
        columns_of(64) + accumulators(128, 2),
    )(info_s, sources, target_rows, lse, target_mass, first_u, hot, mine)
    parts = lax.all_to_all(parts, "tgt", 0, 0)
    sums, last_u, odd = call(
        fourth_kernel,
        "svvvvvvvv",
        [((64, BLK), f32), ((128, BLK), f32), ((32, BLK), jnp.int32)],
        columns_of(128) + accumulators(64, 2),
    )(info_t, rows, targets, parts, source_mass, first_u, first_v, norms, hot)
    sums = lax.all_gather(sums, "src", axis=0, axis_index_groups=cores)
    sums = call(total_kernel, "vv", [((32, 1, BLK), f32)])(sums, odd)
    sums = lax.all_to_all(sums, "src", 0, 0, axis_index_groups=halves)
    last_v = call(last_kernel, "vv", [((1, BLK), f32)])(sums, base)
    return last_u.reshape(-1), last_v.reshape(-1)


def solution(mesh):
    in_specs = (
        P("src", None),
        P(("tgt", "src"), None),
        P("tgt"),
        P("src"),
        P("tgt"),
        P("src", "tgt", None),
        P("src", "tgt", None),
        P("src", "tgt"),
    )
    out_specs = (P("src"), P(("tgt", "src")))
    return jax.shard_map(
        on_device, mesh=mesh, in_specs=in_specs, out_specs=out_specs, check_vma=False
    )
```

time: 164 us -> 158 us (0.963)
  blocking collectives: 122 us -> 110 us
  Pallas kernels: 21.3 us -> 27.1 us
    all_to_all x2, blocking collectives: 35.2 us -> 27.1 us  [on_device(): parts = lax.all_to_all(parts, 'tgt', 0, 0)]
    pallas_call x7, Pallas kernels: 21.3 us -> 27.1 us  [the longest x1 8 us: on_device(): call(first_kernel, 'svvvvvvv', [((8, 128, BLK), f32), ((64, BLK, BLK), bf...]
    all_to_all x1, blocking collectives: 18.7 us -> 16.6 us  [on_device(): sums = lax.all_to_all(sums, 'src', 0, 0, axis_index_groups=halves)]
    unnamed x18 -> x16, local copies, waits for them, and re-layouts: 3.58 us -> 2.96 us
where the time goes in v4:
time: 158 us; the launch traced here: 157 us
  blocking collectives  110 us (70%)
  Pallas kernels  27.1 us (17%)
  starting transfers between devices  13.4 us (8%)
  local copies, waits for them, and re-layouts  3.73 us (2%)
    all_to_all x1, blocking collectives, on_device(): lax.all_to_all(jnp.broadcast_to(mine[None], (16, DIM, BLK)), 'src', 0, 0,...  28.7 us
    all_to_all x2, blocking collectives, on_device(): parts = lax.all_to_all(parts, 'tgt', 0, 0)  27.1 us
    all_to_all x1, blocking collectives, on_device(): lse = lax.all_to_all(lse, 'src', 0, 0, axis_index_groups=ring)  18.5 us
    all_to_all x1, blocking collectives, on_device(): sums = lax.all_to_all(sums, 'src', 0, 0, axis_index_groups=halves)  16.6 us
    all_gather x1, blocking collectives, on_device(): lax.all_gather(lse, 'src', axis=0, axis_index_groups=chips, tiled=True)  8.76 us
    ppermute x1, starting transfers between devices, on_device(): core = lax.ppermute(own, 'src', to_core)  8.37 us
    pallas_call x1, Pallas kernels, on_device(): call(first_kernel, 'svvvvvvv', [((8, 128, BLK), f32), ((64, BLK, BLK), bf...  8 us
    all_to_all x1, blocking collectives, on_device(): lse = lax.all_to_all(lse, 'src', 0, 0, axis_index_groups=chips)  7.58 us
  transfers between devices with their start and end apart: 3, of which 1 were waited for; matrix products, arithmetic and copies ran while one was open for 0% of the time, Pallas kernels for 1%

profile of v4, /device:TPU:1, one launch (start us, length us, event | category | flops | bytes accessed | tf_op | source)
XLA Modules:
  0.0 157.3 jit_solution(1452770304693931166)
XLA Ops:
  0.6 0.8 broadcast_in_dim.2
  1.4 28.7 %all_to_all.30.own = bf16[16,64,128]{2,1,0:T(8,128)(2,1)S(1)} all-to-all(bf16[16,64,128]{2,1,0:T(8,128)(2,1)S(1)} %broadcast_in_dim.2), channel_id=1, replica_groups={{0,32,64,96,128,160,192,224,256,288,320,352,384,416,448,480},{8,40,72,1..., dimensions={0} | all-to-all | bytes 524288 | tf_op jit(solution)/shard_map/all_to_all | solution.py:285
  30.1 3.1 %collective-permute-start.1 = (bf16[16,64,128]{2,1,0:T(8,128)(2,1)S(1)}, bf16[16,64,128]{2,1,0:T(8,128)(2,1)S(1)}, u32[]{:S(2)}, u32[]{:S(2)}) collective-permute-start(bf16[16,64,128]{2,1,0:T(8,128)(2,1)S(1)} %all_to_all.30.own), channel_id=1, source_target_pairs={{0,16},{8,24},{16,0},{24,8},{32,48},{40,56},{48,32},{56,40},{64,80... | collective-permute-start | bytes 786440 | tf_op jit(solution)/shard_map/ppermute | solution.py:286
  33.9 0.0 copy-start
  33.9 1.6 %copy-done = bf16[16384,64]{0,1:T(8,128)(2,1)S(1)} copy-done((bf16[16384,64]{0,1:T(8,128)(2,1)S(1)}, bf16[16384,64]{0,1:T(8,128)(2,1)}, u32[]{:S(2)}) %copy-start) | copy-done | bytes 2097176
  35.5 0.7 copy-done.6
  36.1 0.7 copy-done.7
  36.8 1.2 prepare_kernel.1
  38.0 8.4 %collective-permute-start = (bf16[16,64,128]{2,1,0:T(8,128)(2,1)S(1)}, bf16[16,64,128]{2,1,0:T(8,128)(2,1)S(1)}, u32[]{:S(2)}, u32[]{:S(2)}) collective-permute-start(bf16[16,64,128]{2,1,0:T(8,128)(2,1)S(1)} %all_to_all.30.own), channel_id=1, source_target_pairs={{0,8},{8,0},{16,24},{24,16},{32,40},{40,32},{48,56},{56,48},{64,72... | collective-permute-start | bytes 786440 | tf_op jit(solution)/shard_map/ppermute | solution.py:287
  46.4 1.9 %collective-permute-start.2 = (bf16[16,64,128]{2,1,0:T(8,128)(2,1)S(1)}, bf16[16,64,128]{2,1,0:T(8,128)(2,1)S(1)}, u32[]{:S(2)}, u32[]{:S(2)}) collective-permute-start(bf16[16,64,128]{2,1,0:T(8,128)(2,1)S(1)} %collective-permute-done.1.other), channel_id=1, source_target_pairs={{0,8},{8,0},{16,24},{24,16},{32,40},{40,32},{48,56},{56,48},{64,72... | collective-permute-start | bytes 786440 | tf_op jit(solution)/shard_map/ppermute | solution.py:296
  48.3 0.0 collective-permute-done.core
  48.3 1.5 collective-permute-done.2.both
  49.8 8.0 %first_kernel.1 = (f32[8,128,128]{2,1,0:T(8,128)S(1)}, bf16[64,128,128]{2,1,0:T(8,128)(2,1)S(1)}, bf16[64,64,128]{2,1,0:T(8,128)(2,1)S(1)}) custom-call(s32[8,128]{1,0:T(8,128)S(1)} %get-tuple-element.22.info, bf16[64,16384]{1,0:T(8,128)(2,1)S(1)} %bitcast.11, bf16[16,64,128]{2,1,0:T(8,128)(2,1)S(1)} %all_to_all.30.own, ...), custom_call_target="tpu_custom_call" | custom-call | tf_op jit(solution)/shard_map/first_kernel/pallas_call | solution.py:298
  57.8 13.7 %all_to_all.31.parts = f32[8,128,128]{2,1,0:T(8,128)S(1)} all-to-all(f32[8,128,128]{2,1,0:T(8,128)S(1)} %get-tuple-element.28), channel_id=1, replica_groups=mesh['src'=64,'tgt'=8] {'tgt'}, dimensions={0} | all-to-all | bytes 1048576 | tf_op jit(solution)/shard_map/all_to_all | solution.py:304
  71.6 6.8 %second_kernel.1 = (f32[4,16,128]{2,1,0:T(8,128)S(1)}, f32[128,128]{1,0:T(8,128)S(1)}) custom-call(s32[8,128]{1,0:T(8,128)S(1)} %get-tuple-element.20.info, bf16[128,128,128]{2,1,0:T(8,128)(2,1)S(1)} %get-tuple-element.21.rows, bf16[64,64,128]{2,1,0:T(8,128)(2,1)S(1)} %get-tuple-element.26.targets, f32[8,128,128]{2,1,0:T(8,128)S(1)} %all_to_all.31.parts, ...), custom_call_target="tpu_custom_call" | custom-call | tf_op jit(solution)/shard_map/second_kernel/pallas_call | solution.py:305
  78.4 7.6 %all_to_all.32.parts = f32[4,16,128]{2,1,0:T(8,128)S(1)} all-to-all(f32[4,16,128]{2,1,0:T(8,128)S(1)} %get-tuple-element.29), channel_id=1, replica_groups={{0,8,16,24},{32,40,48,56},{64,72,80,88},{96,104,112,120},{128,136,144,1..., dimensions={0} | all-to-all | bytes 65536 | tf_op jit(solution)/shard_map/all_to_all | solution.py:311
  86.0 18.5 %all_to_all.33.parts = f32[16,16,128]{2,1,0:T(8,128)S(1)} all-to-all(f32[16,16,128]{2,1,0:T(8,128)S(1)} %group_kernel.1), channel_id=1, replica_groups={{0,32,64,96,128,160,192,224,256,288,320,352,384,416,448,480},{8,40,72,1..., dimensions={0} | all-to-all | bytes 262144 | tf_op jit(solution)/shard_map/all_to_all | solution.py:313
  104.6 8.8 %all_gather.9.lse = f32[64,128]{1,0:T(8,128)S(1)} all-gather(f32[16,128]{1,0:T(8,128)S(1)} %ring_kernel.1), channel_id=1, replica_groups={{0,8,16,24},{32,40,48,56},{64,72,80,88},{96,104,112,120},{128,136,144,1..., dimensions={0}, use_global_device_ids=true | all-gather | bytes 40960 | tf_op jit(solution)/shard_map/all_gather | solution.py:315
  113.4 5.1 %third_kernel.1 = (f32[8,128,128]{2,1,0:T(8,128)S(1)}, f32[64,128]{1,0:T(8,128)S(1)}, f32[1,128]{1,0:T(1,128)S(1)}) custom-call(s32[8,128]{1,0:T(8,128)S(1)} %get-tuple-element.22.info, bf16[64,16384]{1,0:T(8,128)(2,1)S(1)} %bitcast.12, bf16[64,128,128]{2,1,0:T(8,128)(2,1)S(1)} %get-tuple-element.27.rows, f32[64,128]{1,0:T(8,128)S(1)} %all_gather.9.lse, ...), custom_call_target="tpu_custom_call" | custom-call | tf_op jit(solution)/shard_map/third_kernel/pallas_call | solution.py:316
  118.5 13.4 %all_to_all.34.parts = f32[8,128,128]{2,1,0:T(8,128)S(1)} all-to-all(f32[8,128,128]{2,1,0:T(8,128)S(1)} %get-tuple-element.31), channel_id=1, replica_groups=mesh['src'=64,'tgt'=8] {'tgt'}, dimensions={0} | all-to-all | bytes 1048576 | tf_op jit(solution)/shard_map/all_to_all | solution.py:322
  131.9 5.4 %fourth_kernel.1 = (f32[64,128]{1,0:T(8,128)S(1)}, f32[128,128]{1,0:T(8,128)}, s32[32,128]{1,0:T(8,128)S(1)}) custom-call(s32[8,128]{1,0:T(8,128)S(1)} %get-tuple-element.20.info, bf16[128,128,128]{2,1,0:T(8,128)(2,1)S(1)} %get-tuple-element.21.rows, bf16[64,64,128]{2,1,0:T(8,128)(2,1)S(1)} %get-tuple-element.26.targets, ...), custom_call_target="tpu_custom_call" | custom-call | tf_op jit(solution)/shard_map/fourth_kernel/pallas_call | solution.py:323
  137.2 2.9 %all-gather = f32[128,128]{1,0:T(8,128)S(1)} all-gather(f32[64,128]{1,0:T(8,128)S(1)} %get-tuple-element.35), channel_id=2, replica_groups={{0,8},{16,24},{32,40},{48,56},{64,72},{80,88},{96,104},{112,120},{128,1..., dimensions={0}, use_global_device_ids=true | all-gather | bytes 98304 | tf_op jit(solution)/shard_map/all_gather | solution.py:329
  140.1 16.6 %all_to_all.35.parts = f32[32,1,128]{2,1,0:T(1,128)S(1)} all-to-all(f32[32,1,128]{2,1,0:T(1,128)S(1)} %total_kernel.1), channel_id=1, replica_groups={{0,16,32,48,64,80,96,112,128,144,160,176,192,208,224,240,256,272,288,30..., dimensions={0} | all-to-all | bytes 32768 | tf_op jit(solution)/shard_map/all_to_all | solution.py:331
  156.7 0.6 last_kernel.1
  (16 shorter events, 0.1 us)
Async XLA Ops:
  0.6 49.2 %copy-start.4 = (f32[8192]{0:T(1024)S(1)}, f32[8192]{0:T(1024)}, u32[]{:S(2)}) copy-start(f32[8192]{0:T(1024)} %param.10) | copy-start | bytes 98308
  30.1 16.3 %collective-permute-start.1 = (bf16[16,64,128]{2,1,0:T(8,128)(2,1)S(1)}, bf16[16,64,128]{2,1,0:T(8,128)(2,1)S(1)}, u32[]{:S(2)}, u32[]{:S(2)}) collective-permute-start(bf16[16,64,128]{2,1,0:T(8,128)(2,1)S(1)} %all_to_all.30.own), channel_id=1, source_target_pairs={{0,16},{8,24},{16,0},{24,8},{32,48},{40,56},{48,32},{56,40},{64,80... | collective-permute-start | bytes 786440 | tf_op jit(solution)/shard_map/ppermute | solution.py:286
  33.9 1.6 %copy-start = (bf16[16384,64]{0,1:T(8,128)(2,1)S(1)}, bf16[16384,64]{0,1:T(8,128)(2,1)}, u32[]{:S(2)}) copy-start(bf16[16384,64]{0,1:T(8,128)(2,1)} %param.8) | copy-start | bytes 6291460
  35.5 0.7 copy-start.6
  36.1 0.7 copy-start.7
  38.0 10.3 %collective-permute-start = (bf16[16,64,128]{2,1,0:T(8,128)(2,1)S(1)}, bf16[16,64,128]{2,1,0:T(8,128)(2,1)S(1)}, u32[]{:S(2)}, u32[]{:S(2)}) collective-permute-start(bf16[16,64,128]{2,1,0:T(8,128)(2,1)S(1)} %all_to_all.30.own), channel_id=1, source_target_pairs={{0,8},{8,0},{16,24},{24,16},{32,40},{40,32},{48,56},{56,48},{64,72... | collective-permute-start | bytes 786440 | tf_op jit(solution)/shard_map/ppermute | solution.py:287
  46.4 3.4 %collective-permute-start.2 = (bf16[16,64,128]{2,1,0:T(8,128)(2,1)S(1)}, bf16[16,64,128]{2,1,0:T(8,128)(2,1)S(1)}, u32[]{:S(2)}, u32[]{:S(2)}) collective-permute-start(bf16[16,64,128]{2,1,0:T(8,128)(2,1)S(1)} %collective-permute-done.1.other), channel_id=1, source_target_pairs={{0,8},{8,0},{16,24},{24,16},{32,40},{40,32},{48,56},{56,48},{64,72... | collective-permute-start | bytes 786440 | tf_op jit(solution)/shard_map/ppermute | solution.py:296
  49.8 21.7 %copy-start.2 = (f32[16384]{0:T(1024)S(1)}, f32[16384]{0:T(1024)}, u32[]{:S(2)}) copy-start(f32[16384]{0:T(1024)} %param.11) | copy-start | bytes 196612
  71.6 41.8 %copy-start.1 = (bf16[16384,64]{0,1:T(8,128)(2,1)S(1)}, bf16[16384,64]{0,1:T(8,128)(2,1)}, u32[]{:S(2)}) copy-start(bf16[16384,64]{0,1:T(8,128)(2,1)} %param.8) | copy-start | bytes 6291460
  71.6 41.8 %copy-start.3 = (bf16[128,64]{0,1:T(8,128)(2,1)S(1)}, bf16[128,64]{0,1:T(8,128)(2,1)}, u32[]{:S(2)}) copy-start(bf16[128,64]{0,1:T(8,128)(2,1)} %param.9) | copy-start | bytes 49156
  71.6 41.8 %copy-start.5 = (f32[8192]{0:T(1024)S(1)}, f32[8192]{0:T(1024)}, u32[]{:S(2)}) copy-start(f32[8192]{0:T(1024)} %param.12) | copy-start | bytes 98308

commit v5 on v4

--- a/solution.py
+++ b/solution.py
@@ -12,13 +12,15 @@
 EPS = 0.1
 SCALE = 2.0 / (DIM * EPS)
 LOG2E = 1.4426950408889634
+LN2 = 0.6931471805599453
 KAPPA = SCALE * LOG2E
 LOWEST = -1e30
+LEAST, MOST = 2.0**-80, 2.0**120
+LIFT = 100.0
 OWNER = 20
 VMEM_LIMIT = 16 * 1024 * 1024
 STEP_BITS = 6
 UNROLL = 1 << STEP_BITS
-WAYS = 4
 VMEM = pltpu.VMEM
 SMEM = pltpu.SMEM
 bf16 = jnp.bfloat16
@@ -57,27 +59,26 @@
     return jnp.dot(left, right, preferred_element_type=f32).reshape(16, 8, BLK)
 
 
-def over_pairs(info, work):
+def over_pairs(info, work, bits=STEP_BITS):
     def group(n, carry):
-        row, first = 1 + (n >> (7 - STEP_BITS)), (n << STEP_BITS) & 127
-        work([info[row, first + q] for q in range(UNROLL)])
+        row, first = 1 + (n >> (7 - bits)), (n << bits) & 127
+        work([info[row, first + q] for q in range(1 << bits)])
         return carry
 
-    lax.fori_loop(0, info[0, 1], group, 0)
+    lax.fori_loop(0, (info[0, 0] + ((1 << bits) - 1)) >> bits, group, 0)
 
 
 def owner_rows(code):
     return pl.ds(pl.multiple_of(code >> OWNER, 8), 8)
 
 
-def strided(accs, g):
-    return [acc[pl.ds(g * 64 + s, 8, stride=8), :] for acc in accs for s in range(8)]
-
-
-def stable_lse(info, tile, tops, sums, owners):
-    for top, total in zip(tops, sums):
-        top[...] = jnp.full(top.shape, LOWEST, f32)
-        total[...] = jnp.zeros(total.shape, f32)
+def strided(acc, g):
+    return [acc[pl.ds(g * 64 + s, 8, stride=8), :] for s in range(8)]
+
+
+def stable_lse(info, tile, top, total, owners):
+    top[...] = jnp.full(top.shape, LOWEST, f32)
+    total[...] = jnp.zeros(total.shape, f32)
 
     def work(slots):
         stats = []
@@ -85,26 +86,28 @@
             z = tile(s)
             most = jnp.max(z, axis=0)
             stats.append((most, jnp.sum(jnp.exp2((z - most[None]) * KAPPA), axis=0)))
-        for q, (s, (most, part)) in enumerate(zip(slots, stats)):
-            rows, top, total = owner_rows(s), tops[q % WAYS], sums[q % WAYS]
+        for s, (most, part) in zip(slots, stats):
+            rows = owner_rows(s)
             old = top[rows, :]
             new = jnp.maximum(old, most)
             total[rows, :] = total[rows, :] * jnp.exp2((old - new) * KAPPA) + part * jnp.exp2((most - new) * KAPPA)
             top[rows, :] = new
 
-    over_pairs(info, work)
+    over_pairs(info, work, 3)
     out = []
     for g in range(owners // 8):
-        rows = strided(tops, g)
+        rows = strided(top, g)
         most = functools.reduce(jnp.maximum, rows)
-        parts = [p * jnp.exp2((r - most) * KAPPA) for r, p in zip(rows, strided(sums, g))]
-        total = functools.reduce(jnp.add, parts)
-        out.append(jnp.where(total > 0.0, most * SCALE + jnp.log(jnp.maximum(total, 1e-30)), LOWEST))
+        parts = [p * jnp.exp2((r - most) * KAPPA) for r, p in zip(rows, strided(total, g))]
+        whole = functools.reduce(jnp.add, parts)
+        out.append(jnp.where(whole > 0.0, most * SCALE + jnp.log(jnp.maximum(whole, 1e-30)), LOWEST))
     return jnp.concatenate(out, axis=0)
 
 
-def plain_sum(info, tile, total, owners, offset):
+def plain_sum(info, tile, total, owners, offset, seen=None):
     total[...] = jnp.zeros(total.shape, f32)
+    if seen is not None:
+        seen[...] = jnp.zeros(seen.shape, f32)
 
     def work(slots):
         parts = []
@@ -113,9 +116,25 @@
         for s, part in zip(slots, parts):
             rows = owner_rows(s)
             total[rows, :] = total[rows, :] + part
+            if seen is not None:
+                seen[rows, :] = jnp.ones((8, BLK), f32)
 
     over_pairs(info, work)
-    return jnp.concatenate([functools.reduce(jnp.add, strided([total], g)) for g in range(owners // 8)], axis=0)
+    return jnp.concatenate([functools.reduce(jnp.add, strided(total, g)) for g in range(owners // 8)], axis=0)
+
+
+def guarded_lse(info, tile, accs, owners, values, offset, write):
+    total_ref, seen_ref = accs
+    repeat_rows(values, offset)
+    total = plain_sum(info, tile, total_ref, owners, offset, seen_ref)
+    seen = seen_ref[pl.ds(0, owners, stride=8), :] > 0.0
+    fine = (total >= LEAST) & (total <= MOST)
+    write(jnp.where(seen, jnp.log(jnp.where(fine, total, 1.0)) - values * LN2, LOWEST))
+    lost = jnp.max(jnp.where(seen & jnp.logical_not(fine), 1.0, 0.0))
+
+    @pl.when(lost > 0.0)
+    def again():
+        write(stable_lse(info, tile, total_ref, seen_ref, owners))
 
 
 def repeat_rows(values, offset):
@@ -173,7 +192,8 @@
 
 
 def first_kernel(
-    info, sources, own, core, other, both, start, hot, out, rows, targets, norms, columns, extra, *accs
+    info, sources, own, core, other, both, start, source_norms, hot,
+    out, rows, targets, potential, norms, columns, extra, offset, *accs,
 ):
     mine = info[0, 2]
     for d, part in enumerate((own, core, other, both)):
@@ -182,21 +202,29 @@
             targets[d * 16 + z] = block
             rows[d * 16 + z] = as_rows(block)
             norms[pl.ds(z * 4 + (d ^ mine), 1), :] = norm_row(block)
-    spread(start[...] * (1.0 / EPS) - norms[...] * (SCALE / 2), columns, extra)
+    new = start[...] * (1.0 / EPS) - norms[...] * (SCALE / 2)
+    potential[...] = new
+    spread(new, columns, extra)
     tile = by_source(rows, sources, extra, hot)
-    lse = stable_lse(info, tile, accs[:WAYS], accs[WAYS:], 128)
-    for k in range(8):
-        out[k] = lse
-
-
-def second_kernel(info, rows, targets, parts, mass, hot, out, potential, columns, extra, *accs):
+
+    def write(lse):
+        for k in range(8):
+            out[k] = lse
+
+    guarded_lse(info, tile, accs, 128, source_norms[...] * (-LOG2E * SCALE / 2), offset, write)
+
+
+def second_kernel(info, rows, targets, parts, mass, former, hot, out, potential, columns, extra, offset, *accs):
     new = mass[...] - merge_lse(parts)
     potential[...] = new
     spread(new, columns, extra)
     tile = by_target(rows, targets, extra, hot)
-    lse = stable_lse(info, tile, accs[:WAYS], accs[WAYS:], 64)
-    for k in range(4):
-        out[k] = lse[16 * k : 16 * k + 16]
+
+    def write(lse):
+        for k in range(4):
+            out[k] = lse[16 * k : 16 * k + 16]
+
+    guarded_lse(info, tile, accs, 64, former[...] * LOG2E + LIFT, offset, write)
 
 
 def group_kernel(parts, out):
@@ -295,19 +323,19 @@
     other, hot = lax.optimization_barrier((other, hot))
     both = lax.ppermute(other, "src", to_core)
 
-    parts, target_rows, targets = call(
+    parts, target_rows, targets, start_v = call(
         first_kernel,
-        "svvvvvvv",
-        [((8, 128, BLK), f32), ((64, BLK, BLK), bf16), ((64, DIM, BLK), bf16)],
-        [VMEM((64, BLK), f32)] + columns_of(64) + accumulators(128, 2 * WAYS),
-    )(info_s, sources, own, core, other, both, start.reshape(-1, BLK), hot)
+        "svvvvvvvv",
+        [((8, 128, BLK), f32), ((64, BLK, BLK), bf16), ((64, DIM, BLK), bf16), ((64, BLK), f32)],
+        [VMEM((64, BLK), f32)] + columns_of(64) + accumulators(128, 3),
+    )(info_s, sources, own, core, other, both, start.reshape(-1, BLK), norms, hot)
     parts = lax.all_to_all(parts, "tgt", 0, 0)
     lse, first_u = call(
         second_kernel,
-        "svvvvv",
+        "svvvvvv",
         [((4, 16, BLK), f32), ((128, BLK), f32)],
-        columns_of(128) + accumulators(64, 2 * WAYS),
-    )(info_t, rows, targets, parts, source_mass, hot)
+        columns_of(128) + accumulators(64, 3),
+    )(info_t, rows, targets, parts, source_mass, start_v, hot)
     lse = lax.all_to_all(lse, "src", 0, 0, axis_index_groups=chips)
     lse = call(group_kernel, "v", [((16, 16, BLK), f32)])(lse)
     lse = lax.all_to_all(lse, "src", 0, 0, axis_index_groups=ring)

time: 158 us -> 172 us (1.089)
  Pallas kernels: 27.1 us -> 39.8 us
  blocking collectives: 110 us -> 112 us
    pallas_call x2, Pallas kernels: 14.8 us -> 27.5 us  [the longest x1 14.3 us: on_device(): call(first_kernel, 'svvvvvvvv', [((8, 128, BLK), f32), ((64, BLK, BLK), b...]
    all_to_all x2, blocking collectives: 27.1 us -> 29.2 us  [on_device(): parts = lax.all_to_all(parts, 'tgt', 0, 0)]
where the time goes in v5:
time: 172 us
  blocking collectives  112 us (65%)
  Pallas kernels  39.8 us (23%)
  starting transfers between devices  13.4 us (8%)
  local copies, waits for them, and re-layouts  3.73 us (2%)
    all_to_all x2, blocking collectives, on_device(): parts = lax.all_to_all(parts, 'tgt', 0, 0)  29.2 us
    all_to_all x1, blocking collectives, on_device(): lax.all_to_all(jnp.broadcast_to(mine[None], (16, DIM, BLK)), 'src', 0, 0,...  28.7 us
    all_to_all x1, blocking collectives, on_device(): lse = lax.all_to_all(lse, 'src', 0, 0, axis_index_groups=ring)  17.1 us
    all_to_all x1, blocking collectives, on_device(): sums = lax.all_to_all(sums, 'src', 0, 0, axis_index_groups=halves)  15 us
    pallas_call x1, Pallas kernels, on_device(): call(first_kernel, 'svvvvvvvv', [((8, 128, BLK), f32), ((64, BLK, BLK), b...  14.3 us
    pallas_call x1, Pallas kernels, on_device(): call(second_kernel, 'svvvvvv', [((4, 16, BLK), f32), ((128, BLK), f32)],...  13.1 us
    all_to_all x1, blocking collectives, on_device(): lse = lax.all_to_all(lse, 'src', 0, 0, axis_index_groups=chips)  9.27 us
    all_gather x1, blocking collectives, on_device(): lax.all_gather(lse, 'src', axis=0, axis_index_groups=chips, tiled=True)  8.76 us
  transfers between devices with their start and end apart: 3, of which 1 were waited for; matrix products, arithmetic and copies ran while one was open for 0% of the time, Pallas kernels for 1%

profile of v5, /device:TPU:1, one launch (start us, length us, event | category | flops | bytes accessed | tf_op | source)
XLA Modules:
  0.0 171.5 jit_solution(684294173801863385)
XLA Ops:
  0.6 0.8 broadcast_in_dim.2
  1.4 28.7 %all_to_all.30.own = bf16[16,64,128]{2,1,0:T(8,128)(2,1)S(1)} all-to-all(bf16[16,64,128]{2,1,0:T(8,128)(2,1)S(1)} %broadcast_in_dim.2), channel_id=1, replica_groups={{0,32,64,96,128,160,192,224,256,288,320,352,384,416,448,480},{8,40,72,1..., dimensions={0} | all-to-all | bytes 524288 | tf_op jit(solution)/shard_map/all_to_all | solution.py:313
  30.1 3.1 %collective-permute-start.1 = (bf16[16,64,128]{2,1,0:T(8,128)(2,1)S(1)}, bf16[16,64,128]{2,1,0:T(8,128)(2,1)S(1)}, u32[]{:S(2)}, u32[]{:S(2)}) collective-permute-start(bf16[16,64,128]{2,1,0:T(8,128)(2,1)S(1)} %all_to_all.30.own), channel_id=1, source_target_pairs={{0,16},{8,24},{16,0},{24,8},{32,48},{40,56},{48,32},{56,40},{64,80... | collective-permute-start | bytes 786440 | tf_op jit(solution)/shard_map/ppermute | solution.py:314
  33.9 0.0 copy-start
  33.9 1.6 copy-done
  35.5 0.7 copy-done.6
  36.1 0.7 copy-done.7
  36.8 1.2 prepare_kernel.1
  38.0 8.4 %collective-permute-start = (bf16[16,64,128]{2,1,0:T(8,128)(2,1)S(1)}, bf16[16,64,128]{2,1,0:T(8,128)(2,1)S(1)}, u32[]{:S(2)}, u32[]{:S(2)}) collective-permute-start(bf16[16,64,128]{2,1,0:T(8,128)(2,1)S(1)} %all_to_all.30.own), channel_id=1, source_target_pairs={{0,8},{8,0},{16,24},{24,16},{32,40},{40,32},{48,56},{56,48},{64,72... | collective-permute-start | bytes 786440 | tf_op jit(solution)/shard_map/ppermute | solution.py:315
  46.4 1.9 %collective-permute-start.2 = (bf16[16,64,128]{2,1,0:T(8,128)(2,1)S(1)}, bf16[16,64,128]{2,1,0:T(8,128)(2,1)S(1)}, u32[]{:S(2)}, u32[]{:S(2)}) collective-permute-start(bf16[16,64,128]{2,1,0:T(8,128)(2,1)S(1)} %collective-permute-done.1.other), channel_id=1, source_target_pairs={{0,8},{8,0},{16,24},{24,16},{32,40},{40,32},{48,56},{56,48},{64,72... | collective-permute-start | bytes 786440 | tf_op jit(solution)/shard_map/ppermute | solution.py:324
  48.3 0.0 collective-permute-done.core
  48.3 1.5 collective-permute-done.2.both
  49.8 14.3 %first_kernel.1 = (f32[8,128,128]{2,1,0:T(8,128)S(1)}, bf16[64,128,128]{2,1,0:T(8,128)(2,1)S(1)}, bf16[64,64,128]{2,1,0:T(8,128)(2,1)S(1)}, f32[64,128]{1,0:T(8,128)S(1)}) custom-call(s32[8,128]{1,0:T(8,128)S(1)} %get-tuple-element.23.info, bf16[64,16384]{1,0:T(8,128)(2,1)S(1)} %bitcast.11, bf16[16,64,128]{2,1,0:T(8,128)(2,1)S(1)} %all_to_all.30.own, ...), custom_call_target="tpu_custom_call" | custom-call | tf_op jit(solution)/shard_map/first_kernel/pallas_call | solution.py:326
  64.2 14.7 %all_to_all.31.parts = f32[8,128,128]{2,1,0:T(8,128)S(1)} all-to-all(f32[8,128,128]{2,1,0:T(8,128)S(1)} %get-tuple-element.30), channel_id=1, replica_groups=mesh['src'=64,'tgt'=8] {'tgt'}, dimensions={0} | all-to-all | bytes 1048576 | tf_op jit(solution)/shard_map/all_to_all | solution.py:332
  78.9 13.1 %second_kernel.1 = (f32[4,16,128]{2,1,0:T(8,128)S(1)}, f32[128,128]{1,0:T(8,128)S(1)}) custom-call(s32[8,128]{1,0:T(8,128)S(1)} %get-tuple-element.21.info, bf16[128,128,128]{2,1,0:T(8,128)(2,1)S(1)} %get-tuple-element.22.rows, bf16[64,64,128]{2,1,0:T(8,128)(2,1)S(1)} %get-tuple-element.28.targets, f32[8,128,128]{2,1,0:T(8,128)S(1)} %all_to_all.31.parts, ...), custom_call_target="tpu_custom_call" | custom-call | tf_op jit(solution)/shard_map/second_kernel/pallas_call | solution.py:333
  92.0 9.3 %all_to_all.32.parts = f32[4,16,128]{2,1,0:T(8,128)S(1)} all-to-all(f32[4,16,128]{2,1,0:T(8,128)S(1)} %get-tuple-element.32), channel_id=1, replica_groups={{0,8,16,24},{32,40,48,56},{64,72,80,88},{96,104,112,120},{128,136,144,1..., dimensions={0} | all-to-all | bytes 65536 | tf_op jit(solution)/shard_map/all_to_all | solution.py:339
  101.3 17.1 %all_to_all.33.parts = f32[16,16,128]{2,1,0:T(8,128)S(1)} all-to-all(f32[16,16,128]{2,1,0:T(8,128)S(1)} %group_kernel.1), channel_id=1, replica_groups={{0,32,64,96,128,160,192,224,256,288,320,352,384,416,448,480},{8,40,72,1..., dimensions={0} | all-to-all | bytes 262144 | tf_op jit(solution)/shard_map/all_to_all | solution.py:341
  118.5 8.8 %all_gather.9.lse = f32[64,128]{1,0:T(8,128)S(1)} all-gather(f32[16,128]{1,0:T(8,128)S(1)} %ring_kernel.1), channel_id=1, replica_groups={{0,8,16,24},{32,40,48,56},{64,72,80,88},{96,104,112,120},{128,136,144,1..., dimensions={0}, use_global_device_ids=true | all-gather | bytes 40960 | tf_op jit(solution)/shard_map/all_gather | solution.py:343
  127.2 5.1 %third_kernel.1 = (f32[8,128,128]{2,1,0:T(8,128)S(1)}, f32[64,128]{1,0:T(8,128)S(1)}, f32[1,128]{1,0:T(1,128)S(1)}) custom-call(s32[8,128]{1,0:T(8,128)S(1)} %get-tuple-element.23.info, bf16[64,16384]{1,0:T(8,128)(2,1)S(1)} %bitcast.12, bf16[64,128,128]{2,1,0:T(8,128)(2,1)S(1)} %get-tuple-element.29.rows, f32[64,128]{1,0:T(8,128)S(1)} %all_gather.9.lse, ...), custom_call_target="tpu_custom_call" | custom-call | tf_op jit(solution)/shard_map/third_kernel/pallas_call | solution.py:344
  132.4 14.5 %all_to_all.34.parts = f32[8,128,128]{2,1,0:T(8,128)S(1)} all-to-all(f32[8,128,128]{2,1,0:T(8,128)S(1)} %get-tuple-element.34), channel_id=1, replica_groups=mesh['src'=64,'tgt'=8] {'tgt'}, dimensions={0} | all-to-all | bytes 1048576 | tf_op jit(solution)/shard_map/all_to_all | solution.py:350
  146.9 5.4 %fourth_kernel.1 = (f32[64,128]{1,0:T(8,128)S(1)}, f32[128,128]{1,0:T(8,128)}, s32[32,128]{1,0:T(8,128)S(1)}) custom-call(s32[8,128]{1,0:T(8,128)S(1)} %get-tuple-element.21.info, bf16[128,128,128]{2,1,0:T(8,128)(2,1)S(1)} %get-tuple-element.22.rows, bf16[64,64,128]{2,1,0:T(8,128)(2,1)S(1)} %get-tuple-element.28.targets, ...), custom_call_target="tpu_custom_call" | custom-call | tf_op jit(solution)/shard_map/fourth_kernel/pallas_call | solution.py:351
  152.2 3.7 %all-gather = f32[128,128]{1,0:T(8,128)S(1)} all-gather(f32[64,128]{1,0:T(8,128)S(1)} %get-tuple-element.37), channel_id=2, replica_groups={{0,8},{16,24},{32,40},{48,56},{64,72},{80,88},{96,104},{112,120},{128,1..., dimensions={0}, use_global_device_ids=true | all-gather | bytes 98304 | tf_op jit(solution)/shard_map/all_gather | solution.py:357
  155.9 15.0 %all_to_all.35.parts = f32[32,1,128]{2,1,0:T(1,128)S(1)} all-to-all(f32[32,1,128]{2,1,0:T(1,128)S(1)} %total_kernel.1), channel_id=1, replica_groups={{0,16,32,48,64,80,96,112,128,144,160,176,192,208,224,240,256,272,288,30..., dimensions={0} | all-to-all | bytes 32768 | tf_op jit(solution)/shard_map/all_to_all | solution.py:359
  171.0 0.6 last_kernel.1
  (16 shorter events, 0.1 us)
Async XLA Ops:
  0.6 49.2 %copy-start.4 = (f32[8192]{0:T(1024)S(1)}, f32[8192]{0:T(1024)}, u32[]{:S(2)}) copy-start(f32[8192]{0:T(1024)} %param.10) | copy-start | bytes 98308
  30.1 16.3 %collective-permute-start.1 = (bf16[16,64,128]{2,1,0:T(8,128)(2,1)S(1)}, bf16[16,64,128]{2,1,0:T(8,128)(2,1)S(1)}, u32[]{:S(2)}, u32[]{:S(2)}) collective-permute-start(bf16[16,64,128]{2,1,0:T(8,128)(2,1)S(1)} %all_to_all.30.own), channel_id=1, source_target_pairs={{0,16},{8,24},{16,0},{24,8},{32,48},{40,56},{48,32},{56,40},{64,80... | collective-permute-start | bytes 786440 | tf_op jit(solution)/shard_map/ppermute | solution.py:314
  33.9 1.6 copy-start
  35.5 0.7 copy-start.6
  36.1 0.7 copy-start.7
  38.0 10.3 %collective-permute-start = (bf16[16,64,128]{2,1,0:T(8,128)(2,1)S(1)}, bf16[16,64,128]{2,1,0:T(8,128)(2,1)S(1)}, u32[]{:S(2)}, u32[]{:S(2)}) collective-permute-start(bf16[16,64,128]{2,1,0:T(8,128)(2,1)S(1)} %all_to_all.30.own), channel_id=1, source_target_pairs={{0,8},{8,0},{16,24},{24,16},{32,40},{40,32},{48,56},{56,48},{64,72... | collective-permute-start | bytes 786440 | tf_op jit(solution)/shard_map/ppermute | solution.py:315
  46.4 3.4 %collective-permute-start.2 = (bf16[16,64,128]{2,1,0:T(8,128)(2,1)S(1)}, bf16[16,64,128]{2,1,0:T(8,128)(2,1)S(1)}, u32[]{:S(2)}, u32[]{:S(2)}) collective-permute-start(bf16[16,64,128]{2,1,0:T(8,128)(2,1)S(1)} %collective-permute-done.1.other), channel_id=1, source_target_pairs={{0,8},{8,0},{16,24},{24,16},{32,40},{40,32},{48,56},{56,48},{64,72... | collective-permute-start | bytes 786440 | tf_op jit(solution)/shard_map/ppermute | solution.py:324
  49.8 29.1 %copy-start.2 = (f32[16384]{0:T(1024)S(1)}, f32[16384]{0:T(1024)}, u32[]{:S(2)}) copy-start(f32[16384]{0:T(1024)} %param.11) | copy-start | bytes 196612
  78.9 48.3 %copy-start.1 = (bf16[16384,64]{0,1:T(8,128)(2,1)S(1)}, bf16[16384,64]{0,1:T(8,128)(2,1)}, u32[]{:S(2)}) copy-start(bf16[16384,64]{0,1:T(8,128)(2,1)} %param.8) | copy-start | bytes 6291460
  78.9 48.3 %copy-start.3 = (bf16[128,64]{0,1:T(8,128)(2,1)S(1)}, bf16[128,64]{0,1:T(8,128)(2,1)}, u32[]{:S(2)}) copy-start(bf16[128,64]{0,1:T(8,128)(2,1)} %param.9) | copy-start | bytes 49156
  78.9 48.3 %copy-start.5 = (f32[8192]{0:T(1024)S(1)}, f32[8192]{0:T(1024)}, u32[]{:S(2)}) copy-start(f32[8192]{0:T(1024)} %param.12) | copy-start | bytes 98308

commit v6 on v5

--- a/solution.py
+++ b/solution.py
@@ -164,16 +164,13 @@
     me = lax.axis_index("src")
     lane = lax.broadcasted_iota(jnp.int32, (1, BLK), 1)
     count = jnp.broadcast_to(pair_count[...], (1, BLK))
-    steps = (count + (UNROLL - 1)) >> STEP_BITS
-    for k, value in enumerate((me, me & 1, me & 3, steps, count)):
-        head = value if k == 0 else jnp.where(lane == 4 - k, value, head)
-    by_src[0:1, :] = jnp.broadcast_to(head, (1, BLK))
-    by_tgt[0:1, :] = jnp.broadcast_to(head, (1, BLK))
+    by_src[0:1, :] = count
+    by_tgt[0:1, :] = count
     for half in range(2):
         used = lane + half * BLK < count
         part = slice(half * BLK, (half + 1) * BLK)
         s, t = jnp.where(used, pair_src[:, part], 0), jnp.where(used, pair_tgt[:, part], 0)
-        place = (((t ^ me) & 3) << 4) + (t >> 2)
+        place = (((t ^ (me & 2)) & 3) << 4) + (t >> 2)
         by_src[half + 1 : half + 2, :] = t + (s << 7) + (place << 14) + (jnp.where(used, s, 128) << (OWNER + 3))
         by_tgt[half + 1 : half + 2, :] = s + (place << 14) + (jnp.where(used, t, 64) << (OWNER + 3))
     line = lax.broadcasted_iota(jnp.int32, (DIM, BLK), 0)
@@ -192,19 +189,22 @@
 
 
 def first_kernel(
-    info, sources, own, core, other, both, start, source_norms, hot,
-    out, rows, targets, potential, norms, columns, extra, offset, *accs,
+    words, sources, own, other, start, source_norms, hot,
+    out, rows, targets, potential, info, arrival, norms, columns, extra, offset, *accs,
 ):
-    mine = info[0, 2]
-    for d, part in enumerate((own, core, other, both)):
+    coming = pltpu.make_async_copy(words, info, arrival)
+    coming.start()
+    mine = lax.axis_index("src") & 2
+    for d in range(4):
         for z in range(16):
-            block = part[z]
+            block = (own, other)[d >> 1][d & 1, z]
             targets[d * 16 + z] = block
             rows[d * 16 + z] = as_rows(block)
             norms[pl.ds(z * 4 + (d ^ mine), 1), :] = norm_row(block)
     new = start[...] * (1.0 / EPS) - norms[...] * (SCALE / 2)
     potential[...] = new
     spread(new, columns, extra)
+    coming.wait()
     tile = by_source(rows, sources, extra, hot)
 
     def write(lse):
@@ -214,10 +214,15 @@
     guarded_lse(info, tile, accs, 128, source_norms[...] * (-LOG2E * SCALE / 2), offset, write)
 
 
-def second_kernel(info, rows, targets, parts, mass, former, hot, out, potential, columns, extra, offset, *accs):
+def second_kernel(
+    words, rows, targets, parts, mass, former, hot, out, potential, info, arrival, columns, extra, offset, *accs
+):
+    coming = pltpu.make_async_copy(words, info, arrival)
+    coming.start()
     new = mass[...] - merge_lse(parts)
     potential[...] = new
     spread(new, columns, extra)
+    coming.wait()
     tile = by_target(rows, targets, extra, hot)
 
     def write(lse):
@@ -238,14 +243,18 @@
 
 
 def third_kernel(
-    info, sources, rows, lse, mass, reference, hot, mine, out, potential, base, columns, extra, offset, acc
+    words, sources, rows, lse, mass, reference, hot, mine,
+    out, potential, base, info, arrival, columns, extra, offset, acc,
 ):
-    me = info[0, 4]
+    coming = pltpu.make_async_copy(words, info, arrival)
+    coming.start()
+    me = lax.axis_index("src")
     new = mass[...] - lse[...]
     potential[...] = new
     base[...] = potential[pl.ds(me, 1), :] + mass[pl.ds(me, 1), :] + norm_row(mine[...]) * (SCALE / 2)
     spread(new, columns, extra)
     repeat_rows(reference[...] * LOG2E, offset)
+    coming.wait()
     tile = by_source(rows, sources, extra, hot)
     total = plain_sum(info, tile, acc, 128, offset)
     for k in range(8):
@@ -253,14 +262,17 @@
 
 
 def fourth_kernel(
-    info, rows, targets, parts, mass, former, reference, norms, hot,
-    out, final, odd, columns, extra, offset, acc,
+    words, rows, targets, parts, mass, former, reference, norms, hot,
+    out, final, odd, info, arrival, columns, extra, offset, acc,
 ):
+    coming = pltpu.make_async_copy(words, info, arrival)
+    coming.start()
     new = former[...] + mass[...] - jnp.log(jnp.sum(parts[...], axis=0))
     spread(new, columns, extra)
     final[...] = EPS * (new + norms[...] * (SCALE / 2))
-    odd[...] = jnp.full(odd.shape, info[0, 3], jnp.int32)
+    odd[...] = jnp.full(odd.shape, lax.axis_index("src") & 1, jnp.int32)
     repeat_rows(reference[...] * LOG2E, offset)
+    coming.wait()
     tile = by_target(rows, targets, extra, hot)
     out[...] = plain_sum(info, tile, acc, 64, offset)
 
@@ -274,14 +286,13 @@
     out[...] = EPS * (base[...] - jnp.log(jnp.sum(parts[...], axis=0)))
 
 
-def call(kernel, kinds, outs, scratch=()):
-    specs = [pl.BlockSpec(memory_space=SMEM if kind == "s" else VMEM) for kind in kinds]
+def call(kernel, inputs, outs, scratch=()):
     out_specs = [pl.BlockSpec(memory_space=VMEM) for _ in outs]
     shapes = [jax.ShapeDtypeStruct(shape, dtype) for shape, dtype in outs]
     single = len(outs) == 1
     return pl.pallas_call(
         kernel,
-        in_specs=specs,
+        in_specs=[pl.BlockSpec(memory_space=VMEM) for _ in range(inputs)],
         out_specs=out_specs[0] if single else out_specs,
         out_shape=shapes[0] if single else shapes,
         scratch_shapes=list(scratch),
@@ -290,6 +301,9 @@
     )
 
 
+WORDS = [SMEM((8, BLK), jnp.int32), pltpu.SemaphoreType.DMA]
+
+
 def columns_of(blocks):
     return [VMEM((blocks * 4, BLK), f32), VMEM((blocks // 16, BLK, BLK), bf16)]
 
@@ -303,7 +317,6 @@
     chips = [[z * 4 + r for r in range(4)] for z in range(16)]
     cores = [[i, i + 1] for i in range(0, 64, 2)]
     halves = [[2 * i + c for i in range(32)] for c in range(2)]
-    to_core = [(i, i ^ 1) for i in range(64)]
     to_chip = [(i, i ^ 2) for i in range(64)]
 
     source_mass = source_logmass.reshape(-1, BLK)
@@ -312,52 +325,52 @@
     mine = target_cells.T
     own = lax.all_to_all(jnp.broadcast_to(mine[None], (16, DIM, BLK)), "src", 0, 0, axis_index_groups=ring)
     other = lax.ppermute(own, "src", to_chip)
-    core = lax.ppermute(own, "src", to_core)
+    own = lax.all_gather(own, "src", axis=0, axis_index_groups=cores)
     sources = source_cells.T
     table = ((8, BLK), jnp.int32)
     rows, norms, hot, info_s, info_t = call(
         prepare_kernel,
-        "vvvv",
+        4,
         [((128, BLK, BLK), bf16), ((128, BLK), f32), ((16, DIM, BLK), bf16), table, table],
     )(sources, pair_src.reshape(1, -1), pair_tgt.reshape(1, -1), pair_count)
     other, hot = lax.optimization_barrier((other, hot))
-    both = lax.ppermute(other, "src", to_core)
+    other = lax.all_gather(other, "src", axis=0, axis_index_groups=cores)
 
     parts, target_rows, targets, start_v = call(
         first_kernel,
-        "svvvvvvvv",
+        7,
         [((8, 128, BLK), f32), ((64, BLK, BLK), bf16), ((64, DIM, BLK), bf16), ((64, BLK), f32)],
-        [VMEM((64, BLK), f32)] + columns_of(64) + accumulators(128, 3),
-    )(info_s, sources, own, core, other, both, start.reshape(-1, BLK), norms, hot)
+        WORDS + [VMEM((64, BLK), f32)] + columns_of(64) + accumulators(128, 3),
+    )(info_s, sources, own, other, start.reshape(-1, BLK), norms, hot)
     parts = lax.all_to_all(parts, "tgt", 0, 0)
     lse, first_u = call(
         second_kernel,
-        "svvvvvv",
+        7,
         [((4, 16, BLK), f32), ((128, BLK), f32)],
-        columns_of(128) + accumulators(64, 3),
+        WORDS + columns_of(128) + accumulators(64, 3),
     )(info_t, rows, targets, parts, source_mass, start_v, hot)
     lse = lax.all_to_all(lse, "src", 0, 0, axis_index_groups=chips)
-    lse = call(group_kernel, "v", [((16, 16, BLK), f32)])(lse)
+    lse = call(group_kernel, 1, [((16, 16, BLK), f32)])(lse)
     lse = lax.all_to_all(lse, "src", 0, 0, axis_index_groups=ring)
-    lse = call(ring_kernel, "v", [((16, BLK), f32)])(lse)
+    lse = call(ring_kernel, 1, [((16, BLK), f32)])(lse)
     lse = lax.all_gather(lse, "src", axis=0, axis_index_groups=chips, tiled=True)
     parts, first_v, base = call(
         third_kernel,
-        "svvvvvvv",
+        8,
         [((8, 128, BLK), f32), ((64, BLK), f32), ((1, BLK), f32)],
-        columns_of(64) + accumulators(128, 2),
+        WORDS + columns_of(64) + accumulators(128, 2),
     )(info_s, sources, target_rows, lse, target_mass, first_u, hot, mine)
     parts = lax.all_to_all(parts, "tgt", 0, 0)
     sums, last_u, odd = call(
         fourth_kernel,
-        "svvvvvvvv",
+        9,
         [((64, BLK), f32), ((128, BLK), f32), ((32, BLK), jnp.int32)],
-        columns_of(128) + accumulators(64, 2),
+        WORDS + columns_of(128) + accumulators(64, 2),
     )(info_t, rows, targets, parts, source_mass, first_u, first_v, norms, hot)
     sums = lax.all_gather(sums, "src", axis=0, axis_index_groups=cores)
-    sums = call(total_kernel, "vv", [((32, 1, BLK), f32)])(sums, odd)
+    sums = call(total_kernel, 2, [((32, 1, BLK), f32)])(sums, odd)
     sums = lax.all_to_all(sums, "src", 0, 0, axis_index_groups=halves)
-    last_v = call(last_kernel, "vv", [((1, BLK), f32)])(sums, base)
+    last_v = call(last_kernel, 2, [((1, BLK), f32)])(sums, base)
     return last_u.reshape(-1), last_v.reshape(-1)
 
 

time: 172 us -> 169 us (0.983)
  blocking collectives: 112 us -> 129 us
  starting transfers between devices: 13.4 us -> 3.11 us
  Pallas kernels: 39.8 us -> 31.6 us
    all_gather x0 -> x2, blocking collectives: none -> 10.4 us  [the longest x1 8.27 us: on_device(): own = lax.all_gather(own, 'src', axis=0, axis_index_groups=cores)]
    ppermute x2 -> x0, starting transfers between devices: 10.3 us -> none  [the longest x1 8.37 us: on_device(): core = lax.ppermute(own, 'src', to_core)]
    pallas_call x9, Pallas kernels: 39.8 us -> 31.6 us  [the longest x1 11.3 us: on_device(): call(first_kernel, 7, [((8, 128, BLK), f32), ((64, BLK, BLK), bf16), ((64...]
    all_to_all x1, blocking collectives: 17.1 us -> 22 us  [on_device(): lse = lax.all_to_all(lse, 'src', 0, 0, axis_index_groups=ring)]
    all_to_all x1, blocking collectives: 15 us -> 17.7 us  [on_device(): sums = lax.all_to_all(sums, 'src', 0, 0, axis_index_groups=halves)]
  transfers between devices with their start and end apart: 3 -> 1, of which waited for: 1 -> 0; matrix products, arithmetic and copies ran while one was open for 0% -> 0% of each run, Pallas kernels for 1% -> 1%
where the time goes in v6:
time: 169 us
  blocking collectives  129 us (76%)
  Pallas kernels  31.6 us (19%)
  local copies, waits for them, and re-layouts  3.73 us (2%)
  starting transfers between devices  3.11 us (2%)
    all_to_all x1, blocking collectives, on_device(): lax.all_to_all(jnp.broadcast_to(mine[None], (16, DIM, BLK)), 'src', 0, 0,...  28.7 us
    all_to_all x2, blocking collectives, on_device(): parts = lax.all_to_all(parts, 'tgt', 0, 0)  27.9 us
    all_to_all x1, blocking collectives, on_device(): lse = lax.all_to_all(lse, 'src', 0, 0, axis_index_groups=ring)  22 us
    all_to_all x1, blocking collectives, on_device(): sums = lax.all_to_all(sums, 'src', 0, 0, axis_index_groups=halves)  17.7 us
    pallas_call x1, Pallas kernels, on_device(): call(first_kernel, 7, [((8, 128, BLK), f32), ((64, BLK, BLK), bf16), ((64...  11.3 us
    pallas_call x1, Pallas kernels, on_device(): call(second_kernel, 7, [((4, 16, BLK), f32), ((128, BLK), f32)], WORDS +...  10.1 us
    all_gather x1, blocking collectives, on_device(): lax.all_gather(lse, 'src', axis=0, axis_index_groups=chips, tiled=True)  8.76 us
    all_to_all x1, blocking collectives, on_device(): lse = lax.all_to_all(lse, 'src', 0, 0, axis_index_groups=chips)  8.63 us
  transfers between devices with their start and end apart: 1, of which 0 were waited for; matrix products, arithmetic and copies ran while one was open for 0% of the time, Pallas kernels for 1%

profile of v6, /device:TPU:1, one launch (start us, length us, event | category | flops | bytes accessed | tf_op | source)
XLA Modules:
  0.0 168.9 jit_solution(12043952451781921496)
XLA Ops:
  0.6 0.8 broadcast_in_dim.2
  1.4 0.0 copy-start.4
  1.4 28.7 %all_to_all.30 = bf16[16,64,128]{2,1,0:T(8,128)(2,1)S(1)} all-to-all(bf16[16,64,128]{2,1,0:T(8,128)(2,1)S(1)} %broadcast_in_dim.2), channel_id=1, replica_groups={{0,32,64,96,128,160,192,224,256,288,320,352,384,416,448,480},{8,40,72,1..., dimensions={0} | all-to-all | bytes 524288 | tf_op jit(solution)/shard_map/all_to_all | solution.py:326
  30.1 3.1 %collective-permute-start = (bf16[16,64,128]{2,1,0:T(8,128)(2,1)S(1)}, bf16[16,64,128]{2,1,0:T(8,128)(2,1)S(1)}, u32[]{:S(2)}, u32[]{:S(2)}) collective-permute-start(bf16[16,64,128]{2,1,0:T(8,128)(2,1)S(1)} %all_to_all.30), channel_id=1, source_target_pairs={{0,16},{8,24},{16,0},{24,8},{32,48},{40,56},{48,32},{56,40},{64,80... | collective-permute-start | bytes 786440 | tf_op jit(solution)/shard_map/ppermute | solution.py:327
  33.9 0.0 copy-start
  33.9 1.6 copy-done
  35.5 0.7 copy-done.6
  36.1 0.7 copy-done.7
  36.8 1.2 prepare_kernel.1
  38.0 8.3 %all-gather = bf16[32,64,128]{2,1,0:T(8,128)(2,1)S(1)} all-gather(bf16[16,64,128]{2,1,0:T(8,128)(2,1)S(1)} %all_to_all.30), channel_id=2, replica_groups={{0,8},{16,24},{32,40},{48,56},{64,72},{80,88},{96,104},{112,120},{128,1..., dimensions={0}, use_global_device_ids=true | all-gather | bytes 786432 | tf_op jit(solution)/shard_map/all_gather | solution.py:328
  46.3 0.0 collective-permute-done
  46.3 2.2 %all-gather.1 = bf16[32,64,128]{2,1,0:T(8,128)(2,1)S(1)} all-gather(bf16[16,64,128]{2,1,0:T(8,128)(2,1)S(1)} %collective-permute-done), channel_id=3, replica_groups={{0,8},{16,24},{32,40},{48,56},{64,72},{80,88},{96,104},{112,120},{128,1..., dimensions={0}, use_global_device_ids=true | all-gather | bytes 786432 | tf_op jit(solution)/shard_map/all_gather | solution.py:337
  48.5 11.3 %first_kernel.1 = (f32[8,128,128]{2,1,0:T(8,128)S(1)}, bf16[64,128,128]{2,1,0:T(8,128)(2,1)S(1)}, bf16[64,64,128]{2,1,0:T(8,128)(2,1)S(1)}, f32[64,128]{1,0:T(8,128)S(1)}) custom-call(s32[8,128]{1,0:T(8,128)S(1)} %get-tuple-element.23.words, bf16[64,16384]{1,0:T(8,128)(2,1)S(1)} %bitcast.13, bf16[2,16,64,128]{3,2,1,0:T(8,128)(2,1)S(1)} %bitcast.15, ...), custom_call_target="tpu_custom_call" | custom-call | tf_op jit(solution)/shard_map/first_kernel/pallas_call | solution.py:339
  59.8 16.4 %all_to_all.31.parts = f32[8,128,128]{2,1,0:T(8,128)S(1)} all-to-all(f32[8,128,128]{2,1,0:T(8,128)S(1)} %get-tuple-element.30), channel_id=1, replica_groups=mesh['src'=64,'tgt'=8] {'tgt'}, dimensions={0} | all-to-all | bytes 1048576 | tf_op jit(solution)/shard_map/all_to_all | solution.py:345
  76.3 10.1 %second_kernel.1 = (f32[4,16,128]{2,1,0:T(8,128)S(1)}, f32[128,128]{1,0:T(8,128)S(1)}) custom-call(s32[8,128]{1,0:T(8,128)S(1)} %get-tuple-element.21.words, bf16[128,128,128]{2,1,0:T(8,128)(2,1)S(1)} %get-tuple-element.22.rows, bf16[64,64,128]{2,1,0:T(8,128)(2,1)S(1)} %get-tuple-element.28.targets, f32[8,128,128]{2,1,0:T(8,128)S(1)} %all_to_all.31.parts, ...), custom_call_target="tpu_custom_call" | custom-call | tf_op jit(solution)/shard_map/second_kernel/pallas_call | solution.py:346
  86.4 8.6 %all_to_all.32.parts = f32[4,16,128]{2,1,0:T(8,128)S(1)} all-to-all(f32[4,16,128]{2,1,0:T(8,128)S(1)} %get-tuple-element.32), channel_id=1, replica_groups={{0,8,16,24},{32,40,48,56},{64,72,80,88},{96,104,112,120},{128,136,144,1..., dimensions={0} | all-to-all | bytes 65536 | tf_op jit(solution)/shard_map/all_to_all | solution.py:352
  95.1 22.0 %all_to_all.33.parts = f32[16,16,128]{2,1,0:T(8,128)S(1)} all-to-all(f32[16,16,128]{2,1,0:T(8,128)S(1)} %group_kernel.1), channel_id=1, replica_groups={{0,32,64,96,128,160,192,224,256,288,320,352,384,416,448,480},{8,40,72,1..., dimensions={0} | all-to-all | bytes 262144 | tf_op jit(solution)/shard_map/all_to_all | solution.py:354
  117.2 8.8 %all_gather.25.lse = f32[64,128]{1,0:T(8,128)S(1)} all-gather(f32[16,128]{1,0:T(8,128)S(1)} %ring_kernel.1), channel_id=1, replica_groups={{0,8,16,24},{32,40,48,56},{64,72,80,88},{96,104,112,120},{128,136,144,1..., dimensions={0}, use_global_device_ids=true | all-gather | bytes 40960 | tf_op jit(solution)/shard_map/all_gather | solution.py:356
  125.9 3.9 %third_kernel.1 = (f32[8,128,128]{2,1,0:T(8,128)S(1)}, f32[64,128]{1,0:T(8,128)S(1)}, f32[1,128]{1,0:T(1,128)S(1)}) custom-call(s32[8,128]{1,0:T(8,128)S(1)} %get-tuple-element.23.words, bf16[64,16384]{1,0:T(8,128)(2,1)S(1)} %bitcast.14, bf16[64,128,128]{2,1,0:T(8,128)(2,1)S(1)} %get-tuple-element.29.rows, f32[64,128]{1,0:T(8,128)S(1)} %all_gather.25.lse, ...), custom_call_target="tpu_custom_call" | custom-call | tf_op jit(solution)/shard_map/third_kernel/pallas_call | solution.py:357
  129.9 11.5 %all_to_all.34.parts = f32[8,128,128]{2,1,0:T(8,128)S(1)} all-to-all(f32[8,128,128]{2,1,0:T(8,128)S(1)} %get-tuple-element.34), channel_id=1, replica_groups=mesh['src'=64,'tgt'=8] {'tgt'}, dimensions={0} | all-to-all | bytes 1048576 | tf_op jit(solution)/shard_map/all_to_all | solution.py:363
  141.4 4.3 %fourth_kernel.1 = (f32[64,128]{1,0:T(8,128)S(1)}, f32[128,128]{1,0:T(8,128)}, s32[32,128]{1,0:T(8,128)S(1)}) custom-call(s32[8,128]{1,0:T(8,128)S(1)} %get-tuple-element.21.words, bf16[128,128,128]{2,1,0:T(8,128)(2,1)S(1)} %get-tuple-element.22.rows, bf16[64,64,128]{2,1,0:T(8,128)(2,1)S(1)} %get-tuple-element.28.targets, ...), custom_call_target="tpu_custom_call" | custom-call | tf_op jit(solution)/shard_map/fourth_kernel/pallas_call | solution.py:364
  145.7 5.0 %all-gather.2 = f32[128,128]{1,0:T(8,128)S(1)} all-gather(f32[64,128]{1,0:T(8,128)S(1)} %get-tuple-element.37), channel_id=4, replica_groups={{0,8},{16,24},{32,40},{48,56},{64,72},{80,88},{96,104},{112,120},{128,1..., dimensions={0}, use_global_device_ids=true | all-gather | bytes 98304 | tf_op jit(solution)/shard_map/all_gather | solution.py:370
  150.7 17.7 %all_to_all.35.parts = f32[32,1,128]{2,1,0:T(1,128)S(1)} all-to-all(f32[32,1,128]{2,1,0:T(1,128)S(1)} %total_kernel.1), channel_id=1, replica_groups={{0,16,32,48,64,80,96,112,128,144,160,176,192,208,224,240,256,272,288,30..., dimensions={0} | all-to-all | bytes 32768 | tf_op jit(solution)/shard_map/all_to_all | solution.py:372
  168.3 0.6 last_kernel.1
  (14 shorter events, 0.1 us)
Async XLA Ops:
  1.4 47.1 %copy-start.4 = (f32[8192]{0:T(1024)S(1)}, f32[8192]{0:T(1024)}, u32[]{:S(2)}) copy-start(f32[8192]{0:T(1024)} %param.10) | copy-start | bytes 98308
  30.1 16.2 %collective-permute-start = (bf16[16,64,128]{2,1,0:T(8,128)(2,1)S(1)}, bf16[16,64,128]{2,1,0:T(8,128)(2,1)S(1)}, u32[]{:S(2)}, u32[]{:S(2)}) collective-permute-start(bf16[16,64,128]{2,1,0:T(8,128)(2,1)S(1)} %all_to_all.30), channel_id=1, source_target_pairs={{0,16},{8,24},{16,0},{24,8},{32,48},{40,56},{48,32},{56,40},{64,80... | collective-permute-start | bytes 786440 | tf_op jit(solution)/shard_map/ppermute | solution.py:327
  33.9 1.6 copy-start
  35.5 0.7 copy-start.6
  36.1 0.7 copy-start.7
  48.5 27.8 %copy-start.2 = (f32[16384]{0:T(1024)S(1)}, f32[16384]{0:T(1024)}, u32[]{:S(2)}) copy-start(f32[16384]{0:T(1024)} %param.11) | copy-start | bytes 196612
  76.3 49.7 %copy-start.1 = (bf16[16384,64]{0,1:T(8,128)(2,1)S(1)}, bf16[16384,64]{0,1:T(8,128)(2,1)}, u32[]{:S(2)}) copy-start(bf16[16384,64]{0,1:T(8,128)(2,1)} %param.8) | copy-start | bytes 6291460
  76.3 49.7 %copy-start.3 = (bf16[128,64]{0,1:T(8,128)(2,1)S(1)}, bf16[128,64]{0,1:T(8,128)(2,1)}, u32[]{:S(2)}) copy-start(bf16[128,64]{0,1:T(8,128)(2,1)} %param.9) | copy-start | bytes 49156
  76.3 49.7 %copy-start.5 = (f32[8192]{0:T(1024)S(1)}, f32[8192]{0:T(1024)}, u32[]{:S(2)}) copy-start(f32[8192]{0:T(1024)} %param.12) | copy-start | bytes 98308

commit v7 on v6

--- a/solution.py
+++ b/solution.py
@@ -19,7 +19,7 @@
 LIFT = 100.0
 OWNER = 20
 VMEM_LIMIT = 16 * 1024 * 1024
-STEP_BITS = 6
+STEP_BITS = 7
 UNROLL = 1 << STEP_BITS
 VMEM = pltpu.VMEM
 SMEM = pltpu.SMEM
@@ -263,7 +263,7 @@
 
 def fourth_kernel(
     words, rows, targets, parts, mass, former, reference, norms, hot,
-    out, final, odd, info, arrival, columns, extra, offset, acc,
+    out, final, odd, info, arrival, held, columns, extra, offset, acc,
 ):
     coming = pltpu.make_async_copy(words, info, arrival)
     coming.start()
@@ -274,12 +274,13 @@
     repeat_rows(reference[...] * LOG2E, offset)
     coming.wait()
     tile = by_target(rows, targets, extra, hot)
-    out[...] = plain_sum(info, tile, acc, 64, offset)
+    held[pl.ds(0, 64), :] = plain_sum(info, tile, acc, 64, offset)
+    for k in range(2):
+        out[k] = held[pl.ds(k, 32, stride=2), :]
 
 
 def total_kernel(parts, odd, out):
-    first, second = [parts[0, pl.ds(k, 32, stride=2), :] + parts[1, pl.ds(k, 32, stride=2), :] for k in range(2)]
-    out[...] = jnp.where(odd[...] == 0, first, second)[:, None, :]
+    out[...] = jnp.where(odd[...] == 0, parts[0, 0] + parts[1, 0], parts[0, 1] + parts[1, 1])[:, None, :]
 
 
 def last_kernel(parts, base, out):
@@ -305,7 +306,7 @@
 
 
 def columns_of(blocks):
-    return [VMEM((blocks * 4, BLK), f32), VMEM((blocks // 16, BLK, BLK), bf16)]
+    return [VMEM((blocks * 4 + 8, BLK), f32), VMEM((blocks // 16, BLK, BLK), bf16)]
 
 
 def accumulators(owners, number):
@@ -364,8 +365,8 @@
     sums, last_u, odd = call(
         fourth_kernel,
         9,
-        [((64, BLK), f32), ((128, BLK), f32), ((32, BLK), jnp.int32)],
-        WORDS + columns_of(128) + accumulators(64, 2),
+        [((2, 32, BLK), f32), ((128, BLK), f32), ((32, BLK), jnp.int32)],
+        WORDS + [VMEM((72, BLK), f32)] + columns_of(128) + accumulators(64, 2),
     )(info_t, rows, targets, parts, source_mass, first_u, first_v, norms, hot)
     sums = lax.all_gather(sums, "src", axis=0, axis_index_groups=cores)
     sums = call(total_kernel, 2, [((32, 1, BLK), f32)])(sums, odd)

time: 169 us -> 168 us (level)
  blocking collectives: 129 us -> 122 us
  Pallas kernels: 31.6 us -> 38.2 us
    all_to_all x1, blocking collectives: 22 us -> 16.9 us  [on_device(): lse = lax.all_to_all(lse, 'src', 0, 0, axis_index_groups=ring)]
    pallas_call x1, Pallas kernels: 11.3 us -> 14.1 us  [on_device(): call(first_kernel, 7, [((8, 128, BLK), f32), ((64, BLK, BLK), bf16), ((64...]
    pallas_call x1, Pallas kernels: 10.1 us -> 12.5 us  [on_device(): call(second_kernel, 7, [((4, 16, BLK), f32), ((128, BLK), f32)], WORDS +...]
    all_to_all x2, blocking collectives: 27.9 us -> 29.6 us  [on_device(): parts = lax.all_to_all(parts, 'tgt', 0, 0)]
    all_to_all x1, blocking collectives: 17.7 us -> 16 us  [on_device(): sums = lax.all_to_all(sums, 'src', 0, 0, axis_index_groups=halves)]
where the time goes in v7:
time: 168 us
  blocking collectives  122 us (73%)
  Pallas kernels  38.2 us (23%)
  local copies, waits for them, and re-layouts  3.73 us (2%)
  starting transfers between devices  3.11 us (2%)
    all_to_all x2, blocking collectives, on_device(): parts = lax.all_to_all(parts, 'tgt', 0, 0)  29.6 us
    all_to_all x1, blocking collectives, on_device(): lax.all_to_all(jnp.broadcast_to(mine[None], (16, DIM, BLK)), 'src', 0, 0,...  28.7 us
    all_to_all x1, blocking collectives, on_device(): lse = lax.all_to_all(lse, 'src', 0, 0, axis_index_groups=ring)  16.9 us
    all_to_all x1, blocking collectives, on_device(): sums = lax.all_to_all(sums, 'src', 0, 0, axis_index_groups=halves)  16 us
    pallas_call x1, Pallas kernels, on_device(): call(first_kernel, 7, [((8, 128, BLK), f32), ((64, BLK, BLK), bf16), ((64...  14.1 us
    pallas_call x1, Pallas kernels, on_device(): call(second_kernel, 7, [((4, 16, BLK), f32), ((128, BLK), f32)], WORDS +...  12.5 us
    all_gather x1, blocking collectives, on_device(): lax.all_gather(lse, 'src', axis=0, axis_index_groups=chips, tiled=True)  8.76 us
    all_gather x1, blocking collectives, on_device(): own = lax.all_gather(own, 'src', axis=0, axis_index_groups=cores)  8.27 us
  transfers between devices with their start and end apart: 1, of which 0 were waited for; matrix products, arithmetic and copies ran while one was open for 0% of the time, Pallas kernels for 1%

profile of v7, /device:TPU:1, one launch (start us, length us, event | category | flops | bytes accessed | tf_op | source)
XLA Modules:
  0.0 167.9 jit_solution(3265434007231189664)
XLA Ops:
  0.6 0.8 broadcast_in_dim.2
  1.4 0.0 copy-start.4
  1.4 28.7 %all_to_all.30 = bf16[16,64,128]{2,1,0:T(8,128)(2,1)S(1)} all-to-all(bf16[16,64,128]{2,1,0:T(8,128)(2,1)S(1)} %broadcast_in_dim.2), channel_id=1, replica_groups={{0,32,64,96,128,160,192,224,256,288,320,352,384,416,448,480},{8,40,72,1..., dimensions={0} | all-to-all | bytes 524288 | tf_op jit(solution)/shard_map/all_to_all | solution.py:327
  30.1 3.1 %collective-permute-start = (bf16[16,64,128]{2,1,0:T(8,128)(2,1)S(1)}, bf16[16,64,128]{2,1,0:T(8,128)(2,1)S(1)}, u32[]{:S(2)}, u32[]{:S(2)}) collective-permute-start(bf16[16,64,128]{2,1,0:T(8,128)(2,1)S(1)} %all_to_all.30), channel_id=1, source_target_pairs={{0,16},{8,24},{16,0},{24,8},{32,48},{40,56},{48,32},{56,40},{64,80... | collective-permute-start | bytes 786440 | tf_op jit(solution)/shard_map/ppermute | solution.py:328
  33.9 0.0 copy-start
  33.9 1.6 copy-done
  35.5 0.7 copy-done.6
  36.1 0.7 copy-done.7
  36.8 1.2 prepare_kernel.1
  38.0 8.3 %all-gather = bf16[32,64,128]{2,1,0:T(8,128)(2,1)S(1)} all-gather(bf16[16,64,128]{2,1,0:T(8,128)(2,1)S(1)} %all_to_all.30), channel_id=2, replica_groups={{0,8},{16,24},{32,40},{48,56},{64,72},{80,88},{96,104},{112,120},{128,1..., dimensions={0}, use_global_device_ids=true | all-gather | bytes 786432 | tf_op jit(solution)/shard_map/all_gather | solution.py:329
  46.3 0.0 collective-permute-done
  46.3 2.2 %all-gather.1 = bf16[32,64,128]{2,1,0:T(8,128)(2,1)S(1)} all-gather(bf16[16,64,128]{2,1,0:T(8,128)(2,1)S(1)} %collective-permute-done), channel_id=3, replica_groups={{0,8},{16,24},{32,40},{48,56},{64,72},{80,88},{96,104},{112,120},{128,1..., dimensions={0}, use_global_device_ids=true | all-gather | bytes 786432 | tf_op jit(solution)/shard_map/all_gather | solution.py:338
  48.5 14.1 %first_kernel.1 = (f32[8,128,128]{2,1,0:T(8,128)S(1)}, bf16[64,128,128]{2,1,0:T(8,128)(2,1)S(1)}, bf16[64,64,128]{2,1,0:T(8,128)(2,1)S(1)}, f32[64,128]{1,0:T(8,128)S(1)}) custom-call(s32[8,128]{1,0:T(8,128)S(1)} %get-tuple-element.23.words, bf16[64,16384]{1,0:T(8,128)(2,1)S(1)} %bitcast.13, bf16[2,16,64,128]{3,2,1,0:T(8,128)(2,1)S(1)} %bitcast.15, ...), custom_call_target="tpu_custom_call" | custom-call | tf_op jit(solution)/shard_map/first_kernel/pallas_call | solution.py:340
  62.5 16.6 %all_to_all.31.parts = f32[8,128,128]{2,1,0:T(8,128)S(1)} all-to-all(f32[8,128,128]{2,1,0:T(8,128)S(1)} %get-tuple-element.30), channel_id=1, replica_groups=mesh['src'=64,'tgt'=8] {'tgt'}, dimensions={0} | all-to-all | bytes 1048576 | tf_op jit(solution)/shard_map/all_to_all | solution.py:346
  79.2 12.5 %second_kernel.1 = (f32[4,16,128]{2,1,0:T(8,128)S(1)}, f32[128,128]{1,0:T(8,128)S(1)}) custom-call(s32[8,128]{1,0:T(8,128)S(1)} %get-tuple-element.21.words, bf16[128,128,128]{2,1,0:T(8,128)(2,1)S(1)} %get-tuple-element.22.rows, bf16[64,64,128]{2,1,0:T(8,128)(2,1)S(1)} %get-tuple-element.28.targets, f32[8,128,128]{2,1,0:T(8,128)S(1)} %all_to_all.31.parts, ...), custom_call_target="tpu_custom_call" | custom-call | tf_op jit(solution)/shard_map/second_kernel/pallas_call | solution.py:347
  91.7 7.2 %all_to_all.32.parts = f32[4,16,128]{2,1,0:T(8,128)S(1)} all-to-all(f32[4,16,128]{2,1,0:T(8,128)S(1)} %get-tuple-element.32), channel_id=1, replica_groups={{0,8,16,24},{32,40,48,56},{64,72,80,88},{96,104,112,120},{128,136,144,1..., dimensions={0} | all-to-all | bytes 65536 | tf_op jit(solution)/shard_map/all_to_all | solution.py:353
  98.9 16.9 %all_to_all.33.parts = f32[16,16,128]{2,1,0:T(8,128)S(1)} all-to-all(f32[16,16,128]{2,1,0:T(8,128)S(1)} %group_kernel.1), channel_id=1, replica_groups={{0,32,64,96,128,160,192,224,256,288,320,352,384,416,448,480},{8,40,72,1..., dimensions={0} | all-to-all | bytes 262144 | tf_op jit(solution)/shard_map/all_to_all | solution.py:355
  115.8 8.8 %all_gather.25.lse = f32[64,128]{1,0:T(8,128)S(1)} all-gather(f32[16,128]{1,0:T(8,128)S(1)} %ring_kernel.1), channel_id=1, replica_groups={{0,8,16,24},{32,40,48,56},{64,72,80,88},{96,104,112,120},{128,136,144,1..., dimensions={0}, use_global_device_ids=true | all-gather | bytes 40960 | tf_op jit(solution)/shard_map/all_gather | solution.py:357
  124.6 4.7 %third_kernel.1 = (f32[8,128,128]{2,1,0:T(8,128)S(1)}, f32[64,128]{1,0:T(8,128)S(1)}, f32[1,128]{1,0:T(1,128)S(1)}) custom-call(s32[8,128]{1,0:T(8,128)S(1)} %get-tuple-element.23.words, bf16[64,16384]{1,0:T(8,128)(2,1)S(1)} %bitcast.14, bf16[64,128,128]{2,1,0:T(8,128)(2,1)S(1)} %get-tuple-element.29.rows, f32[64,128]{1,0:T(8,128)S(1)} %all_gather.25.lse, ...), custom_call_target="tpu_custom_call" | custom-call | tf_op jit(solution)/shard_map/third_kernel/pallas_call | solution.py:358
  129.3 13.0 %all_to_all.34.parts = f32[8,128,128]{2,1,0:T(8,128)S(1)} all-to-all(f32[8,128,128]{2,1,0:T(8,128)S(1)} %get-tuple-element.34), channel_id=1, replica_groups=mesh['src'=64,'tgt'=8] {'tgt'}, dimensions={0} | all-to-all | bytes 1048576 | tf_op jit(solution)/shard_map/all_to_all | solution.py:364
  142.3 5.0 %fourth_kernel.1 = (f32[2,32,128]{2,1,0:T(8,128)S(1)}, f32[128,128]{1,0:T(8,128)}, s32[32,128]{1,0:T(8,128)S(1)}) custom-call(s32[8,128]{1,0:T(8,128)S(1)} %get-tuple-element.21.words, bf16[128,128,128]{2,1,0:T(8,128)(2,1)S(1)} %get-tuple-element.22.rows, bf16[64,64,128]{2,1,0:T(8,128)(2,1)S(1)} %get-tuple-element.28.targets, ...), custom_call_target="tpu_custom_call" | custom-call | tf_op jit(solution)/shard_map/fourth_kernel/pallas_call | solution.py:365
  147.4 4.0 %all-gather.2 = f32[4,32,128]{2,1,0:T(8,128)S(1)} all-gather(f32[2,32,128]{2,1,0:T(8,128)S(1)} %get-tuple-element.37), channel_id=4, replica_groups={{0,8},{16,24},{32,40},{48,56},{64,72},{80,88},{96,104},{112,120},{128,1..., dimensions={0}, use_global_device_ids=true | all-gather | bytes 98304 | tf_op jit(solution)/shard_map/all_gather | solution.py:371
  151.4 16.0 %all_to_all.35.parts = f32[32,1,128]{2,1,0:T(1,128)S(1)} all-to-all(f32[32,1,128]{2,1,0:T(1,128)S(1)} %total_kernel.1), channel_id=1, replica_groups={{0,16,32,48,64,80,96,112,128,144,160,176,192,208,224,240,256,272,288,30..., dimensions={0} | all-to-all | bytes 32768 | tf_op jit(solution)/shard_map/all_to_all | solution.py:373
  167.4 0.6 last_kernel.1
  (14 shorter events, 0.1 us)
Async XLA Ops:
  1.4 47.1 %copy-start.4 = (f32[8192]{0:T(1024)S(1)}, f32[8192]{0:T(1024)}, u32[]{:S(2)}) copy-start(f32[8192]{0:T(1024)} %param.10) | copy-start | bytes 98308
  30.1 16.2 %collective-permute-start = (bf16[16,64,128]{2,1,0:T(8,128)(2,1)S(1)}, bf16[16,64,128]{2,1,0:T(8,128)(2,1)S(1)}, u32[]{:S(2)}, u32[]{:S(2)}) collective-permute-start(bf16[16,64,128]{2,1,0:T(8,128)(2,1)S(1)} %all_to_all.30), channel_id=1, source_target_pairs={{0,16},{8,24},{16,0},{24,8},{32,48},{40,56},{48,32},{56,40},{64,80... | collective-permute-start | bytes 786440 | tf_op jit(solution)/shard_map/ppermute | solution.py:328
  33.9 1.6 copy-start
  35.5 0.7 copy-start.6
  36.1 0.7 copy-start.7
  48.5 30.7 %copy-start.2 = (f32[16384]{0:T(1024)S(1)}, f32[16384]{0:T(1024)}, u32[]{:S(2)}) copy-start(f32[16384]{0:T(1024)} %param.11) | copy-start | bytes 196612
  79.2 45.4 %copy-start.1 = (bf16[16384,64]{0,1:T(8,128)(2,1)S(1)}, bf16[16384,64]{0,1:T(8,128)(2,1)}, u32[]{:S(2)}) copy-start(bf16[16384,64]{0,1:T(8,128)(2,1)} %param.8) | copy-start | bytes 6291460
  79.2 45.4 %copy-start.3 = (bf16[128,64]{0,1:T(8,128)(2,1)S(1)}, bf16[128,64]{0,1:T(8,128)(2,1)}, u32[]{:S(2)}) copy-start(bf16[128,64]{0,1:T(8,128)(2,1)} %param.9) | copy-start | bytes 49156
  79.2 45.5 %copy-start.5 = (f32[8192]{0:T(1024)S(1)}, f32[8192]{0:T(1024)}, u32[]{:S(2)}) copy-start(f32[8192]{0:T(1024)} %param.12) | copy-start | bytes 98308

commit v8 on v7

--- a/solution.py
+++ b/solution.py
@@ -188,6 +188,10 @@
     return top + jnp.log(total)
 
 
+def ring_place(k, core):
+    return (k + 8 * core) % 16
+
+
 def first_kernel(
     words, sources, own, other, start, source_norms, hot,
     out, rows, targets, potential, info, arrival, norms, columns, extra, offset, *accs,
@@ -196,8 +200,9 @@
     coming.start()
     mine = lax.axis_index("src") & 2
     for d in range(4):
-        for z in range(16):
-            block = (own, other)[d >> 1][d & 1, z]
+        for k in range(16):
+            z = ring_place(k, d & 1)
+            block = (own, other)[d >> 1][d & 1, k]
             targets[d * 16 + z] = block
             rows[d * 16 + z] = as_rows(block)
             norms[pl.ds(z * 4 + (d ^ mine), 1), :] = norm_row(block)
@@ -280,7 +285,9 @@
 
 
 def total_kernel(parts, odd, out):
-    out[...] = jnp.where(odd[...] == 0, parts[0, 0] + parts[1, 0], parts[0, 1] + parts[1, 1])[:, None, :]
+    second = parts[0, 1] + parts[1, 1]
+    second = jnp.concatenate([second[16:], second[:16]], axis=0)
+    out[...] = jnp.where(odd[...] == 0, parts[0, 0] + parts[1, 0], second)[:, None, :]
 
 
 def last_kernel(parts, base, out):
@@ -314,10 +321,11 @@
 
 
 def on_device(source_cells, target_cells, start, source_logmass, target_logmass, pair_src, pair_tgt, pair_count):
-    ring = [[z * 4 + r for z in range(16)] for r in range(4)]
+    ring = [[ring_place(k, r & 1) * 4 + r for k in range(16)] for r in range(4)]
     chips = [[z * 4 + r for r in range(4)] for z in range(16)]
     cores = [[i, i + 1] for i in range(0, 64, 2)]
-    halves = [[2 * i + c for i in range(32)] for c in range(2)]
+    halves = [[2 * ((i + 16 * c) % 32) + c for i in range(32)] for c in range(2)]
+    columns = [[8 * i + (k + 4 * (i & 1)) % 8 for k in range(8)] for i in range(64)]
     to_chip = [(i, i ^ 2) for i in range(64)]
 
     source_mass = source_logmass.reshape(-1, BLK)
@@ -343,7 +351,7 @@
         [((8, 128, BLK), f32), ((64, BLK, BLK), bf16), ((64, DIM, BLK), bf16), ((64, BLK), f32)],
         WORDS + [VMEM((64, BLK), f32)] + columns_of(64) + accumulators(128, 3),
     )(info_s, sources, own, other, start.reshape(-1, BLK), norms, hot)
-    parts = lax.all_to_all(parts, "tgt", 0, 0)
+    parts = lax.all_to_all(parts, ("src", "tgt"), 0, 0, axis_index_groups=columns)
     lse, first_u = call(
         second_kernel,
         7,
@@ -361,7 +369,7 @@
         [((8, 128, BLK), f32), ((64, BLK), f32), ((1, BLK), f32)],
         WORDS + columns_of(64) + accumulators(128, 2),
     )(info_s, sources, target_rows, lse, target_mass, first_u, hot, mine)
-    parts = lax.all_to_all(parts, "tgt", 0, 0)
+    parts = lax.all_to_all(parts, ("src", "tgt"), 0, 0, axis_index_groups=columns)
     sums, last_u, odd = call(
         fourth_kernel,
         9,

time: 168 us -> 165 us (0.982); the launches traced: 168 us -> 162 us
  Pallas kernels: 38.2 us -> 31.7 us
    all_gather x1, blocking collectives: 8.27 us -> 2.91 us  [on_device(): own = lax.all_gather(own, 'src', axis=0, axis_index_groups=cores)]
    all_to_all x1, blocking collectives: 7.23 us -> 11.6 us  [on_device(): lse = lax.all_to_all(lse, 'src', 0, 0, axis_index_groups=chips)]
    all_to_all x1, blocking collectives: 16.9 us -> 20.7 us  [on_device(): lse = lax.all_to_all(lse, 'src', 0, 0, axis_index_groups=ring)]
    pallas_call x1, Pallas kernels: 14.1 us -> 10.7 us  [on_device(): call(first_kernel, 7, [((8, 128, BLK), f32), ((64, BLK, BLK), bf16), ((64...]
    pallas_call x1, Pallas kernels: 12.5 us -> 9.28 us  [on_device(): call(second_kernel, 7, [((4, 16, BLK), f32), ((128, BLK), f32)], WORDS +...]
    all_to_all x1, blocking collectives: 28.7 us -> 31.3 us  [on_device(): lax.all_to_all(jnp.broadcast_to(mine[None], (16, DIM, BLK)), 'src', 0, 0,...]
    all_to_all x1, blocking collectives: 16 us -> 14 us  [on_device(): sums = lax.all_to_all(sums, 'src', 0, 0, axis_index_groups=halves)]
where the time goes in v8:
time: 165 us; the launch traced here: 162 us
  blocking collectives  122 us (74%)
  Pallas kernels  31.7 us (19%)
  local copies, waits for them, and re-layouts  3.73 us (2%)
  starting transfers between devices  3.11 us (2%)
    all_to_all x1, blocking collectives, on_device(): lax.all_to_all(jnp.broadcast_to(mine[None], (16, DIM, BLK)), 'src', 0, 0,...  31.3 us
    all_to_all x2, blocking collectives, on_device(): lax.all_to_all(parts, ('src', 'tgt'), 0, 0, axis_index_groups=columns)  28 us
    all_to_all x1, blocking collectives, on_device(): lse = lax.all_to_all(lse, 'src', 0, 0, axis_index_groups=ring)  20.7 us
    all_to_all x1, blocking collectives, on_device(): sums = lax.all_to_all(sums, 'src', 0, 0, axis_index_groups=halves)  14 us
    all_to_all x1, blocking collectives, on_device(): lse = lax.all_to_all(lse, 'src', 0, 0, axis_index_groups=chips)  11.6 us
    pallas_call x1, Pallas kernels, on_device(): call(first_kernel, 7, [((8, 128, BLK), f32), ((64, BLK, BLK), bf16), ((64...  10.7 us
    pallas_call x1, Pallas kernels, on_device(): call(second_kernel, 7, [((4, 16, BLK), f32), ((128, BLK), f32)], WORDS +...  9.28 us
    all_gather x1, blocking collectives, on_device(): lax.all_gather(lse, 'src', axis=0, axis_index_groups=chips, tiled=True)  8.65 us
  transfers between devices with their start and end apart: 1, of which 0 were waited for; matrix products, arithmetic and copies ran while one was open for 0% of the time, Pallas kernels for 1%

profile of v8, /device:TPU:1, one launch (start us, length us, event | category | flops | bytes accessed | tf_op | source)
XLA Modules:
  0.0 161.9 jit_solution(12956322731953905380)
XLA Ops:
  0.6 0.8 broadcast_in_dim.2
  1.4 0.0 copy-start.4
  1.4 31.3 %all_to_all.30 = bf16[16,64,128]{2,1,0:T(8,128)(2,1)S(1)} all-to-all(bf16[16,64,128]{2,1,0:T(8,128)(2,1)S(1)} %broadcast_in_dim.2), channel_id=1, replica_groups={{0,32,64,96,128,160,192,224,256,288,320,352,384,416,448,480},{264,296,3..., dimensions={0} | all-to-all | bytes 524288 | tf_op jit(solution)/shard_map/all_to_all | solution.py:335
  32.7 3.1 %collective-permute-start = (bf16[16,64,128]{2,1,0:T(8,128)(2,1)S(1)}, bf16[16,64,128]{2,1,0:T(8,128)(2,1)S(1)}, u32[]{:S(2)}, u32[]{:S(2)}) collective-permute-start(bf16[16,64,128]{2,1,0:T(8,128)(2,1)S(1)} %all_to_all.30), channel_id=1, source_target_pairs={{0,16},{8,24},{16,0},{24,8},{32,48},{40,56},{48,32},{56,40},{64,80... | collective-permute-start | bytes 786440 | tf_op jit(solution)/shard_map/ppermute | solution.py:336
  36.5 0.0 copy-start
  36.5 1.6 copy-done
  38.0 0.7 copy-done.6
  38.7 0.7 copy-done.7
  39.4 1.2 prepare_kernel.1
  40.6 2.9 %all-gather = bf16[32,64,128]{2,1,0:T(8,128)(2,1)S(1)} all-gather(bf16[16,64,128]{2,1,0:T(8,128)(2,1)S(1)} %all_to_all.30), channel_id=2, replica_groups={{0,8},{16,24},{32,40},{48,56},{64,72},{80,88},{96,104},{112,120},{128,1..., dimensions={0}, use_global_device_ids=true | all-gather | bytes 786432 | tf_op jit(solution)/shard_map/all_gather | solution.py:337
  43.5 0.0 collective-permute-done
  43.5 2.2 %all-gather.1 = bf16[32,64,128]{2,1,0:T(8,128)(2,1)S(1)} all-gather(bf16[16,64,128]{2,1,0:T(8,128)(2,1)S(1)} %collective-permute-done), channel_id=3, replica_groups={{0,8},{16,24},{32,40},{48,56},{64,72},{80,88},{96,104},{112,120},{128,1..., dimensions={0}, use_global_device_ids=true | all-gather | bytes 786432 | tf_op jit(solution)/shard_map/all_gather | solution.py:346
  45.7 10.7 %first_kernel.1 = (f32[8,128,128]{2,1,0:T(8,128)S(1)}, bf16[64,128,128]{2,1,0:T(8,128)(2,1)S(1)}, bf16[64,64,128]{2,1,0:T(8,128)(2,1)S(1)}, f32[64,128]{1,0:T(8,128)S(1)}) custom-call(s32[8,128]{1,0:T(8,128)S(1)} %get-tuple-element.23.words, bf16[64,16384]{1,0:T(8,128)(2,1)S(1)} %bitcast.13, bf16[2,16,64,128]{3,2,1,0:T(8,128)(2,1)S(1)} %bitcast.15, ...), custom_call_target="tpu_custom_call" | custom-call | tf_op jit(solution)/shard_map/first_kernel/pallas_call | solution.py:348
  56.4 14.2 %all_to_all.31.parts = f32[8,128,128]{2,1,0:T(8,128)S(1)} all-to-all(f32[8,128,128]{2,1,0:T(8,128)S(1)} %get-tuple-element.30), channel_id=1, replica_groups={{0,1,2,3,4,5,6,7},{12,13,14,15,8,9,10,11},{16,17,18,19,20,21,22,23},{28..., dimensions={0} | all-to-all | bytes 1048576 | tf_op jit(solution)/shard_map/all_to_all | solution.py:354
  70.6 9.3 %second_kernel.1 = (f32[4,16,128]{2,1,0:T(8,128)S(1)}, f32[128,128]{1,0:T(8,128)S(1)}) custom-call(s32[8,128]{1,0:T(8,128)S(1)} %get-tuple-element.21.words, bf16[128,128,128]{2,1,0:T(8,128)(2,1)S(1)} %get-tuple-element.22.rows, bf16[64,64,128]{2,1,0:T(8,128)(2,1)S(1)} %get-tuple-element.28.targets, f32[8,128,128]{2,1,0:T(8,128)S(1)} %all_to_all.31.parts, ...), custom_call_target="tpu_custom_call" | custom-call | tf_op jit(solution)/shard_map/second_kernel/pallas_call | solution.py:355
  79.9 11.6 %all_to_all.32.parts = f32[4,16,128]{2,1,0:T(8,128)S(1)} all-to-all(f32[4,16,128]{2,1,0:T(8,128)S(1)} %get-tuple-element.32), channel_id=1, replica_groups={{0,8,16,24},{32,40,48,56},{64,72,80,88},{96,104,112,120},{128,136,144,1..., dimensions={0} | all-to-all | bytes 65536 | tf_op jit(solution)/shard_map/all_to_all | solution.py:361
  91.5 20.7 %all_to_all.33.parts = f32[16,16,128]{2,1,0:T(8,128)S(1)} all-to-all(f32[16,16,128]{2,1,0:T(8,128)S(1)} %group_kernel.1), channel_id=1, replica_groups={{0,32,64,96,128,160,192,224,256,288,320,352,384,416,448,480},{264,296,3..., dimensions={0} | all-to-all | bytes 262144 | tf_op jit(solution)/shard_map/all_to_all | solution.py:363
  112.3 8.6 %all_gather.25.lse = f32[64,128]{1,0:T(8,128)S(1)} all-gather(f32[16,128]{1,0:T(8,128)S(1)} %ring_kernel.1), channel_id=1, replica_groups={{0,8,16,24},{32,40,48,56},{64,72,80,88},{96,104,112,120},{128,136,144,1..., dimensions={0}, use_global_device_ids=true | all-gather | bytes 40960 | tf_op jit(solution)/shard_map/all_gather | solution.py:365
  121.0 4.7 %third_kernel.1 = (f32[8,128,128]{2,1,0:T(8,128)S(1)}, f32[64,128]{1,0:T(8,128)S(1)}, f32[1,128]{1,0:T(1,128)S(1)}) custom-call(s32[8,128]{1,0:T(8,128)S(1)} %get-tuple-element.23.words, bf16[64,16384]{1,0:T(8,128)(2,1)S(1)} %bitcast.14, bf16[64,128,128]{2,1,0:T(8,128)(2,1)S(1)} %get-tuple-element.29.rows, f32[64,128]{1,0:T(8,128)S(1)} %all_gather.25.lse, ...), custom_call_target="tpu_custom_call" | custom-call | tf_op jit(solution)/shard_map/third_kernel/pallas_call | solution.py:366
  125.7 13.8 %all_to_all.34.parts = f32[8,128,128]{2,1,0:T(8,128)S(1)} all-to-all(f32[8,128,128]{2,1,0:T(8,128)S(1)} %get-tuple-element.34), channel_id=1, replica_groups={{0,1,2,3,4,5,6,7},{12,13,14,15,8,9,10,11},{16,17,18,19,20,21,22,23},{28..., dimensions={0} | all-to-all | bytes 1048576 | tf_op jit(solution)/shard_map/all_to_all | solution.py:372
  139.5 5.1 %fourth_kernel.1 = (f32[2,32,128]{2,1,0:T(8,128)S(1)}, f32[128,128]{1,0:T(8,128)}, s32[32,128]{1,0:T(8,128)S(1)}) custom-call(s32[8,128]{1,0:T(8,128)S(1)} %get-tuple-element.21.words, bf16[128,128,128]{2,1,0:T(8,128)(2,1)S(1)} %get-tuple-element.22.rows, bf16[64,64,128]{2,1,0:T(8,128)(2,1)S(1)} %get-tuple-element.28.targets, ...), custom_call_target="tpu_custom_call" | custom-call | tf_op jit(solution)/shard_map/fourth_kernel/pallas_call | solution.py:373
  144.7 2.7 %all-gather.2 = f32[4,32,128]{2,1,0:T(8,128)S(1)} all-gather(f32[2,32,128]{2,1,0:T(8,128)S(1)} %get-tuple-element.37), channel_id=4, replica_groups={{0,8},{16,24},{32,40},{48,56},{64,72},{80,88},{96,104},{112,120},{128,1..., dimensions={0}, use_global_device_ids=true | all-gather | bytes 98304 | tf_op jit(solution)/shard_map/all_gather | solution.py:379
  147.4 14.0 %all_to_all.35.parts = f32[32,1,128]{2,1,0:T(1,128)S(1)} all-to-all(f32[32,1,128]{2,1,0:T(1,128)S(1)} %total_kernel.1), channel_id=1, replica_groups={{0,16,32,48,64,80,96,112,128,144,160,176,192,208,224,240,256,272,288,30..., dimensions={0} | all-to-all | bytes 32768 | tf_op jit(solution)/shard_map/all_to_all | solution.py:381
  161.4 0.6 last_kernel.1
  (14 shorter events, 0.1 us)
Async XLA Ops:
  1.4 44.3 %copy-start.4 = (f32[8192]{0:T(1024)S(1)}, f32[8192]{0:T(1024)}, u32[]{:S(2)}) copy-start(f32[8192]{0:T(1024)} %param.10) | copy-start | bytes 98308
  32.7 10.8 %collective-permute-start = (bf16[16,64,128]{2,1,0:T(8,128)(2,1)S(1)}, bf16[16,64,128]{2,1,0:T(8,128)(2,1)S(1)}, u32[]{:S(2)}, u32[]{:S(2)}) collective-permute-start(bf16[16,64,128]{2,1,0:T(8,128)(2,1)S(1)} %all_to_all.30), channel_id=1, source_target_pairs={{0,16},{8,24},{16,0},{24,8},{32,48},{40,56},{48,32},{56,40},{64,80... | collective-permute-start | bytes 786440 | tf_op jit(solution)/shard_map/ppermute | solution.py:336
  36.5 1.6 copy-start
  38.0 0.7 copy-start.6
  38.7 0.7 copy-start.7
  45.7 24.9 %copy-start.2 = (f32[16384]{0:T(1024)S(1)}, f32[16384]{0:T(1024)}, u32[]{:S(2)}) copy-start(f32[16384]{0:T(1024)} %param.11) | copy-start | bytes 196612
  70.6 50.4 %copy-start.1 = (bf16[16384,64]{0,1:T(8,128)(2,1)S(1)}, bf16[16384,64]{0,1:T(8,128)(2,1)}, u32[]{:S(2)}) copy-start(bf16[16384,64]{0,1:T(8,128)(2,1)} %param.8) | copy-start | bytes 6291460
  70.6 50.4 %copy-start.3 = (bf16[128,64]{0,1:T(8,128)(2,1)S(1)}, bf16[128,64]{0,1:T(8,128)(2,1)}, u32[]{:S(2)}) copy-start(bf16[128,64]{0,1:T(8,128)(2,1)} %param.9) | copy-start | bytes 49156
  70.6 50.4 %copy-start.5 = (f32[8192]{0:T(1024)S(1)}, f32[8192]{0:T(1024)}, u32[]{:S(2)}) copy-start(f32[8192]{0:T(1024)} %param.12) | copy-start | bytes 98308
